TPU v7x, 32 devices: a whole 2x2x4 slice. The times are simulated.
32 devices in a mesh: rep: 8 (over y, x, core), shard: 4 (over z).
Axes of the slice: x: 2, y: 2, z: 4, core: 2. Of those that a mesh axis runs over, the one named last changes fastest.
Arguments:
- tokens: bfloat16 [16384, 1536], P(('rep', 'shard')), may hold values from -6 to 6
- cotangent: bfloat16 [16384, 1536], P(('rep', 'shard'))
- seg_ids: int32 [32, 512], P(('rep', 'shard')), may hold values from 0 to 12, as said below
- parents: int32 [32, 13], P(('rep', 'shard')), may hold values from -1 to 4, as said below
- positions: int32 [32, 512], P(('rep', 'shard')), may hold values from 0 to 1023, as said below
- routes: int32 [16384, 4], P(('rep', 'shard')), may hold values from 0 to 7, all different within a row
- query_weight: float32 [1536, 1536], P('shard', 'rep'), may hold values from -0.15625 to 0.15625
- pair_weight: float32 [2, 1536, 256], P(None, 'shard', 'rep'), may hold values from -0.15625 to 0.15625
- output_weight: float32 [1536, 1536], P('shard', 'rep'), may hold values from -1.75 to 1.75
- inner_weight: float32 [2, 8, 1536, 768], P(None, None, 'shard', 'rep'), may hold values from -0.15625 to 0.15625
- outer_weight: float32 [8, 768, 1536], P(None, 'shard', 'rep'), may hold values from -0.3125 to 0.3125
- router_weight: float32 [1536, 8], P('shard'), may hold values from -0.0546875 to 0.0546875
- norm_gains: float32 [2, 1536], P(None, 'shard'), may hold values from 0 to 3
- query_moment: float32 [1536, 1536], P('shard', 'rep'), may hold values from -0.75 to 0.75
- pair_moment: float32 [2, 1536, 256], P(None, 'shard', 'rep'), may hold values from -0.75 to 0.75
- output_moment: float32 [1536, 1536], P('shard', 'rep'), may hold values from -0.75 to 0.75
- inner_moment: float32 [2, 8, 1536, 768], P(None, None, 'shard', 'rep'), may hold values from -0.75 to 0.75
- outer_moment: float32 [8, 768, 1536], P(None, 'shard', 'rep'), may hold values from -0.75 to 0.75
- router_moment: float32 [1536, 8], P('shard'), may hold values from -0.75 to 0.75
- gains_moment: float32 [2, 1536], P(None, 'shard'), may hold values from -0.75 to 0.75
- query_error: float32 [8, 1536, 1536], P('rep', 'shard')
- pair_error: float32 [8, 2, 1536, 256], P('rep', None, 'shard')
- output_error: float32 [8, 1536, 1536], P('rep', 'shard')
- inner_error: float32 [8, 2, 8, 1536, 768], P('rep', None, None, 'shard')
- outer_error: float32 [8, 8, 768, 1536], P('rep', None, 'shard')
- query_start: float32 [1536, 8], replicated, may hold values from -6 to 6
- pair_start: float32 [2, 256, 8], replicated, may hold values from -6 to 6
- output_start: float32 [1536, 8], replicated, may hold values from -6 to 6
- inner_start: float32 [2, 8, 768, 8], replicated, may hold values from -6 to 6
- outer_start: float32 [8, 1536, 8], replicated, may hold values from -6 to 6
Outputs:
- output: bfloat16 [16384, 1536], P(('rep', 'shard'))
- input_grad: bfloat16 [16384, 1536], P(('rep', 'shard'))
- query_left: float32 [1536, 8], P('shard')
- pair_left: float32 [2, 1536, 8], P(None, 'shard')
- output_left: float32 [1536, 8], P('shard')
- inner_left: float32 [2, 8, 1536, 8], P(None, None, 'shard')
- outer_left: float32 [8, 768, 8], P(None, 'shard')
- query_right: float32 [1536, 8], replicated
- pair_right: float32 [2, 256, 8], replicated
- output_right: float32 [1536, 8], replicated
- inner_right: float32 [2, 8, 768, 8], replicated
- outer_right: float32 [8, 1536, 8], replicated
- query_feedback: float32 [8, 1536, 1536], P('rep', 'shard')
- pair_feedback: float32 [8, 2, 1536, 256], P('rep', None, 'shard')
- output_feedback: float32 [8, 1536, 1536], P('rep', 'shard')
- inner_feedback: float32 [8, 2, 8, 1536, 768], P('rep', None, None, 'shard')
- outer_feedback: float32 [8, 8, 768, 1536], P('rep', None, 'shard')
- query_momentum: float32 [1536, 1536], P('shard', 'rep')
- pair_momentum: float32 [2, 1536, 256], P(None, 'shard', 'rep')
- output_momentum: float32 [1536, 1536], P('shard', 'rep')
- inner_momentum: float32 [2, 8, 1536, 768], P(None, None, 'shard', 'rep')
- outer_momentum: float32 [8, 768, 1536], P(None, 'shard', 'rep')
- router_momentum: float32 [1536, 8], P('shard')
- gains_momentum: float32 [2, 1536], P(None, 'shard')
- query_master: float32 [1536, 1536], P('shard', 'rep')
- pair_master: float32 [2, 1536, 256], P(None, 'shard', 'rep')
- output_master: float32 [1536, 1536], P('shard', 'rep')
- inner_master: float32 [2, 8, 1536, 768], P(None, None, 'shard', 'rep')
- outer_master: float32 [8, 768, 1536], P(None, 'shard', 'rep')
- router_master: float32 [1536, 8], P('shard')
- gains_master: float32 [2, 1536], P(None, 'shard')
- feedback_rms: float32 [28], replicated
Inputs may be any that keep to these rules, and one draw needn't show every extreme that they name: `seg_ids`: each row holds one tree's 13 segments in order, never falling: 0 the trunk, 1 to 4 branches, 5 to 12 leaves. `parents`: a tree's row: -1 for the trunk, 0 for the branches, each branch parent of two leaves. `positions`: a tree's offset plus the number of tokens before a token on its path.
All inputs are finite; a program needn't handle non-finite values.
Results may differ from a plain program's by a relative error of at most 0.023.
The roundings to bfloat16 on the way count: a program that leaves them out, or rounds other values in their place, can miss the bound.
Values may be sent and summed in bfloat16 or wider, within the bound.
A program may use at most 448 MiB of HBM per device.

v0:
```python
import jax
import jax.numpy as jnp
from jax import lax
from jax.sharding import PartitionSpec as P

D = 1536
HQ = 12
HK = 2
HD = 128
F = 768
E = 8
TOK_DEV = 512
QW = 1536


EPSILON = 1e-05
ROPE_BASE = 1000000.0
MOMENTUM_DECAY = 0.9
WEIGHT_DECAY = 0.01
STEP_RATE = 4.0
GAIN_RATE = 3.0
HIGHEST = lax.Precision.HIGHEST


def rms_norm(hidden, gain_row):
    return (
        hidden * lax.rsqrt(jnp.mean(hidden * hidden, axis=-1, keepdims=True) + EPSILON) * gain_row
    )


def rotate(heads_in, position, handed):
    half_size = heads_in.shape[-1] // 2
    frequency = ROPE_BASE ** (-2.0 * jnp.arange(half_size, dtype=jnp.float32) / heads_in.shape[-1])
    angles = position.astype(jnp.float32)[:, None] * frequency[None, :]
    cosine = jnp.cos(angles)[:, None, :]
    sine_part = handed * jnp.sin(angles)[:, None, :]
    former = heads_in[..., :half_size]
    latter = heads_in[..., half_size:]
    return jnp.concatenate(
        [former * cosine - latter * sine_part, latter * cosine + former * sine_part], axis=-1
    )


def path_mask(segment, parent_row):
    table_ids = jnp.arange(parent_row.shape[0], dtype=jnp.int32)
    parent_one = jnp.sum(
        jnp.where(segment[:, None] == table_ids[None, :], parent_row[None, :], 0), axis=1
    )
    parent_two = jnp.where(
        parent_one >= 0,
        jnp.sum(
            jnp.where(parent_one[:, None] == table_ids[None, :], parent_row[None, :], 0), axis=1
        ),
        -1,
    )
    token_order = jnp.arange(segment.shape[0], dtype=jnp.int32)
    same_path = (segment[:, None] == segment[None, :]) & (
        token_order[None, :] <= token_order[:, None]
    )
    return (
        same_path
        | (segment[None, :] == parent_one[:, None])
        | (segment[None, :] == parent_two[:, None])
    )


def scores_of(query_block, key_rot, mask_block):
    rows_here = query_block.shape[0]
    key_heads = key_rot.shape[1]
    shaped = query_block.reshape(
        rows_here, key_heads, query_block.shape[1] // key_heads, query_block.shape[2]
    )
    raw = jnp.einsum(
        "qkgd,tkd->kgqt", shaped, key_rot, preferred_element_type=jnp.float32
    ) * query_block.shape[2] ** (-0.5)
    return (jnp.where(mask_block[None, None], raw, -1e30), shaped)


def orthonormal(left_factor, gram_matrix):
    lower_factor = jnp.linalg.cholesky(gram_matrix)
    solved = jax.scipy.linalg.solve_triangular(
        lower_factor, jnp.swapaxes(left_factor, -1, -2), lower=True
    )
    return jnp.swapaxes(solved, -1, -2)


def advance(weight_now, moment_now, direction, step_rate, decay_rate):
    moment_new = MOMENTUM_DECAY * moment_now + (1.0 - MOMENTUM_DECAY) * direction
    return (weight_now - step_rate * (moment_new + decay_rate * weight_now), moment_new)


def per_device(
    tokens,
    cotangent,
    seg_ids,
    parents,
    positions,
    routes,
    query_weight,
    pair_weight,
    output_weight,
    inner_weight,
    outer_weight,
    router_weight,
    norm_gains,
    query_moment,
    pair_moment,
    output_moment,
    inner_moment,
    outer_moment,
    router_moment,
    gains_moment,
    query_error,
    pair_error,
    output_error,
    inner_error,
    outer_error,
    query_start,
    pair_start,
    output_start,
    inner_start,
    outer_start,
):
    low_query = query_weight.astype(jnp.bfloat16)
    low_pair = pair_weight.astype(jnp.bfloat16)
    low_output = output_weight.astype(jnp.bfloat16)
    low_inner = inner_weight.astype(jnp.bfloat16)
    low_outer = outer_weight.astype(jnp.bfloat16)
    router_low = router_weight.astype(jnp.bfloat16)
    gains_low = norm_gains.astype(jnp.bfloat16)
    heightened = (
        lax.all_gather(low_query, "shard", axis=0, tiled=True),
        lax.all_gather(low_pair, "shard", axis=1, tiled=True),
        lax.all_gather(low_output, "shard", axis=0, tiled=True),
        lax.all_gather(low_inner, "shard", axis=2, tiled=True),
        lax.all_gather(low_outer, "shard", axis=1, tiled=True),
        lax.all_gather(router_low, "shard", axis=0, tiled=True),
        lax.all_gather(gains_low, "shard", axis=1, tiled=True),
    )
    widened = (
        lax.all_gather(heightened[0], "rep", axis=1, tiled=True),
        lax.all_gather(heightened[1], "rep", axis=2, tiled=True),
        lax.all_gather(heightened[2], "rep", axis=1, tiled=True),
        lax.all_gather(heightened[3], "rep", axis=3, tiled=True),
        lax.all_gather(heightened[4], "rep", axis=2, tiled=True),
    )
    full_set = (
        widened[0],
        widened[1],
        widened[2],
        widened[3],
        widened[4],
        heightened[5],
        heightened[6],
    )
    full_query, full_pair, full_output, full_inner, full_outer, full_router, full_gains = full_set
    replicas = lax.axis_size("rep")
    shard_count = lax.axis_size("shard")
    gain_values = full_gains.astype(jnp.float32)
    hidden = tokens.astype(jnp.float32)
    length = hidden.shape[0]
    position = positions[0]
    allowed = path_mask(seg_ids[0], parents[0])
    first_low = rms_norm(hidden, gain_values[0]).astype(jnp.bfloat16)
    query_pre = jnp.dot(first_low, full_query, preferred_element_type=jnp.float32)
    pair_pre = jnp.einsum("td,adw->atw", first_low, full_pair, preferred_element_type=jnp.float32)
    query_rot = rotate(query_pre.reshape(length, HQ, HD), position, 1.0).astype(jnp.bfloat16)
    key_rot = rotate(pair_pre[0].reshape(length, HK, HD), position, 1.0).astype(jnp.bfloat16)
    values = pair_pre[1].reshape(length, HK, HD).astype(jnp.bfloat16)
    block_rows = min(512, length)
    masked, shaped = scores_of(query_rot, key_rot, allowed)
    top_score = jnp.max(masked, axis=-1, keepdims=True)
    raised = jnp.exp(masked - top_score)
    total_sum = jnp.sum(raised, axis=-1, keepdims=True)
    attention = (raised / total_sum).astype(jnp.bfloat16)
    lse_parts = top_score + jnp.log(total_sum)
    mixed_block = jnp.einsum(
        "kgqt,tkd->qkgd", attention, values, preferred_element_type=jnp.float32
    )
    mixed_parts = mixed_block.reshape(block_rows, HQ * HD)
    mixed_low = mixed_parts.astype(jnp.bfloat16)
    middle = hidden + jnp.dot(mixed_low, full_output, preferred_element_type=jnp.float32)
    second_low = rms_norm(middle, gain_values[1]).astype(jnp.bfloat16)
    logits = jnp.dot(second_low, full_router, preferred_element_type=jnp.float32)
    expert_ids = jnp.arange(E, dtype=jnp.int32)
    route_mask = jnp.any(routes[:, :, None] == expert_ids[None, None, :], axis=1)
    route_top = jnp.max(jnp.where(route_mask, logits, -1e30), axis=-1, keepdims=True)
    raised_gate = jnp.where(route_mask, jnp.exp(logits - route_top), 0.0)
    shares = raised_gate / jnp.sum(raised_gate, axis=-1, keepdims=True)
    gate_up = jnp.einsum(
        "td,aedf->aetf", second_low, full_inner, preferred_element_type=jnp.float32
    )
    activated = (jax.nn.gelu(gate_up[0]) * gate_up[1]).astype(jnp.bfloat16)
    expert_out = jnp.einsum(
        "etf,efd->etd", activated, full_outer, preferred_element_type=jnp.float32
    )
    combined = middle + jnp.einsum("te,etd->td", shares, expert_out, precision=HIGHEST)
    output = combined.astype(jnp.bfloat16)
    upstream = cotangent.astype(jnp.float32)
    combine_grad = jnp.einsum("td,etd->te", upstream, expert_out, precision=HIGHEST)
    logit_low = (
        shares * (combine_grad - jnp.sum(shares * combine_grad, axis=-1, keepdims=True))
    ).astype(jnp.bfloat16)
    branch_low = (jnp.transpose(shares)[:, :, None] * upstream[None]).astype(jnp.bfloat16)
    act_grad = jnp.einsum(
        "etd,efd->etf", branch_low, full_outer, preferred_element_type=jnp.float32
    )
    _, act_pull = jax.vjp(
        lambda gate_in, up_in: jax.nn.gelu(gate_in) * up_in, gate_up[0], gate_up[1]
    )
    gate_grad, up_grad = act_pull(act_grad)
    gate_up_low = jnp.stack([gate_grad, up_grad]).astype(jnp.bfloat16)
    grad_inner = jnp.einsum(
        "td,aetf->aedf", second_low, gate_up_low, preferred_element_type=jnp.float32
    )
    grad_router = jnp.einsum("td,te->de", second_low, logit_low, preferred_element_type=jnp.float32)
    second_grad = jnp.einsum(
        "aetf,aedf->td", gate_up_low, full_inner, preferred_element_type=jnp.float32
    ) + jnp.einsum("te,de->td", logit_low, full_router, preferred_element_type=jnp.float32)
    _, second_pull = jax.vjp(rms_norm, middle, gain_values[1])
    middle_part, gain_two = second_pull(second_grad)
    middle_grad = upstream + middle_part
    middle_low = middle_grad.astype(jnp.bfloat16)
    grad_output = jnp.einsum("tq,td->qd", mixed_low, middle_low, preferred_element_type=jnp.float32)
    mixed_grad = jnp.einsum(
        "td,qd->tq", middle_low, full_output, preferred_element_type=jnp.float32
    ).astype(jnp.bfloat16)
    masked, shaped = scores_of(query_rot, key_rot, allowed)
    attention_full = jnp.exp(masked - lse_parts)
    upstream_block = mixed_grad.reshape(block_rows, HK, HQ // HK, HD)
    attn_grad = jnp.einsum(
        "qkgd,tkd->kgqt", upstream_block, values, preferred_element_type=jnp.float32
    )
    score_low = (
        attention_full * (attn_grad - jnp.sum(attention_full * attn_grad, axis=-1, keepdims=True))
    ).astype(jnp.bfloat16)
    query_block_grad = jnp.einsum(
        "kgqt,tkd->qkgd", score_low, key_rot, preferred_element_type=jnp.float32
    ) * HD ** (-0.5)
    query_parts = query_block_grad.reshape(block_rows, HQ, HD)
    key_rot_grad = jnp.einsum(
        "kgqt,qkgd->tkd", score_low, shaped, preferred_element_type=jnp.float32
    ) * HD ** (-0.5)
    value_grad = jnp.einsum(
        "kgqt,qkgd->tkd",
        attention_full.astype(jnp.bfloat16),
        upstream_block,
        preferred_element_type=jnp.float32,
    )
    query_grad = rotate(query_parts, position, -1.0).reshape(length, HQ * HD).astype(jnp.bfloat16)
    pair_low = jnp.stack(
        [
            rotate(key_rot_grad, position, -1.0).reshape(length, HK * HD),
            value_grad.reshape(length, HK * HD),
        ]
    ).astype(jnp.bfloat16)
    grad_query = jnp.einsum("td,tq->dq", first_low, query_grad, preferred_element_type=jnp.float32)
    grad_pair = jnp.einsum("td,atw->adw", first_low, pair_low, preferred_element_type=jnp.float32)
    first_grad = jnp.einsum(
        "tq,dq->td", query_grad, full_query, preferred_element_type=jnp.float32
    ) + jnp.einsum("atw,adw->td", pair_low, full_pair, preferred_element_type=jnp.float32)
    _, first_pull = jax.vjp(rms_norm, hidden, gain_values[0])
    hidden_part, gain_one = first_pull(first_grad)
    input_grad = (middle_grad + hidden_part).astype(jnp.bfloat16)
    grad_gains = jnp.stack([gain_one, gain_two])
    grad_outer = jnp.einsum(
        "etf,etd->efd", activated, branch_low, preferred_element_type=jnp.float32
    )
    grouped = (
        lax.psum_scatter(
            grad_query.astype(jnp.bfloat16), "shard", scatter_dimension=0, tiled=True
        ).astype(jnp.float32),
        lax.psum_scatter(
            grad_pair.astype(jnp.bfloat16), "shard", scatter_dimension=1, tiled=True
        ).astype(jnp.float32),
        lax.psum_scatter(
            grad_output.astype(jnp.bfloat16), "shard", scatter_dimension=0, tiled=True
        ).astype(jnp.float32),
        lax.psum_scatter(
            grad_inner.astype(jnp.bfloat16), "shard", scatter_dimension=2, tiled=True
        ).astype(jnp.float32),
        lax.psum_scatter(
            grad_outer.astype(jnp.bfloat16), "shard", scatter_dimension=1, tiled=True
        ).astype(jnp.float32),
        lax.psum_scatter(
            grad_router.astype(jnp.bfloat16), "shard", scatter_dimension=0, tiled=True
        ).astype(jnp.float32),
        lax.psum_scatter(
            grad_gains.astype(jnp.bfloat16), "shard", scatter_dimension=1, tiled=True
        ).astype(jnp.float32),
    )
    errors = (query_error[0], pair_error[0], output_error[0], inner_error[0], outer_error[0])
    starts = (query_start, pair_start, output_start, inner_start, outer_start)
    merged = tuple((grouped[matrix_index] + errors[matrix_index] for matrix_index in range(5)))
    local_left = tuple(
        (
            jnp.einsum(
                "...mn,...nk->...mk", merged[matrix_index], starts[matrix_index], precision=HIGHEST
            )
            for matrix_index in range(5)
        )
    )
    left_sum = (
        lax.psum(local_left[0].astype(jnp.bfloat16), "rep").astype(jnp.float32),
        lax.psum(local_left[1].astype(jnp.bfloat16), "rep").astype(jnp.float32),
        lax.psum(local_left[2].astype(jnp.bfloat16), "rep").astype(jnp.float32),
        lax.psum(local_left[3].astype(jnp.bfloat16), "rep").astype(jnp.float32),
        lax.psum(local_left[4].astype(jnp.bfloat16), "rep").astype(jnp.float32),
        lax.psum(grouped[5].astype(jnp.bfloat16), "rep").astype(jnp.float32),
        lax.psum(grouped[6].astype(jnp.bfloat16), "rep").astype(jnp.float32),
    )
    router_total = left_sum[5]
    gains_total = left_sum[6]
    local_gram = tuple(
        (
            jnp.einsum(
                "...mk,...ml->...kl",
                left_sum[matrix_index],
                left_sum[matrix_index],
                precision=HIGHEST,
            )
            for matrix_index in range(5)
        )
    )
    gram_sum = lax.psum(
        (
            local_gram[0],
            local_gram[1],
            local_gram[2],
            local_gram[3],
            local_gram[4],
            jnp.sum(router_total * router_total),
            jnp.sum(gains_total * gains_total, axis=1),
        ),
        "shard",
    )
    bases = tuple(
        (orthonormal(left_sum[matrix_index], gram_sum[matrix_index]) for matrix_index in range(5))
    )
    local_right = tuple(
        (
            jnp.einsum(
                "...mn,...mk->...nk", merged[matrix_index], bases[matrix_index], precision=HIGHEST
            )
            for matrix_index in range(5)
        )
    )
    right_sum = lax.psum(
        (local_right[0], local_right[1], local_right[2], local_right[3], local_right[4]),
        ("rep", "shard"),
    )
    column_index = lax.axis_index("rep")
    weights_now = (query_weight, pair_weight, output_weight, inner_weight, outer_weight)
    moments_now = (query_moment, pair_moment, output_moment, inner_moment, outer_moment)
    step_rates = (
        STEP_RATE * D ** (-0.5),
        STEP_RATE * D ** (-0.5),
        STEP_RATE * (QW * 4 // TOK_DEV + 1) ** (-0.5),
        STEP_RATE * D ** (-0.5),
        STEP_RATE * (F // 2) ** (-0.5),
    )
    feedbacks = []
    momenta = []
    new_masters = []
    square_parts = []
    right_squares = []
    entry_counts = []
    for matrix_index in range(5):
        basis_rows = bases[matrix_index]
        right_factor = right_sum[matrix_index]
        columns = right_factor.shape[-2]
        entries = basis_rows.shape[-2] * shard_count * columns
        own_columns = columns // replicas
        approx_full = jnp.einsum("...mk,...nk->...mn", basis_rows, right_factor, precision=HIGHEST)
        feedback = merged[matrix_index] - approx_full / replicas
        squared_right = jnp.sum(right_factor * right_factor, axis=(-2, -1))
        scale_norm = jnp.sqrt(squared_right / entries + 1e-06)
        own_right = lax.dynamic_slice_in_dim(
            right_factor, column_index * own_columns, own_columns, axis=right_factor.ndim - 2
        )
        direction = (
            jnp.einsum("...mk,...nk->...mn", basis_rows, own_right, precision=HIGHEST)
            / scale_norm[..., None, None]
        )
        new_master, new_moment = advance(
            weights_now[matrix_index],
            moments_now[matrix_index],
            direction,
            step_rates[matrix_index],
            WEIGHT_DECAY,
        )
        feedbacks.append(feedback[None])
        momenta.append(new_moment)
        new_masters.append(new_master)
        square_parts.append(jnp.sum(feedback * feedback, axis=(-2, -1)))
        right_squares.append(squared_right)
        entry_counts.append(entries)
    squares_sum = lax.psum(
        (square_parts[0], square_parts[1], square_parts[2], square_parts[3], square_parts[4]),
        ("rep", "shard"),
    )
    feedback_rms = jnp.concatenate(
        [
            jnp.sqrt(squares_sum[matrix_index] / (replicas * entry_counts[matrix_index])).reshape(
                -1
            )
            for matrix_index in range(5)
        ]
    )
    router_direction = router_total / jnp.sqrt(
        gram_sum[5] / (router_total.shape[0] * shard_count * router_total.shape[1]) + 1e-06
    )
    gains_direction = (
        gains_total / jnp.sqrt(gram_sum[6] / (gains_total.shape[1] * shard_count) + 1e-06)[:, None]
    )
    router_master, router_momentum = advance(
        router_weight, router_moment, router_direction, STEP_RATE * (8 * D) ** (-0.5), WEIGHT_DECAY
    )
    gains_master, gains_momentum = advance(
        norm_gains, gains_moment, gains_direction, GAIN_RATE, 0.0
    )
    return (
        output,
        input_grad,
        bases[0],
        bases[1],
        bases[2],
        bases[3],
        bases[4],
        right_sum[0],
        right_sum[1],
        right_sum[2],
        right_sum[3],
        right_sum[4],
        feedbacks[0],
        feedbacks[1],
        feedbacks[2],
        feedbacks[3],
        feedbacks[4],
        momenta[0],
        momenta[1],
        momenta[2],
        momenta[3],
        momenta[4],
        router_momentum,
        gains_momentum,
        new_masters[0],
        new_masters[1],
        new_masters[2],
        new_masters[3],
        new_masters[4],
        router_master,
        gains_master,
        feedback_rms,
    )


def solution(mesh):
    in_specs = (
        P(("rep", "shard"), None),
        P(("rep", "shard"), None),
        P(("rep", "shard"), None),
        P(("rep", "shard"), None),
        P(("rep", "shard"), None),
        P(("rep", "shard"), None),
        P("shard", "rep"),
        P(None, "shard", "rep"),
        P("shard", "rep"),
        P(None, None, "shard", "rep"),
        P(None, "shard", "rep"),
        P("shard", None),
        P(None, "shard"),
        P("shard", "rep"),
        P(None, "shard", "rep"),
        P("shard", "rep"),
        P(None, None, "shard", "rep"),
        P(None, "shard", "rep"),
        P("shard", None),
        P(None, "shard"),
        P("rep", "shard", None),
        P("rep", None, "shard", None),
        P("rep", "shard", None),
        P("rep", None, None, "shard", None),
        P("rep", None, "shard", None),
        P(),
        P(),
        P(),
        P(),
        P(),
    )
    out_specs = (
        P(("rep", "shard"), None),
        P(("rep", "shard"), None),
        P("shard", None),
        P(None, "shard", None),
        P("shard", None),
        P(None, None, "shard", None),
        P(None, "shard", None),
        P(),
        P(),
        P(),
        P(),
        P(),
        P("rep", "shard", None),
        P("rep", None, "shard", None),
        P("rep", "shard", None),
        P("rep", None, None, "shard", None),
        P("rep", None, "shard", None),
        P("shard", "rep"),
        P(None, "shard", "rep"),
        P("shard", "rep"),
        P(None, None, "shard", "rep"),
        P(None, "shard", "rep"),
        P("shard", None),
        P(None, "shard"),
        P("shard", "rep"),
        P(None, "shard", "rep"),
        P("shard", "rep"),
        P(None, None, "shard", "rep"),
        P(None, "shard", "rep"),
        P("shard", None),
        P(None, "shard"),
        P(),
    )
    return jax.shard_map(
        per_device, mesh=mesh, in_specs=in_specs, out_specs=out_specs, check_vma=False
    )
```

profile of v0, /device:TPU:0, one launch (start us, length us, event | category | flops | bytes accessed | tf_op | source)
XLA Modules:
  0.0 2584.5 jit_solution(17778671126910399483)
XLA Ops:
  29.2 26.8 %all_gather.39 = bf16[1536,192]{0,1:T(8,128)(2,1)} all-gather(bf16[384,192]{0,1:T(8,128)(2,1)S(1)} %convert_element_type.179), channel_id=1, replica_groups=mesh['rep'=8,'shard'=4] {'shard'}, dimensions={0}, use_global_device_ids=true | all-gather | bytes 737280 | tf_op jit(solution)/shard_map/all_gather | solution.py:132
  56.2 25.8 all_gather.41
  82.0 39.9 %all-gather.14.cloned.1.call-done = bf16[2,8,1536,96]{2,3,1,0:T(8,128)(2,1)} async-done(((bf16[2,8,384,96]{2,3,1,0:T(8,128)(2,1)}), bf16[2,8,1536,96]{2,3,1,0:T(8,128)(2,1)}) %all-gather.14.cloned.1.call-update) | async-done | bytes 4718608 | tf_op jit(solution)/shard_map/all_gather | solution.py:135
  122.0 64.0 %all-gather.18.cloned.1.call-done = bf16[8,768,192]{2,0,1:T(8,128)(2,1)} async-done(((bf16[8,192,192]{2,0,1:T(8,128)(2,1)}), bf16[8,768,192]{2,0,1:T(8,128)(2,1)}) %all-gather.18.cloned.1.call-update) | async-done | bytes 2359312 | tf_op jit(solution)/shard_map/all_gather | solution.py:136
  301.2 173.8 %all-gather.16.cloned.1.call-done = bf16[2,8,1536,768]{2,3,1,0:T(8,128)(2,1)} async-done(((bf16[2,8,1536,96]{2,3,1,0:T(8,128)(2,1)}), bf16[2,8,1536,768]{2,3,1,0:T(8,128)(2,1)}) %all-gather.16.cloned.1.call-update) | async-done | bytes 37748752 | tf_op jit(solution)/shard_map/all_gather | solution.py:144
  475.0 30.8 %convolution_bitcast_fusion = f32[2,8,512,768]{3,2,1,0:T(8,128)} fusion(bf16[2,8,1536,768]{2,3,1,0:T(8,128)(2,1)} %all-gather.16.cloned.1.call-done, bf16[512,1536]{1,0:T(8,128)(2,1)S(1)} %multiply_convert_fusion.7), kind=kOutput, calls=%fused_computation.45 | convolution fusion | flops 19327352832 | bytes 64487424 | tf_op jit(solution)/shard_map/td,aedf->aetf/dot_general | solution.py:190
  505.8 70.5 %all-gather.20.cloned.1.call-done = bf16[8,768,1536]{1,2,0:T(8,128)(2,1)} async-done(((bf16[8,768,192]{1,2,0:T(8,128)(2,1)}), bf16[8,768,1536]{1,2,0:T(8,128)(2,1)}) %all-gather.20.cloned.1.call-update) | async-done | bytes 18874384 | tf_op jit(solution)/shard_map/all_gather | solution.py:145
  576.3 31.3 %fusion.30 = (bf16[1,8,512,768]{3,2,1,0:T(8,128)(2,1)}, bf16[1,8,512,768]{3,2,1,0:T(8,128)(2,1)}, bf16[8,512,768]{2,1,0:T(8,128)(2,1)}) fusion(f32[2,8,512,768]{3,2,1,0:T(8,128)} %convolution_bitcast_fusion, bf16[8,768,1536]{1,2,0:T(8,128)(2,1)} %all-gather.20.cloned.1.call-done, f32[512,1536]{1,0:T(8,128)} %convert_element_type.191, f32[8,512]{1,0:T(8,128)S(1)} %fusion.140), kind=kOutput, calls=%fused_computation.59 | convolution fusion | flops 9758048256 | bytes 66076672 | tf_op jit(solution)/shard_map/etd,efd->etf/dot_general | solution.py:205
  630.1 46.3 %fusion = f32[512,1,8]{2,1,0:T(1,128)S(1)} fusion(f32[8,512,1536]{2,1,0:T(8,128)} %fusion.151, bf16[512,1536,1]{1,0,2:T(8,128)(2,1)S(1)} %bitcast.373), kind=kOutput, calls=%fused_computation.2 | convolution fusion | flops 75497472 | bytes 26755072 | tf_op jit(solution)/shard_map/td,etd->te/dot_general | solution.py:200
  677.2 25.1 fusion.36
  707.8 43.4 %fusion.2 = f32[512,1,1536]{2,1,0:T(1,128)S(1)} fusion(f32[512,8,1]{1,2,0:T(1,128)} %copy.300, f32[8,512,1536]{2,1,0:T(8,128)} %fusion.151), kind=kOutput, calls=%fused_computation.4 | convolution fusion | flops 75497472 | bytes 28327936 | tf_op jit(solution)/shard_map/te,etd->td/dot_general | solution.py:197
  852.8 29.7 %convert_bitcast_fusion = bf16[2,8,1536,768]{2,3,1,0:T(8,128)(2,1)} fusion(bf16[1,8,512,768]{3,2,1,0:T(8,128)(2,1)} %get-tuple-element.134, bf16[1,8,512,768]{3,2,1,0:T(8,128)(2,1)} %get-tuple-element.133, bf16[512,1536]{1,0:T(8,128)(2,1)S(1)} %copy-done.13), kind=kOutput, calls=%fused_computation | convolution fusion | flops 19352518656 | bytes 51904512 | tf_op jit(solution)/shard_map/td,aetf->aedf/dot_general | solution.py:213
  882.5 48.9 %copy.332 = bf16[2,8,1536,768]{3,1,0,2:T(8,128)(2,1)} copy(bf16[2,8,1536,768]{2,3,1,0:T(8,128)(2,1)} %convert_bitcast_fusion) | data formatting | bytes 75497472
  931.4 26.2 %copy.343 = bf16[192,8,16,768]{3,1,2,0:T(8,128)(2,1)} copy(bf16[192,8,16,768]{3,2,1,0:T(8,128)(2,1)} %bitcast.354) | data formatting | bytes 75497472
  976.9 84.0 %reduce-scatter.18.cloned.1.call-done = bf16[384,1536]{1,0:T(8,128)(2,1)} async-done(((bf16[1536,1536]{1,0:T(8,128)(2,1)}), bf16[384,1536]{1,0:T(8,128)(2,1)}) %reduce-scatter.18.cloned.1.call-update) | async-done | bytes 1179664 | tf_op jit(solution)/shard_map/reduce_scatter | solution.py:276
  1065.6 312.5 %reduce-scatter.20.cloned.1.call-done = bf16[8,192,1536]{2,1,0:T(8,128)(2,1)} async-done(((bf16[8,768,1536]{2,1,0:T(8,128)(2,1)}), bf16[8,192,1536]{2,1,0:T(8,128)(2,1)}) %reduce-scatter.20.cloned.1.call-update) | async-done | bytes 4718608 | tf_op jit(solution)/shard_map/reduce_scatter | solution.py:282
  1390.4 26.6 %all-reduce.4 = (bf16[384,8]{0,1:T(8,128)(2,1)}, bf16[2,384,8]{1,2,0:T(8,128)(2,1)S(1)}, bf16[384,8]{0,1:T(8,128)(2,1)}, bf16[8,192,8]{1,2,0:T(8,128)(2,1)}, bf1...) all-reduce(bf16[384,8]{0,1:T(8,128)(2,1)} %convolution_convert_fusion, ...), channel_id=1, replica_groups=mesh['rep'=8,'shard'=4] {'rep'}, use_global_device_ids=true, to_apply=%region_14.15 | all-reduce | flops 28416 | bytes 113664 | tf_op jit(solution)/shard_map/psum | solution.py:304
  1422.9 577.8 %reduce-scatter.24.cloned.1.call-done = bf16[384,12288]{1,0:T(8,128)(2,1)} async-done(((bf16[1536,12288]{1,0:T(8,128)(2,1)}), bf16[384,12288]{1,0:T(8,128)(2,1)}) %reduce-scatter.24.cloned.1.call-update) | async-done | bytes 9437200
  2011.2 26.0 %convolution_convert_fusion.5 = bf16[2,8,384,8]{2,3,1,0:T(8,128)(2,1)} fusion(f32[2,8,768,8]{2,3,1,0:T(8,128)S(1)} %copy-done, f32[1,2,8,384,768]{4,3,2,1,0:T(8,128)} %param.56, bf16[2,8,384,768]{3,1,0,2:T(8,128)(2,1)} %bitcast.348), kind=kOutput, calls=%fused_computation.129 | convolution fusion | flops 462471168 | bytes 28803072 | tf_op jit(solution)/shard_map/...mn,...nk->...mk/dot_general | solution.py:297
  2038.6 51.3 %all-reduce.9.cloned.1.call-done = bf16[2,8,384,8]{2,3,1,0:T(8,128)(2,1)} async-done(((bf16[2,8,384,8]{2,3,1,0:T(8,128)(2,1)}), bf16[2,8,384,8]{2,3,1,0:T(8,128)(2,1)}) %all-reduce.9.cloned.1.call-update) | async-done | bytes 98320 | tf_op jit(solution)/shard_map/psum | solution.py:307
  2232.4 108.5 %all-reduce.11.cloned.1.call-done = (f32[1536,8]{0,1:T(8,128)}, f32[2,256,8]{1,2,0:T(8,128)}, f32[1536,8]{0,1:T(8,128)}) async-done(((f32[1536,8]{0,1:T(8,128)}, f32[2,256,8]{1,2,0:T(8,128)}, f32[1536,8]{0,1:T(8,128)}), (f32[1536,8]{0,1:T(8,128)}, f32[2,256,8]{1,2,0:T(8,128)}, f32[1536,8]{0,1:T(8,128)})) %all-reduce.11.cloned.1.call-update) | async-done | bytes 114704 | tf_op jit(solution)/shard_map/psum | solution.py:348
  2364.8 113.8 %all-reduce.13.cloned.1.call-done = (f32[2,8,768,8]{2,3,1,0:T(8,128)}, f32[8,1536,8]{1,2,0:T(8,128)}) async-done(((f32[2,8,768,8]{2,3,1,0:T(8,128)}, f32[8,1536,8]{1,2,0:T(8,128)}), (f32[2,8,768,8]{2,3,1,0:T(8,128)}, f32[8,1536,8]{1,2,0:T(8,128)})) %all-reduce.13.cloned.1.call-update) | async-done | bytes 786448 | tf_op jit(solution)/shard_map/psum | solution.py:348
  2478.6 31.8 %multiply_reduce_fusion = (f32[2,8]{1,0:T(2,128)S(1)}, f32[1,2,8,384,768]{4,3,2,1,0:T(8,128)}) fusion(f32[1,2,8,384,768]{4,3,2,1,0:T(8,128)} %param.56, bf16[2,8,384,768]{3,1,0,2:T(8,128)(2,1)} %bitcast.350, f32[2,8,8,384]{3,2,1,0:T(8,128)S(1)} %copy-done.28, f32[2,8,768,8]{2,3,1,0:T(8,128)} %get-tuple-element.195), kind=kOutput, calls=%fused_computation.7 | convolution fusion | flops 481296384 | bytes 47775808 | tf_op jit(solution)/shard_map/...mk,...nk->...mn/dot_general | solution.py:374
  2522.7 39.7 %all-reduce = (f32[]{:T(128)}, f32[2]{0:T(128)S(1)}, f32[]{:T(128)}, f32[2,8]{1,0:T(2,128)S(1)}, f32[8]{0:T(128)S(1)}) all-reduce(f32[]{:T(128)} %get-tuple-element.173, f32[2]{0:T(128)S(1)} %get-tuple-element.175, f32[]{:T(128)} %get-tuple-element.177, ...), channel_id=1, replica_groups=mesh['rep'=8,'shard'=4] {'rep','shard'}, use_global_device_ids=true, to_apply=%region_57.60 | all-reduce | flops 28 | bytes 224 | tf_op jit(solution)/shard_map/psum | solution.py:398
  (423 shorter events, 510.9 us)
Async XLA Ops:
  7.2 2004.0 %copy-start = (f32[2,8,768,8]{2,3,1,0:T(8,128)S(1)}, f32[2,8,768,8]{2,3,1,0:T(8,128)}, u32[]{:S(2)}) copy-start(f32[2,8,768,8]{2,3,1,0:T(8,128)} %param.61) | copy-start | bytes 1179652
  7.2 114.6 %all-gather.14.cloned.1.call-start = ((), (), s32[]{:S(2)}) async-start(), calls=%async_computation.10 | async-start | bytes 5898240 | tf_op jit(solution)/shard_map/all_gather | solution.py:135
  10.3 175.7 %all-gather.18.cloned.1.call-start = ((), (), s32[]{:S(2)}) async-start(), calls=%async_computation.12 | async-start | bytes 3932160 | tf_op jit(solution)/shard_map/all_gather | solution.py:136
  12.1 218.3 %all-gather.8.cloned.1.call-start = ((), (), s32[]{:S(2)}) async-start(), calls=%async_computation.7 | async-start | bytes 1769472 | tf_op jit(solution)/shard_map/all_gather | solution.py:142
  29.1 223.9 %all-gather.10.cloned.1.call-start = ((), (), s32[]{:S(2)}) async-start(), calls=%async_computation.8 | async-start | bytes 5308416 | tf_op jit(solution)/shard_map/all_gather | solution.py:141
  56.1 237.6 %all-gather.12.cloned.1.call-start = ((), (), s32[]{:S(2)}) async-start(), calls=%async_computation.9 | async-start | bytes 5308416 | tf_op jit(solution)/shard_map/all_gather | solution.py:143
  82.0 393.1 %all-gather.16.cloned.1.call-start = ((), (), s32[]{:S(2)}) async-start(), calls=%async_computation.11 | async-start | bytes 42467328 | tf_op jit(solution)/shard_map/all_gather | solution.py:144
  121.9 68.9 %copy-start.82 = (f32[2,384]{1,0:T(2,128)S(1)}, f32[2,384]{1,0:T(2,128)}, u32[]{:S(2)}) copy-start(f32[2,384]{1,0:T(2,128)} %param.45) | copy-start | bytes 9220
  121.9 81.6 %copy-start.88 = (s32[1,512]{1,0:T(1,128)S(1)}, s32[1,512]{1,0:T(1,128)}, u32[]{:S(2)}) copy-start(s32[1,512]{1,0:T(1,128)} %param.37) | copy-start | bytes 6148
  121.9 454.3 %all-gather.20.cloned.1.call-start = ((), (), s32[]{:S(2)}) async-start(), calls=%async_computation.13 | async-start | bytes 21233664 | tf_op jit(solution)/shard_map/all_gather | solution.py:145
  190.8 773.3 %reduce-scatter.28.cloned.1.call-start = ((), (), s32[]{:S(2)}) async-start(), calls=%async_computation.21 | async-start | bytes 491520
  228.9 70.0 %copy-start.59 = (f32[1536]{0:T(1024)}, f32[1536]{0:T(1024)S(1)}, u32[]{:S(2)}) copy-start(f32[1536]{0:T(1024)S(1)} %get-tuple-element.102) | copy-start | bytes 18436
  299.8 206.0 %copy-start.12 = (bf16[512,1536]{1,0:T(8,128)(2,1)}, bf16[512,1536]{1,0:T(8,128)(2,1)S(1)}, u32[]{:S(2)}) copy-start(bf16[512,1536]{1,0:T(8,128)(2,1)S(1)} %multiply_convert_fusion.7) | copy-start | bytes 4718596
  300.6 275.7 %copy-start.80 = (f32[8,512]{1,0:T(8,128)}, f32[8,512]{1,0:T(8,128)S(1)}, u32[]{:S(2)}) copy-start(f32[8,512]{1,0:T(8,128)S(1)} %fusion.140) | copy-start | bytes 49156
  807.4 157.7 %reduce-scatter.26.cloned.1.call-start = ((), (), s32[]{:S(2)}) async-start(), calls=%async_computation.20 | async-start | bytes 491520
  810.1 156.6 %reduce-scatter.22.cloned.1.call-start = ((), (), s32[]{:S(2)}) async-start(), calls=%async_computation.18 | async-start | bytes 1966080
  821.2 151.6 %reduce-scatter.16.cloned.1.call-start = ((), (), s32[]{:S(2)}) async-start(), calls=%async_computation.14 | async-start | bytes 5898240 | tf_op jit(solution)/shard_map/reduce_scatter | solution.py:270
  827.5 233.3 %reduce-scatter.18.cloned.1.call-start = ((), (), s32[]{:S(2)}) async-start(), calls=%async_computation.15 | async-start | bytes 5898240 | tf_op jit(solution)/shard_map/reduce_scatter | solution.py:276
  835.0 543.1 %reduce-scatter.20.cloned.1.call-start = ((), (), s32[]{:S(2)}) async-start(), calls=%async_computation.17 | async-start | bytes 23592960 | tf_op jit(solution)/shard_map/reduce_scatter | solution.py:282
  852.8 1148.0 %reduce-scatter.24.cloned.1.call-start = ((), (), s32[]{:S(2)}) async-start(), calls=%async_computation.19 | async-start | bytes 47185920
  957.7 1132.2 %all-reduce.9.cloned.1.call-start = ((), (), s32[]{:S(2)}) async-start(), calls=%async_computation.16 | async-start | bytes 196608 | tf_op jit(solution)/shard_map/psum | solution.py:307
  2037.2 303.7 %all-reduce.11.cloned.1.call-start = ((), (), s32[]{:S(2)}) async-start(), calls=%async_computation.22 | async-start | bytes 229376 | tf_op jit(solution)/shard_map/psum | solution.py:348
  2221.4 257.1 %all-reduce.13.cloned.1.call-start = ((), (), s32[]{:S(2)}) async-start(), calls=%async_computation.23 | async-start | bytes 1572864 | tf_op jit(solution)/shard_map/psum | solution.py:348
  2359.3 119.2 %copy-start.28 = (f32[2,8,8,384]{3,2,1,0:T(8,128)S(1)}, f32[2,8,8,384]{3,2,1,0:T(8,128)}, u32[]{:S(2)}) copy-start(f32[2,8,8,384]{3,2,1,0:T(8,128)} %copy-done.27) | copy-start | bytes 589828
  (94 other events, 1163.3 us)
Sparse Core Ops, SparseCore 0:
  10.4 111.4 all-gather.13
  124.0 61.9 all-gather.17
  187.9 24.3 all-gather.7
  214.0 38.9 all-gather.9
  254.7 38.9 all-gather.11
  295.4 179.5 all-gather.15
  477.5 98.7 all-gather.19
  807.5 20.5 reduce-scatter.27
  831.1 18.8 reduce-scatter.25
  852.7 33.5 reduce-scatter.21
  888.6 84.2 reduce-scatter.15
  975.0 85.7 reduce-scatter.17
  1063.7 314.2 reduce-scatter.19
  1380.4 620.2 reduce-scatter.23
  2037.3 52.5 all-reduce.8
  2221.5 119.3 all-reduce.10
  2348.2 130.2 all-reduce.12
where the time goes:
time: 2600 us; the launch traced here: 2580 us
  waiting for transfers between devices  1630 us (63%)
  matrix products  494 us (19%)
  blocking collectives  184 us (7%)
  local copies, waits for them, and re-layouts  143 us (6%)
  other arithmetic  113 us (4%)
    unnamed x21, waiting for transfers between devices  578 us
    reduce_scatter x1, waiting for transfers between devices, per_device(): lax.psum_scatter(grad_outer.astype(jnp.bfloat16), 'shard', scatter_dimens...  312 us
    psum x2, waiting for transfers between devices, per_device(): lax.psum((local_right[0], local_right[1], local_right[2], local_right[3],...  222 us
    all_gather x1, waiting for transfers between devices, per_device(): lax.all_gather(heightened[3], 'rep', axis=3, tiled=True)  174 us
    unnamed x220, local copies, waits for them, and re-layouts  114 us
    reduce_scatter x1, waiting for transfers between devices, per_device(): lax.psum_scatter(grad_output.astype(jnp.bfloat16), 'shard', scatter_dimen...  84 us
    all_gather x1, waiting for transfers between devices, per_device(): lax.all_gather(heightened[4], 'rep', axis=2, tiled=True)  70.5 us
    all_gather x1, waiting for transfers between devices, per_device(): lax.all_gather(low_outer, 'shard', axis=1, tiled=True)  64 us
  transfers between devices with their start and end apart: 17, of which 13 were waited for; matrix products, arithmetic and copies ran while one was open for 12% of the time, Pallas kernels for 0%

commit v1 on v0

v1 whole, which is shorter than its diff:
```python
import functools

import jax
import jax.numpy as jnp
from jax import lax
from jax.experimental import pallas as pl
from jax.experimental.pallas import tpu as pltpu
from jax.sharding import PartitionSpec as P

D = 1536
HQ = 12
HK = 2
HD = 128
F = 768
E = 8
TOK_DEV = 512
QW = 1536


EPSILON = 1e-05
ROPE_BASE = 1000000.0
MOMENTUM_DECAY = 0.9
WEIGHT_DECAY = 0.01
STEP_RATE = 4.0
GAIN_RATE = 3.0
HIGHEST = lax.Precision.HIGHEST


def rms_norm(hidden, gain_row):
    return (
        hidden * lax.rsqrt(jnp.mean(hidden * hidden, axis=-1, keepdims=True) + EPSILON) * gain_row
    )


def rotate(heads_in, position, handed):
    half_size = heads_in.shape[-1] // 2
    frequency = ROPE_BASE ** (-2.0 * jnp.arange(half_size, dtype=jnp.float32) / heads_in.shape[-1])
    angles = position.astype(jnp.float32)[:, None] * frequency[None, :]
    cosine = jnp.cos(angles)[:, None, :]
    sine_part = handed * jnp.sin(angles)[:, None, :]
    former = heads_in[..., :half_size]
    latter = heads_in[..., half_size:]
    return jnp.concatenate(
        [former * cosine - latter * sine_part, latter * cosine + former * sine_part], axis=-1
    )


def path_mask(segment, parent_row):
    table_ids = jnp.arange(parent_row.shape[0], dtype=jnp.int32)
    parent_one = jnp.sum(
        jnp.where(segment[:, None] == table_ids[None, :], parent_row[None, :], 0), axis=1
    )
    parent_two = jnp.where(
        parent_one >= 0,
        jnp.sum(
            jnp.where(parent_one[:, None] == table_ids[None, :], parent_row[None, :], 0), axis=1
        ),
        -1,
    )
    token_order = jnp.arange(segment.shape[0], dtype=jnp.int32)
    same_path = (segment[:, None] == segment[None, :]) & (
        token_order[None, :] <= token_order[:, None]
    )
    return (
        same_path
        | (segment[None, :] == parent_one[:, None])
        | (segment[None, :] == parent_two[:, None])
    )


def scores_of(query_block, key_rot, mask_block):
    rows_here = query_block.shape[0]
    key_heads = key_rot.shape[1]
    shaped = query_block.reshape(
        rows_here, key_heads, query_block.shape[1] // key_heads, query_block.shape[2]
    )
    raw = jnp.einsum(
        "qkgd,tkd->kgqt", shaped, key_rot, preferred_element_type=jnp.float32
    ) * query_block.shape[2] ** (-0.5)
    return (jnp.where(mask_block[None, None], raw, -1e30), shaped)


def advance(weight_now, moment_now, direction, step_rate, decay_rate):
    moment_new = MOMENTUM_DECAY * moment_now + (1.0 - MOMENTUM_DECAY) * direction
    return (weight_now - step_rate * (moment_new + decay_rate * weight_now), moment_new)


CHUNKS = 4
GELU_C = 0.7978845608028654
GELU_A = 0.044715
MESH = pl.DeviceIdType.MESH
VMEM_LIMIT = 60 * 1024 * 1024
F32 = jnp.float32
BF16 = jnp.bfloat16


def z_ring(block):
    size = lax.axis_size("shard")
    here = lax.axis_index("shard")
    up = down = block
    ups, downs = [block], [block]
    for _ in range(size - 1):
        up = lax.ppermute(up, "shard", [(i, i + 1) for i in range(size - 1)])
        down = lax.ppermute(down, "shard", [(i + 1, i) for i in range(size - 1)])
        ups.append(up)
        downs.append(down)
    return here, ups, downs


def z_gather(block):
    here, ups, downs = z_ring(block)
    size = len(ups)
    parts = []
    for k in range(size):
        part = ups[0]
        for other in range(size):
            if other > k:
                part = jnp.where(here == other, ups[other - k], part)
            elif other < k:
                part = jnp.where(here == other, downs[k - other], part)
        parts.append(part)
    return jnp.stack(parts)


def z_slots(block):
    here, ups, downs = z_ring(block)
    size = len(ups)
    return jnp.stack([block] + [jnp.where(here >= j, ups[j], downs[size - j]) for j in range(1, size)])


def nn(a, b, precision=None):
    return jnp.dot(a, b, preferred_element_type=F32, precision=precision)


def nt(a, b, precision=None):
    return lax.dot_general(
        a, b, (((1,), (1,)), ((), ())), preferred_element_type=F32, precision=precision
    )


def tn(a, b):
    return lax.dot_general(a, b, (((0,), (0,)), ((), ())), preferred_element_type=F32)


def up_to(count, unit):
    return -(-count // unit) * unit


def two_terms(value):
    high = value.astype(BF16)
    return high, (value - high.astype(F32)).astype(BF16)


def three_terms(value):
    high = value.astype(BF16)
    rest = value - high.astype(F32)
    middle = rest.astype(BF16)
    low = (rest - middle.astype(F32)).astype(BF16)
    return jnp.concatenate([high.astype(F32), middle.astype(F32), low.astype(F32)], axis=0).astype(BF16)


def folded(value, rows=8):
    return value[:rows] + value[rows : 2 * rows] + value[2 * rows : 3 * rows]


def exact_nn(value, other):
    return folded(nn(three_terms(value), other))


def exact_nt(value, other):
    return folded(nt(three_terms(value), other))


def padded(value, width):
    if value.shape[1] == width:
        return value
    return jnp.concatenate(
        [value, jnp.zeros((value.shape[0], width - value.shape[1]), value.dtype)], axis=1
    )


def params(**more):
    return pltpu.CompilerParams(vmem_limit_bytes=VMEM_LIMIT, **more)


def vmem_specs(count):
    return [pl.BlockSpec(memory_space=pltpu.VMEM)] * count


def struct(shape, dtype=F32):
    return jax.ShapeDtypeStruct(shape, dtype)


def expert_kernel(
    first_expert,
    aliased,
    x_ref,
    u_ref,
    up_ref,
    w1_ref,
    w2_ref,
    err_in_ref,
    err_out_ref,
    start_in_ref,
    start_out_ref,
    *rest,
):
    if aliased:
        rest = rest[2:]
    min_ref, mout_ref, y_ref, sg_ref, cg_ref, lin_ref, lout_ref, gt_ref, act_ref, br_ref = rest
    expert = first_expert + pl.program_id(0)
    tree = pl.program_id(1)
    width = up_ref.shape[1]
    groups, lanes, _, double, span1 = w1_ref.shape
    f_cols = double // 2
    hidden = groups * f_cols
    lanes2, _, groups2, _, f_rows, span2 = w2_ref.shape
    rows = min_ref.shape[2]
    out_rows = mout_ref.shape[1]
    here = lax.axis_index("shard")

    def first_weight(a, low, high):
        parts = [
            w1_ref[low:high, k, 0, a * f_cols : (a + 1) * f_cols, :].reshape(
                (high - low) * f_cols, span1
            )
            for k in range(lanes)
        ]
        return parts[0] if lanes == 1 else jnp.concatenate(parts, axis=1)

    def second_weight(low, high):
        parts = [
            w2_ref[k, 0, low:high, 0, :, :].reshape((high - low) * f_rows, span2)
            for k in range(lanes2)
        ]
        return parts[0] if lanes2 == 1 else jnp.concatenate(parts, axis=1)

    x = x_ref[0, :width, :]
    tail = x_ref[0, width:, :].astype(F32)
    shares8 = tail[:E] + tail[E:]
    picked = lax.broadcasted_iota(jnp.int32, shares8.shape, 0) == expert
    share = jnp.sum(jnp.where(picked, shares8, 0.0), axis=0, keepdims=True)
    br_ref[...] = (share * u_ref[0].astype(F32)).astype(BF16)
    halves = 2 if groups % 2 == 0 and groups2 % 2 == 0 else 1
    half = hidden // halves
    for part in range(halves):
        span = slice(part * half, (part + 1) * half)
        g_low, g_high = part * groups // halves, (part + 1) * groups // halves
        h_low, h_high = part * groups2 // halves, (part + 1) * groups2 // halves
        gate = nn(first_weight(0, g_low, g_high), x)
        up = nn(first_weight(1, g_low, g_high), x)
        act_grad = nn(second_weight(h_low, h_high), br_ref[...])
        square = gate * gate
        bent = jnp.tanh(GELU_C * (gate + GELU_A * (square * gate)))
        lifted = 0.5 * (1.0 + bent)
        gelu = gate * lifted
        slope = lifted + 0.5 * gate * (1.0 - bent * bent) * (
            GELU_C * (1.0 + 3.0 * GELU_A * square)
        )
        act_ref[span, :] = (gelu * up).astype(BF16)
        gt_ref[span, :] = (act_grad * up * slope).astype(BF16)
        gt_ref[hidden + part * half : hidden + (part + 1) * half, :] = (act_grad * gelu).astype(
            BF16
        )

    @pl.when(tree == 0)
    def _():
        min_ref[...] = err_in_ref[...]
        mout_ref[...] = err_out_ref[...]

    own_x = x_ref[0, pl.ds(pl.multiple_of(here * rows, 16), rows), :]
    min_ref[0, 0] += nt(own_x, gt_ref[:hidden, :])
    min_ref[1, 0] += nt(own_x, gt_ref[hidden:, :])
    own_act = act_ref[pl.ds(pl.multiple_of(here * out_rows, 16), out_rows), :]
    mout_ref[0] += nt(own_act, br_ref[...])

    @pl.when(tree == 0)
    def _():
        expert_out = tn(act_ref[...], second_weight(0, groups2))
        cg_ref[0] = jnp.sum(up_ref[...].astype(F32) * expert_out, axis=1, keepdims=True)
        share_col = jnp.transpose(jnp.broadcast_to(share, (8, share.shape[1])))[:, :1]
        added = share_col * expert_out
        grown = tn(gt_ref[:hidden, :], first_weight(0, 0, groups)) + tn(
            gt_ref[hidden:, :], first_weight(1, 0, groups)
        )
        first = pl.program_id(0) == 0
        y_ref[...] = jnp.where(first, added, y_ref[...] + added)
        sg_ref[...] = jnp.where(first, grown, sg_ref[...] + grown)

    @pl.when(tree == pl.num_programs(1) - 1)
    def _():
        lin_ref[...] = jnp.zeros_like(lin_ref)
        lout_ref[...] = jnp.zeros_like(lout_ref)
        for a in range(2):
            lin_ref[0, a, :, :rows] = nt(start_in_ref[a, 0], min_ref[a, 0], HIGHEST)
        lout_ref[0, :, :out_rows] = nt(start_out_ref[0], mout_ref[0], HIGHEST)


def expert_chunk(
    first_expert, x4, u4, upstream, w1, w2, err_in, err_out, start_in, start_out, merged
):
    count = w2.shape[1]
    hidden = err_in.shape[3]
    trees, width, length = u4.shape
    rows, out_rows = err_in.shape[2], err_out.shape[1]
    last_block = w2.shape[3] - 1
    one = pl.Buffered(1)

    def spec(block, index, **more):
        return pl.BlockSpec(block, index, **more)

    in_specs = [
        spec((1, x4.shape[1], length), lambda e, t: (t, 0, 0)),
        spec((1, width, length), lambda e, t: (t, 0, 0)),
        spec((length, width), lambda e, t: (0, 0), pipeline_mode=one),
        spec((*w1.shape[:2], 1, *w1.shape[3:]), lambda e, t: (0, 0, e, 0, 0)),
        spec(
            (w2.shape[0], 1, w2.shape[2], 1, *w2.shape[4:]),
            lambda e, t: (0, e, 0, last_block, 0, 0),
        ),
        spec((2, 1, rows, hidden), lambda e, t: (0, first_expert + e, 0, 0)),
        spec((1, out_rows, width), lambda e, t: (first_expert + e, 0, 0)),
        spec((2, 1, 8, hidden), lambda e, t: (0, first_expert + e, 0, 0)),
        spec((1, 8, width), lambda e, t: (first_expert + e, 0, 0)),
    ]
    operands = [x4, u4, upstream, w1, w2, err_in, err_out, start_in, start_out]
    aliases = {}
    if merged is not None:
        in_specs += [pl.BlockSpec(memory_space=pl.ANY)] * 2
        aliases = {len(operands): 0, len(operands) + 1: 1}
        operands += list(merged)
    wide, wide_out = up_to(rows, 128), up_to(out_rows, 128)
    out_specs = [
        spec((2, 1, rows, hidden), lambda e, t: (0, first_expert + e, 0, 0)),
        spec((1, out_rows, width), lambda e, t: (first_expert + e, 0, 0)),
        spec((length, width), lambda e, t: (0, 0), pipeline_mode=one),
        spec((length, width), lambda e, t: (0, 0), pipeline_mode=one),
        spec((1, length, 1), lambda e, t: (e, 0, 0)),
        spec((1, 2, 8, wide), lambda e, t: (e, 0, 0, 0)),
        spec((1, 8, wide_out), lambda e, t: (e, 0, 0)),
    ]
    out_shape = [
        struct(err_in.shape),
        struct(err_out.shape),
        struct((length, width)),
        struct((length, width)),
        struct((count, length, 1)),
        struct((count, 2, 8, wide)),
        struct((count, 8, wide_out)),
    ]
    flops = 2 * count * hidden * width * length * (3 * trees + 3) + 2 * count * trees * length * (
        2 * rows * hidden + out_rows * width
    )
    return pl.pallas_call(
        functools.partial(expert_kernel, first_expert, merged is not None),
        grid=(count, trees),
        in_specs=in_specs,
        out_specs=out_specs,
        out_shape=out_shape,
        scratch_shapes=[
            pltpu.VMEM((2 * hidden, length), BF16),
            pltpu.VMEM((hidden, length), BF16),
            pltpu.VMEM((width, length), BF16),
        ],
        input_output_aliases=aliases,
        cost_estimate=pl.CostEstimate(
            flops=flops,
            bytes_accessed=count * (2 * 3 * hidden * width + 8 * 3 * rows * hidden),
            transcendentals=count * trees * length * hidden,
        ),
        compiler_params=params(),
        name="experts",
    )(*operands)


def left_parts_kernel(
    shards, rows, wide, first_ref, joint_ref, mixed_ref, middle_ref, sq_ref, sk_ref, sv_ref, so_ref,
    eq_ref, ep_ref, eo_ref, router_ref, gains_ref, z_ref, own_ref,
):
    qw, kv = sq_ref.shape[1], sk_ref.shape[1]
    first = first_ref[...]
    pieces = []
    for start_ref, low in ((sq_ref, 0), (sk_ref, qw), (sv_ref, qw + kv)):
        high = low + start_ref.shape[1]
        pieces.append(exact_nn(exact_nt(start_ref[...], joint_ref[:, low:high]), first))
    pieces.append(exact_nn(exact_nt(so_ref[...], middle_ref[...]), mixed_ref[...]))
    pieces.append(router_ref[...])
    pieces.append(gains_ref[...])
    for shard in range(shards):
        for k, piece in enumerate(pieces):
            z_ref[shard, :, k * wide : (k + 1) * wide] = padded(
                piece[:, shard * rows : (shard + 1) * rows], wide
            )
    errors = (
        nt(sq_ref[...], eq_ref[...], HIGHEST),
        nt(sk_ref[...], ep_ref[0], HIGHEST),
        nt(sv_ref[...], ep_ref[1], HIGHEST),
        nt(so_ref[...], eo_ref[...], HIGHEST),
    )
    for k, piece in enumerate(errors):
        own_ref[:, k * wide : (k + 1) * wide] = padded(piece, wide)


def left_parts(shards, rows, operands):
    wide = up_to(rows, 128)
    return pl.pallas_call(
        functools.partial(left_parts_kernel, shards, rows, wide),
        in_specs=vmem_specs(len(operands)),
        out_specs=vmem_specs(2),
        out_shape=[struct((shards, 8, 6 * wide)), struct((8, 4 * wide))],
        compiler_params=params(),
        name="left_parts",
    )(*operands)


def greet(reps, shards):
    rep, shard = lax.axis_index("rep"), lax.axis_index("shard")
    barrier = pltpu.get_barrier_semaphore()
    for step in range(1, shards):
        pl.semaphore_signal(
            barrier, inc=1, device_id={"shard": lax.rem(shard + step, shards)}, device_id_type=MESH
        )
    for step in range(1, reps):
        pl.semaphore_signal(
            barrier, inc=1, device_id={"rep": lax.rem(rep + step, reps)}, device_id_type=MESH
        )
    pl.semaphore_wait(barrier, reps + shards - 2)


def send_all(axis, size, source, target, send, recv):
    here = lax.axis_index(axis)
    copies = []
    for step in range(1, size):
        to = lax.rem(here + step, size)
        copy = pltpu.make_async_remote_copy(
            src_ref=source(to),
            dst_ref=target(step),
            send_sem=send.at[step - 1],
            recv_sem=recv.at[step - 1],
            device_id={axis: to},
            device_id_type=MESH,
        )
        copy.start()
        copies.append(copy)
    for copy in copies:
        copy.wait()


def blocks_on_diagonal(square):
    size = square.shape[0]
    row = lax.broadcasted_iota(jnp.int32, (size, size), 0) // 8
    lane = lax.broadcasted_iota(jnp.int32, (size, size), 1) // 8
    kept = jnp.where(row == lane, square, 0.0)
    total = kept[:8]
    for k in range(1, size // 8):
        total = total + kept[8 * k : 8 * k + 8]
    return total


def spread_on_diagonal(flat):
    size = flat.shape[1]
    tall = jnp.concatenate([flat] * (size // 8), axis=0)
    row = lax.broadcasted_iota(jnp.int32, (size, size), 0) // 8
    lane = lax.broadcasted_iota(jnp.int32, (size, size), 1) // 8
    return jnp.transpose(jnp.where(row == lane, tall, 0.0))


def left_sync_kernel(reps, shards, wide, wide_out, piece, count, *refs):
    z_ref, own_ref = refs[:2]
    lin_refs, lout_refs = refs[2 : 2 + count], refs[2 + count : 2 + 2 * count]
    left_ref, left_out_ref, totals_ref, squares_ref, leftz_ref = refs[2 + 2 * count : 7 + 2 * count]
    (zbuf, parts, heard, total, grams, lanes_z, zs, zr, ps, pr, gs, gr, hs, hr, ls, lr) = refs[
        7 + 2 * count :
    ]
    rep, shard = lax.axis_index("rep"), lax.axis_index("shard")
    greet(reps, shards)
    send_all("shard", shards, lambda to: z_ref.at[to], lambda step: zbuf.at[step - 1], zs, zr)
    front = z_ref[shard]
    for step in range(shards - 1):
        front = front + zbuf[step]
    ins = [ref[e, a] for a in range(2) for ref in lin_refs for e in range(ref.shape[0])]
    outs = [ref[e] for ref in lout_refs for e in range(ref.shape[0])]
    line = jnp.concatenate(
        [front[:, : 4 * wide] + own_ref[...], front[:, 4 * wide :], *ins, *outs], axis=1
    )
    line = padded(line, reps * piece)
    for k in range(reps):
        parts[k] = line[:, k * piece : (k + 1) * piece]
    send_all("rep", reps, lambda to: parts.at[to], lambda step: heard.at[step - 1], ps, pr)
    mine = parts[rep]
    for step in range(reps - 1):
        mine = mine + heard[step]
    total[rep] = mine
    send_all("rep", reps, lambda to: total.at[rep], lambda step: total.at[rep], gs, gr)
    line = jnp.concatenate([total[k] for k in range(reps)], axis=1)
    inner = len(ins)
    matrices = [line[:, k * wide : (k + 1) * wide] for k in range(4)]
    matrices += [line[:, (6 + k) * wide : (7 + k) * wide] for k in range(inner)]
    base = (6 + inner) * wide
    outers = [line[:, base + k * wide_out : base + (k + 1) * wide_out] for k in range(len(outs))]
    router, gains = line[:, 4 * wide : 5 * wide], line[:, 5 * wide : 6 * wide]
    size, size_out = up_to(8 * len(matrices), 128), up_to(8 * len(outers), 128)
    stack = jnp.concatenate(
        matrices + [jnp.zeros((size - 8 * len(matrices), wide), F32)], axis=0
    )
    stack_out = jnp.concatenate(
        outers + [jnp.zeros((size_out - 8 * len(outers), wide_out), F32)], axis=0
    )
    gram = blocks_on_diagonal(nt(stack, stack, HIGHEST))
    gram_out = blocks_on_diagonal(nt(stack_out, stack_out, HIGHEST))
    row = lax.broadcasted_iota(jnp.int32, (8, 128), 0)
    lane = lax.broadcasted_iota(jnp.int32, (8, 128), 1)
    more = jnp.where(lane == 0, jnp.sum(router * router, axis=1, keepdims=True), 0.0)
    more = jnp.where(lane == 1, jnp.sum(gains * gains, axis=1, keepdims=True), more)
    grams[shard] = jnp.concatenate([gram, gram_out, more], axis=1)
    send_all("shard", shards, lambda to: grams.at[shard], lambda step: grams.at[shard], hs, hr)
    gram = grams[0]
    for k in range(1, shards):
        gram = gram + grams[k]
    both = size + size_out
    squares_ref[...] = gram[:, both:]
    totals_ref[0] = router
    totals_ref[1] = gains
    where_from = lax.broadcasted_iota(jnp.int32, (both, 1024), 0)
    where_to = lax.broadcasted_iota(jnp.int32, (both, 1024), 1)
    chosen = jnp.where(
        (where_from % 8 == where_to // 128) & (where_from // 8 == where_to % 128), 1.0, 0.0
    ).astype(BF16)
    lines = exact_nn(gram[:, :both], chosen)
    used = (lane < len(matrices)) | ((lane >= size // 8) & (lane < size // 8 + len(outers)))
    table = [
        jnp.where(used, lines[:, 128 * k : 128 * k + 128], jnp.where(row == k, 1.0, 0.0))
        for k in range(8)
    ]
    inverse = [jnp.where(row == k, 1.0, 0.0) for k in range(8)]
    for k in range(8):
        pivot = table[k][k : k + 1]
        over = 1.0 / pivot
        for i in range(k + 1, 8):
            factor = table[i][k : k + 1] * over
            table[i] = table[i] - factor * table[k]
            inverse[i] = inverse[i] - factor * inverse[k]
        inverse[k] = inverse[k] / jnp.sqrt(pivot)
    flat = exact_nt(jnp.concatenate(inverse, axis=1), chosen)
    lefts = nn(spread_on_diagonal(flat[:, :size]), stack, HIGHEST)
    lefts_out = nn(spread_on_diagonal(flat[:, size:]), stack_out, HIGHEST)
    left_ref[...] = lefts[: left_ref.shape[0]]
    left_out_ref[...] = lefts_out[: left_out_ref.shape[0]]
    lanes_z[shard] = lefts[:32]
    send_all("shard", shards, lambda to: lanes_z.at[shard], lambda step: lanes_z.at[shard], ls, lr)
    leftz_ref[...] = lanes_z[...]


def left_sync(reps, shards, z_part, own, lins, louts):
    wide, wide_out = lins[0].shape[3], louts[0].shape[2]
    inner, outer = 2 * sum(x.shape[0] for x in lins), sum(x.shape[0] for x in louts)
    piece = up_to(-(-((6 + inner) * wide + outer * wide_out) // reps), 128)
    matrices = 4 + inner
    size, size_out = up_to(8 * matrices, 128), up_to(8 * outer, 128)
    dma = pltpu.SemaphoreType.DMA
    operands = [z_part, own, *lins, *louts]
    return pl.pallas_call(
        functools.partial(left_sync_kernel, reps, shards, wide, wide_out, piece, len(lins)),
        in_specs=vmem_specs(len(operands)),
        out_specs=vmem_specs(5),
        out_shape=[
            struct((8 * matrices, wide)),
            struct((8 * outer, wide_out)),
            struct((2, 8, wide)),
            struct((8, 128)),
            struct((shards, 32, wide)),
        ],
        scratch_shapes=[
            pltpu.VMEM((shards - 1, 8, 6 * wide), F32),
            pltpu.VMEM((reps, 8, piece), F32),
            pltpu.VMEM((reps - 1, 8, piece), F32),
            pltpu.VMEM((reps, 8, piece), F32),
            pltpu.VMEM((shards, 8, size + size_out + 128), F32),
            pltpu.VMEM((shards, 32, wide), F32),
            dma((shards - 1,)),
            dma((shards - 1,)),
            dma((reps - 1,)),
            dma((reps - 1,)),
            dma((reps - 1,)),
            dma((reps - 1,)),
            dma((shards - 1,)),
            dma((shards - 1,)),
            dma((shards - 1,)),
            dma((shards - 1,)),
        ],
        compiler_params=params(collective_id=1, has_side_effects=True),
        name="left_sync",
    )(*operands)


def right_expert_kernel(left_ref, left_out_ref, min_ref, mout_ref, right_ref):
    rows, out_rows = min_ref.shape[2], mout_ref.shape[1]
    hidden = min_ref.shape[3]

    def product(left, matrix):
        high, low = two_terms(left)
        both = jnp.concatenate([high.astype(F32), low.astype(F32)], axis=0).astype(BF16)
        top, rest = two_terms(matrix)
        first = nn(both, top)
        return first[:8] + first[8:] + nn(both, rest)[:8]

    for a in range(2):
        right_ref[0, :, a * hidden : (a + 1) * hidden] = product(
            left_ref[a, 0, :, :rows], min_ref[a, 0]
        )
    right_ref[0, :, 2 * hidden :] = product(left_out_ref[0, :, :out_rows], mout_ref[0])


def right_experts(lefts, lefts_out, merged_in, merged_out):
    count, rows, hidden = merged_in.shape[1:]
    out_rows, width = merged_out.shape[1:]
    wide, wide_out = lefts.shape[3], lefts_out.shape[2]
    return pl.pallas_call(
        right_expert_kernel,
        grid=(count,),
        in_specs=[
            pl.BlockSpec((2, 1, 8, wide), lambda e: (0, e, 0, 0)),
            pl.BlockSpec((1, 8, wide_out), lambda e: (e, 0, 0)),
            pl.BlockSpec((2, 1, rows, hidden), lambda e: (0, e, 0, 0)),
            pl.BlockSpec((1, out_rows, width), lambda e: (e, 0, 0)),
        ],
        out_specs=pl.BlockSpec((1, 8, 2 * hidden + width), lambda e: (e, 0, 0)),
        out_shape=struct((count, 8, 2 * hidden + width)),
        compiler_params=params(),
        name="right_experts",
    )(lefts, lefts_out, merged_in, merged_out)


def right_attention_kernel(
    shards, rows, left_ref, leftz_ref, first_ref, joint_ref, mixed_ref, middle_ref, eq_ref, ep_ref,
    eo_ref, right_ref,
):
    qw, kv = eq_ref.shape[1], ep_ref.shape[2]
    width = eo_ref.shape[1]

    def whole(k):
        return jnp.concatenate(
            [leftz_ref[z, 8 * k : 8 * k + 8, :rows] for z in range(shards)], axis=1
        )

    def own(k):
        return left_ref[8 * k : 8 * k + 8, :rows]

    first = first_ref[...]
    at = 0
    for k, error in ((0, eq_ref[...]), (1, ep_ref[0]), (2, ep_ref[1])):
        grown = exact_nn(exact_nt(whole(k), first), joint_ref[:, at : at + error.shape[1]])
        right_ref[:, at : at + error.shape[1]] = grown + nn(own(k), error, HIGHEST)
        at += error.shape[1]
    grown = exact_nn(exact_nt(whole(3), mixed_ref[...]), middle_ref[...])
    right_ref[:, at : at + width] = grown + nn(own(3), eo_ref[...], HIGHEST)


def right_attention(shards, rows, operands):
    width = operands[6].shape[1] + 2 * operands[7].shape[2] + operands[8].shape[1]
    return pl.pallas_call(
        functools.partial(right_attention_kernel, shards, rows),
        in_specs=vmem_specs(len(operands)),
        out_specs=pl.BlockSpec(memory_space=pltpu.VMEM),
        out_shape=struct((8, width)),
        compiler_params=params(),
        name="right_attention",
    )(*operands)


def right_sync_kernel(
    reps, shards, piece, experts_ref, attention_ref, out_ref, parts, heard, across, total, ps, pr,
    zs, zr, gs, gr,
):
    rep, shard = lax.axis_index("rep"), lax.axis_index("shard")
    half = piece // 2
    greet(reps, shards)
    line = jnp.concatenate(
        [experts_ref[e] for e in range(experts_ref.shape[0])] + [attention_ref[...]], axis=1
    )
    line = padded(line, reps * piece)
    for k in range(reps):
        at = k * piece
        parts[k] = jnp.concatenate(
            [line[:, at : at + half], line[:, at + half : at + piece]], axis=0
        ).astype(BF16)
    send_all("rep", reps, lambda to: parts.at[to], lambda step: heard.at[step - 1], ps, pr)
    mine = parts[rep].astype(F32)
    for step in range(reps - 1):
        mine = mine + heard[step].astype(F32)
    across[shard] = mine.astype(BF16)
    send_all("shard", shards, lambda to: across.at[shard], lambda step: across.at[shard], zs, zr)
    summed = across[0].astype(F32)
    for k in range(1, shards):
        summed = summed + across[k].astype(F32)
    total[rep] = summed.astype(BF16)
    send_all("rep", reps, lambda to: total.at[rep], lambda step: total.at[rep], gs, gr)
    for k in range(reps):
        block = total[k].astype(F32)
        out_ref[:, k * piece : k * piece + half] = block[:8]
        out_ref[:, k * piece + half : (k + 1) * piece] = block[8:]


def right_sync(reps, shards, experts, attention):
    columns = experts.shape[0] * experts.shape[2] + attention.shape[1]
    piece = up_to(-(-columns // reps), 256)
    dma = pltpu.SemaphoreType.DMA
    return pl.pallas_call(
        functools.partial(right_sync_kernel, reps, shards, piece),
        in_specs=vmem_specs(2),
        out_specs=pl.BlockSpec(memory_space=pltpu.VMEM),
        out_shape=struct((8, reps * piece)),
        scratch_shapes=[
            pltpu.VMEM((reps, 16, piece // 2), BF16),
            pltpu.VMEM((reps - 1, 16, piece // 2), BF16),
            pltpu.VMEM((shards, 16, piece // 2), BF16),
            pltpu.VMEM((reps, 16, piece // 2), BF16),
            dma((reps - 1,)),
            dma((reps - 1,)),
            dma((shards - 1,)),
            dma((shards - 1,)),
            dma((reps - 1,)),
            dma((reps - 1,)),
        ],
        compiler_params=params(collective_id=2, has_side_effects=True),
        name="right_sync",
    )(experts, attention)


def low_rank(left, right):
    high, low = two_terms(left)
    lefts = jnp.concatenate([high.astype(F32), low.astype(F32)], axis=0).astype(BF16)
    rights = jnp.concatenate([right, right], axis=0).astype(BF16)
    return tn(lefts, rights)


def feedback_expert_kernel(
    replicas, left_ref, left_out_ref, right_ref, min_ref, mout_ref, fin_ref, fout_ref, sq_ref
):
    expert = pl.program_id(0)
    rows, hidden = min_ref.shape[2:]
    out_rows = mout_ref.shape[1]
    row = lax.broadcasted_iota(jnp.int32, (8, 128), 0)
    lane = lax.broadcasted_iota(jnp.int32, (8, 128), 1)

    @pl.when(expert == 0)
    def _():
        sq_ref[...] = jnp.zeros_like(sq_ref)

    added = jnp.zeros((8, 128), F32)
    for a in range(2):
        approx = low_rank(
            left_ref[a, 0, :, :rows], right_ref[:, a * hidden : (a + 1) * hidden]
        )
        left_over = min_ref[a, 0] - approx * (1.0 / replicas)
        fin_ref[a, 0] = left_over
        added = jnp.where(lane == a, jnp.sum(left_over * left_over), added)
    approx = low_rank(left_out_ref[0, :, :out_rows], right_ref[:, 2 * hidden :])
    left_over = mout_ref[0] - approx * (1.0 / replicas)
    fout_ref[0] = left_over
    added = jnp.where(lane == 2, jnp.sum(left_over * left_over), added)
    sq_ref[...] += jnp.where(row == expert, added, 0.0)


def feedback_experts(replicas, lefts, lefts_out, rights, merged_in, merged_out):
    count, rows, hidden = merged_in.shape[1:]
    out_rows, width = merged_out.shape[1:]
    wide, wide_out = lefts.shape[3], lefts_out.shape[2]
    in_block = pl.BlockSpec((2, 1, rows, hidden), lambda e: (0, e, 0, 0))
    out_block = pl.BlockSpec((1, out_rows, width), lambda e: (e, 0, 0))
    return pl.pallas_call(
        functools.partial(feedback_expert_kernel, replicas),
        grid=(count,),
        in_specs=[
            pl.BlockSpec((2, 1, 8, wide), lambda e: (0, e, 0, 0)),
            pl.BlockSpec((1, 8, wide_out), lambda e: (e, 0, 0)),
            pl.BlockSpec((8, 2 * hidden + width), lambda e: (0, e)),
            in_block,
            out_block,
        ],
        out_specs=[in_block, out_block, pl.BlockSpec((8, 128), lambda e: (0, 0))],
        out_shape=[struct(merged_in.shape), struct(merged_out.shape), struct((8, 128))],
        compiler_params=params(),
        name="feedback_experts",
    )(lefts, lefts_out, rights, merged_in, merged_out)


def feedback_attention_kernel(
    replicas, rows, left_ref, right_ref, gj_ref, go_ref, eq_ref, ep_ref, eo_ref, fq_ref, fp_ref,
    fo_ref, sq_ref,
):
    qw, kv = eq_ref.shape[1], ep_ref.shape[2]
    lane = lax.broadcasted_iota(jnp.int32, (8, 128), 1)
    row = lax.broadcasted_iota(jnp.int32, (8, 128), 0)
    added = jnp.zeros((8, 128), F32)
    at = 0
    jobs = (
        (gj_ref, 0, eq_ref, fq_ref),
        (gj_ref, qw, ep_ref.at[0], fp_ref.at[0]),
        (gj_ref, qw + kv, ep_ref.at[1], fp_ref.at[1]),
        (go_ref, 0, eo_ref, fo_ref),
    )
    for k, (grad_ref, low, error_ref, out_ref) in enumerate(jobs):
        width = error_ref.shape[1]
        approx = low_rank(left_ref[8 * k : 8 * k + 8, :rows], right_ref[:, at : at + width])
        merged = grad_ref[:, low : low + width].astype(F32) + error_ref[...]
        left_over = merged - approx * (1.0 / replicas)
        out_ref[...] = left_over
        added = jnp.where(lane == 3 + k, jnp.sum(left_over * left_over), added)
        at += width
    sq_ref[...] = jnp.where(row == 0, added, 0.0)


def feedback_attention(replicas, rows, operands):
    shapes = [operands[k].shape for k in (4, 5, 6)]
    return pl.pallas_call(
        functools.partial(feedback_attention_kernel, replicas, rows),
        in_specs=vmem_specs(len(operands)),
        out_specs=vmem_specs(4),
        out_shape=[struct(shape) for shape in shapes] + [struct((8, 128))],
        compiler_params=params(),
        name="feedback_attention",
    )(*operands)


def squares_sync_kernel(reps, shards, a_ref, b_ref, out_ref, plane, line, ps, pr, zs, zr):
    rep, shard = lax.axis_index("rep"), lax.axis_index("shard")
    greet(reps, shards)
    plane[rep] = a_ref[...] + b_ref[...]
    send_all("rep", reps, lambda to: plane.at[rep], lambda step: plane.at[rep], ps, pr)
    summed = plane[0]
    for k in range(1, reps):
        summed = summed + plane[k]
    line[shard] = summed
    send_all("shard", shards, lambda to: line.at[shard], lambda step: line.at[shard], zs, zr)
    summed = line[0]
    for k in range(1, shards):
        summed = summed + line[k]
    out_ref[...] = summed


def squares_sync(reps, shards, first, second):
    dma = pltpu.SemaphoreType.DMA
    return pl.pallas_call(
        functools.partial(squares_sync_kernel, reps, shards),
        in_specs=vmem_specs(2),
        out_specs=pl.BlockSpec(memory_space=pltpu.VMEM),
        out_shape=struct((8, 128)),
        scratch_shapes=[
            pltpu.VMEM((reps, 8, 128), F32),
            pltpu.VMEM((shards, 8, 128), F32),
            dma((reps - 1,)),
            dma((reps - 1,)),
            dma((shards - 1,)),
            dma((shards - 1,)),
        ],
        compiler_params=params(collective_id=3, has_side_effects=True),
        name="squares_sync",
    )(first, second)


def per_device(
    tokens,
    cotangent,
    seg_ids,
    parents,
    positions,
    routes,
    query_weight,
    pair_weight,
    output_weight,
    inner_weight,
    outer_weight,
    router_weight,
    norm_gains,
    query_moment,
    pair_moment,
    output_moment,
    inner_moment,
    outer_moment,
    router_moment,
    gains_moment,
    query_error,
    pair_error,
    output_error,
    inner_error,
    outer_error,
    query_start,
    pair_start,
    output_start,
    inner_start,
    outer_start,
):
    replicas = lax.axis_size("rep")
    shard_count = lax.axis_size("shard")
    here = lax.axis_index("shard")
    both = ("rep", "shard")
    bf16 = jnp.bfloat16
    query_t = jnp.swapaxes(query_weight, 0, 1).astype(bf16)
    pair_t = jnp.swapaxes(pair_weight, 1, 2).astype(bf16)
    output_t = jnp.swapaxes(output_weight, 0, 1).astype(bf16)
    inner_t = jnp.transpose(inner_weight, (1, 0, 3, 2)).astype(bf16)
    outer_low = outer_weight.astype(bf16)
    router_t = jnp.swapaxes(router_weight, 0, 1).astype(bf16)
    gains_low = norm_gains.astype(bf16)
    own_rows = query_t.shape[1]
    q_cols, p_cols, f_cols = query_t.shape[0], pair_t.shape[1], inner_t.shape[2]
    f_rows = outer_low.shape[1]
    small = jnp.concatenate([router_t, gains_low], axis=0)
    small = jnp.pad(small, ((0, 16 - small.shape[0]), (0, 0)))
    packed = jnp.concatenate(
        [query_t, pair_t.reshape(2 * p_cols, own_rows), output_t, small], axis=0
    )
    spread = lax.all_gather(packed, both).reshape(replicas, shard_count, packed.shape[0], own_rows)

    per_chunk = E // CHUNKS
    outer_cols = outer_low.shape[2]
    paired = replicas % 2 == 0 and per_chunk == 2 and own_rows == 2 * outer_cols == 2 * f_rows
    paired = paired and 2 * f_cols == f_rows and f_cols % 16 == 0 and own_rows % 128 == 0

    def whole_weights(inner_all, outer_all):
        inner_all = inner_all.reshape(replicas, shard_count, per_chunk, 2, f_cols, own_rows)
        w1 = jnp.transpose(inner_all, (2, 3, 0, 4, 1, 5)).reshape(
            1, 1, per_chunk, 2 * replicas * f_cols, shard_count * own_rows
        )
        w2 = jnp.transpose(outer_all, (2, 1, 3, 0, 4)).reshape(
            1, per_chunk, 1, 1, shard_count * f_rows, replicas * outer_cols
        )
        return w1, w2

    if paired:
        core = lax.axis_index("rep") % 2
        outer_pairs = outer_low.reshape(CHUNKS, 2, f_rows, outer_cols)
        keep = jnp.where(core == 0, outer_pairs[:, 0], outer_pairs[:, 1])
        give = jnp.where(core == 0, outer_pairs[:, 1], outer_pairs[:, 0])
        got = lax.ppermute(give, "rep", [(i, i + 1 - 2 * (i % 2)) for i in range(replicas)])
        wide_outer = jnp.concatenate(
            [jnp.where(core == 0, keep, got), jnp.where(core == 0, got, keep)], axis=2
        )
        packs = jnp.concatenate(
            [inner_t.reshape(CHUNKS, per_chunk * 2 * f_cols, own_rows), wide_outer], axis=1
        )
        height = packs.shape[1]
        split = CHUNKS // 2
        early = z_gather(packs[:split].reshape(split * height, own_rows))
        held, spread = lax.optimization_barrier((packs[split:], spread))
        late = z_gather(held.reshape((CHUNKS - split) * height, own_rows))
        chunk_weights = []
        for index in range(CHUNKS):
            source = early if index < split else late
            at = (index % split) * height
            part = lax.all_gather(source[:, at : at + height], "rep")
            w1 = part.reshape(replicas, shard_count, 3, f_rows, own_rows)
            w2 = part.reshape(replicas // 2, 2, shard_count, 3, f_rows, own_rows)
            chunk_weights.append((w1, w2))
        _, cot_t = lax.optimization_barrier((late, jnp.transpose(cotangent)))
    else:
        chunk_weights = []
        for index in range(CHUNKS):
            span = slice(index * per_chunk, (index + 1) * per_chunk)
            chunk_weights.append(
                whole_weights(
                    lax.all_gather(inner_t[span], both),
                    lax.all_gather(outer_low[span], both).reshape(
                        replicas, shard_count, per_chunk, f_rows, outer_cols
                    ),
                )
            )
        cot_t = jnp.transpose(cotangent)

    def joined(piece):
        return jnp.transpose(piece, (0, 2, 1, 3)).reshape(-1, shard_count * own_rows)

    query_full = joined(spread[:, :, :q_cols])
    pair_full = jnp.stack(
        [
            joined(spread[:, :, q_cols + a * p_cols : q_cols + (a + 1) * p_cols])
            for a in range(2)
        ]
    )
    at = q_cols + 2 * p_cols
    output_full = joined(spread[:, :, at : at + q_cols])
    at += q_cols
    router_full = joined(spread[:1, :, at : at + E])
    gain_values = joined(spread[:1, :, at + E : at + E + 2]).astype(jnp.float32)

    upstream_slots = z_slots(cot_t)

    hidden = tokens.astype(jnp.float32)
    length = hidden.shape[0]
    position = positions[0]
    allowed = path_mask(seg_ids[0], parents[0])
    first_low = rms_norm(hidden, gain_values[0]).astype(bf16)
    query_pre = jnp.einsum("td,qd->tq", first_low, query_full, preferred_element_type=jnp.float32)
    pair_pre = jnp.einsum("td,awd->atw", first_low, pair_full, preferred_element_type=jnp.float32)
    query_rot = rotate(query_pre.reshape(length, HQ, HD), position, 1.0).astype(bf16)
    key_rot = rotate(pair_pre[0].reshape(length, HK, HD), position, 1.0).astype(bf16)
    values = pair_pre[1].reshape(length, HK, HD).astype(bf16)
    block_rows = min(512, length)
    masked, shaped = scores_of(query_rot, key_rot, allowed)
    top_score = jnp.max(masked, axis=-1, keepdims=True)
    raised = jnp.exp(masked - top_score)
    total_sum = jnp.sum(raised, axis=-1, keepdims=True)
    attention = (raised / total_sum).astype(bf16)
    lse_parts = top_score + jnp.log(total_sum)
    mixed_block = jnp.einsum(
        "kgqt,tkd->qkgd", attention, values, preferred_element_type=jnp.float32
    )
    mixed_low = mixed_block.reshape(block_rows, HQ * HD).astype(bf16)
    middle = hidden + jnp.einsum(
        "tq,dq->td", mixed_low, output_full, preferred_element_type=jnp.float32
    )
    second_low = rms_norm(middle, gain_values[1]).astype(bf16)
    logits = jnp.einsum("td,ed->te", second_low, router_full, preferred_element_type=jnp.float32)
    expert_ids = jnp.arange(E, dtype=jnp.int32)
    route_mask = jnp.any(routes[:, :, None] == expert_ids[None, None, :], axis=1)
    route_top = jnp.max(jnp.where(route_mask, logits, -1e30), axis=-1, keepdims=True)
    raised_gate = jnp.where(route_mask, jnp.exp(logits - route_top), 0.0)
    shares = raised_gate / jnp.sum(raised_gate, axis=-1, keepdims=True)
    shares_t = jnp.transpose(shares)
    shares_high = shares_t.astype(bf16)
    shares_rest = (shares_t - shares_high.astype(jnp.float32)).astype(bf16)
    second_slots = z_slots(
        jnp.concatenate([jnp.transpose(second_low), shares_high, shares_rest], axis=0)
    )

    upstream = cotangent.astype(jnp.float32)
    start_in = jnp.swapaxes(inner_start, 2, 3)
    start_out = jnp.swapaxes(outer_start, 1, 2)
    merged_experts = None
    combined = middle
    second_grad = None
    combine_parts, lins, louts = [], [], []
    for index in range(CHUNKS):
        w1, w2 = chunk_weights[index]
        done = expert_chunk(
            index * per_chunk,
            second_slots,
            upstream_slots,
            cotangent,
            w1,
            w2,
            inner_error[0],
            outer_error[0],
            start_in,
            start_out,
            merged_experts,
        )
        merged_experts = (done[0], done[1])
        combined = combined + done[2]
        second_grad = done[3] if second_grad is None else second_grad + done[3]
        combine_parts.append(done[4][:, :, 0])
        lins.append(done[5])
        louts.append(done[6])
    output = combined.astype(bf16)
    combine_grad = jnp.transpose(jnp.concatenate(combine_parts, axis=0))
    logit_low = (
        shares * (combine_grad - jnp.sum(shares * combine_grad, axis=-1, keepdims=True))
    ).astype(bf16)
    grad_router = jnp.einsum("td,te->de", second_low, logit_low, preferred_element_type=jnp.float32)
    second_grad = second_grad + jnp.einsum(
        "te,ed->td", logit_low, router_full, preferred_element_type=jnp.float32
    )
    _, second_pull = jax.vjp(rms_norm, middle, gain_values[1])
    middle_part, gain_two = second_pull(second_grad)
    middle_grad = upstream + middle_part
    middle_low = middle_grad.astype(bf16)
    grad_output = jnp.einsum("tq,td->qd", mixed_low, middle_low, preferred_element_type=jnp.float32)
    group_output = lax.psum_scatter(
        grad_output.astype(bf16), "shard", scatter_dimension=0, tiled=True
    )
    mixed_grad = jnp.einsum(
        "td,dq->tq", middle_low, output_full, preferred_element_type=jnp.float32
    ).astype(bf16)
    masked, shaped = scores_of(query_rot, key_rot, allowed)
    attention_full = jnp.exp(masked - lse_parts)
    upstream_block = mixed_grad.reshape(block_rows, HK, HQ // HK, HD)
    attn_grad = jnp.einsum(
        "qkgd,tkd->kgqt", upstream_block, values, preferred_element_type=jnp.float32
    )
    score_low = (
        attention_full * (attn_grad - jnp.sum(attention_full * attn_grad, axis=-1, keepdims=True))
    ).astype(bf16)
    query_block_grad = jnp.einsum(
        "kgqt,tkd->qkgd", score_low, key_rot, preferred_element_type=jnp.float32
    ) * HD ** (-0.5)
    query_parts = query_block_grad.reshape(block_rows, HQ, HD)
    key_rot_grad = jnp.einsum(
        "kgqt,qkgd->tkd", score_low, shaped, preferred_element_type=jnp.float32
    ) * HD ** (-0.5)
    value_grad = jnp.einsum(
        "kgqt,qkgd->tkd",
        attention_full.astype(bf16),
        upstream_block,
        preferred_element_type=jnp.float32,
    )
    query_grad = rotate(query_parts, position, -1.0).reshape(length, HQ * HD).astype(bf16)
    key_grad = rotate(key_rot_grad, position, -1.0).reshape(length, HK * HD).astype(bf16)
    value_low = value_grad.reshape(length, HK * HD).astype(bf16)
    joint_grad = jnp.concatenate([query_grad, key_grad, value_low], axis=1)
    grad_joint = jnp.einsum("td,tq->dq", first_low, joint_grad, preferred_element_type=jnp.float32)
    group_joint = lax.psum_scatter(
        grad_joint.astype(bf16), "shard", scatter_dimension=0, tiled=True
    )
    joint_full = jnp.concatenate([query_full, pair_full[0], pair_full[1]], axis=0)
    first_grad = jnp.dot(joint_grad, joint_full, preferred_element_type=jnp.float32)
    _, first_pull = jax.vjp(rms_norm, hidden, gain_values[0])
    hidden_part, gain_one = first_pull(first_grad)
    input_grad = (middle_grad + hidden_part).astype(bf16)
    grad_gains = jnp.stack([gain_one, gain_two])

    small_rows = [jnp.transpose(grad_router), jnp.pad(grad_gains, ((0, 6), (0, 0)))]
    start_q, start_o = jnp.transpose(query_start), jnp.transpose(output_start)
    start_p = jnp.swapaxes(pair_start, 1, 2)
    z_part, own_left = left_parts(
        shard_count,
        own_rows,
        (
            first_low, joint_grad, mixed_low, middle_low, start_q, start_p[0], start_p[1], start_o,
            query_error[0], pair_error[0], output_error[0], *small_rows,
        ),
    )
    left_flat, left_out_flat, totals, total_squares, left_lines = left_sync(
        replicas, shard_count, z_part, own_left, lins, louts
    )
    wide, wide_out = left_flat.shape[1], left_out_flat.shape[1]
    lefts = left_flat.reshape(-1, 8, wide)
    lefts_in = lefts[4:].reshape(2, E, 8, wide)
    lefts_out = left_out_flat.reshape(E, 8, wide_out)
    lefts_t = (
        lefts[0, :, :own_rows],
        lefts[1:3, :, :own_rows],
        lefts[3, :, :own_rows],
        lefts_in[..., :own_rows],
        lefts_out[..., :f_rows],
    )
    bases = tuple(jnp.swapaxes(left, -1, -2) for left in lefts_t)

    right_parts = right_experts(lefts_in, lefts_out, *merged_experts)
    right_rest = right_attention(
        shard_count,
        own_rows,
        (
            left_flat[:32], left_lines, first_low, joint_grad, mixed_low, middle_low,
            query_error[0], pair_error[0], output_error[0],
        ),
    )
    rights = right_sync(replicas, shard_count, right_parts, right_rest)
    hidden_units = merged_experts[0].shape[3]
    step = 2 * hidden_units + D
    by_expert = rights[:, : E * step].reshape(8, E, step)
    rest = rights[:, E * step :]
    kv = HK * HD
    rights_t = (
        rest[:, :QW],
        jnp.stack([rest[:, QW : QW + kv], rest[:, QW + kv : QW + 2 * kv]]),
        rest[:, QW + 2 * kv : QW + 2 * kv + D],
        jnp.transpose(by_expert[:, :, : 2 * hidden_units].reshape(8, E, 2, hidden_units), (2, 1, 0, 3)),
        jnp.transpose(by_expert[:, :, 2 * hidden_units :], (1, 0, 2)),
    )
    right_out = tuple(jnp.swapaxes(right, -1, -2) for right in rights_t)

    feedback_in, feedback_out, squares_experts = feedback_experts(
        replicas, lefts_in, lefts_out, rights, *merged_experts
    )
    feedback_q, feedback_p, feedback_o, squares_rest = feedback_attention(
        replicas,
        own_rows,
        (
            left_flat[:32], rest[:, : QW + 2 * kv + D], group_joint, group_output,
            query_error[0], pair_error[0], output_error[0],
        ),
    )
    feedbacks = tuple(
        part[None] for part in (feedback_q, feedback_p, feedback_o, feedback_in, feedback_out)
    )
    squares = squares_sync(replicas, shard_count, squares_experts, squares_rest)
    flat_squares = jnp.concatenate(
        [squares[0, 3:7], squares[:, 0], squares[:, 1], squares[:, 2]], axis=0
    )

    column_index = lax.axis_index("rep")
    weights_now = (query_weight, pair_weight, output_weight, inner_weight, outer_weight)
    moments_now = (query_moment, pair_moment, output_moment, inner_moment, outer_moment)
    step_rates = (
        STEP_RATE * D ** (-0.5),
        STEP_RATE * D ** (-0.5),
        STEP_RATE * (QW * 4 // TOK_DEV + 1) ** (-0.5),
        STEP_RATE * D ** (-0.5),
        STEP_RATE * (F // 2) ** (-0.5),
    )
    momenta = []
    new_masters = []
    entry_list = []
    for index in range(5):
        left, right = lefts_t[index], rights_t[index]
        columns = right.shape[-1]
        entries = left.shape[-1] * shard_count * columns
        own_columns = columns // replicas
        squared_right = jnp.sum(right * right, axis=(-2, -1))
        scale_norm = jnp.sqrt(squared_right / entries + 1e-06)
        own_right = lax.dynamic_slice_in_dim(
            right, column_index * own_columns, own_columns, axis=right.ndim - 1
        )
        direction = (
            jnp.einsum("...km,...kn->...mn", left, own_right, precision=HIGHEST)
            / scale_norm[..., None, None]
        )
        new_master, new_moment = advance(
            weights_now[index], moments_now[index], direction, step_rates[index], WEIGHT_DECAY
        )
        momenta.append(new_moment)
        new_masters.append(new_master)
        entry_list += [float(replicas * entries)] * (left.size // (8 * left.shape[-1]))
    feedback_rms = jnp.sqrt(flat_squares / jnp.array(entry_list, F32))
    router_total = jnp.transpose(totals[0, :, :own_rows])
    gains_total = totals[1, :2, :own_rows]
    router_square = jnp.sum(total_squares[:, 0])
    gains_square = total_squares[:2, 1]
    router_direction = router_total / jnp.sqrt(
        router_square / (router_total.shape[0] * shard_count * router_total.shape[1]) + 1e-06
    )
    gains_direction = (
        gains_total / jnp.sqrt(gains_square / (gains_total.shape[1] * shard_count) + 1e-06)[:, None]
    )
    router_master, router_momentum = advance(
        router_weight, router_moment, router_direction, STEP_RATE * (8 * D) ** (-0.5), WEIGHT_DECAY
    )
    gains_master, gains_momentum = advance(
        norm_gains, gains_moment, gains_direction, GAIN_RATE, 0.0
    )
    return (
        output,
        input_grad,
        *bases,
        *right_out,
        *feedbacks,
        *momenta,
        router_momentum,
        gains_momentum,
        *new_masters,
        router_master,
        gains_master,
        feedback_rms,
    )


def solution(mesh):
    in_specs = (
        P(("rep", "shard"), None),
        P(("rep", "shard"), None),
        P(("rep", "shard"), None),
        P(("rep", "shard"), None),
        P(("rep", "shard"), None),
        P(("rep", "shard"), None),
        P("shard", "rep"),
        P(None, "shard", "rep"),
        P("shard", "rep"),
        P(None, None, "shard", "rep"),
        P(None, "shard", "rep"),
        P("shard", None),
        P(None, "shard"),
        P("shard", "rep"),
        P(None, "shard", "rep"),
        P("shard", "rep"),
        P(None, None, "shard", "rep"),
        P(None, "shard", "rep"),
        P("shard", None),
        P(None, "shard"),
        P("rep", "shard", None),
        P("rep", None, "shard", None),
        P("rep", "shard", None),
        P("rep", None, None, "shard", None),
        P("rep", None, "shard", None),
        P(),
        P(),
        P(),
        P(),
        P(),
    )
    out_specs = (
        P(("rep", "shard"), None),
        P(("rep", "shard"), None),
        P("shard", None),
        P(None, "shard", None),
        P("shard", None),
        P(None, None, "shard", None),
        P(None, "shard", None),
        P(),
        P(),
        P(),
        P(),
        P(),
        P("rep", "shard", None),
        P("rep", None, "shard", None),
        P("rep", "shard", None),
        P("rep", None, None, "shard", None),
        P("rep", None, "shard", None),
        P("shard", "rep"),
        P(None, "shard", "rep"),
        P("shard", "rep"),
        P(None, None, "shard", "rep"),
        P(None, "shard", "rep"),
        P("shard", None),
        P(None, "shard"),
        P("shard", "rep"),
        P(None, "shard", "rep"),
        P("shard", "rep"),
        P(None, None, "shard", "rep"),
        P(None, "shard", "rep"),
        P("shard", None),
        P(None, "shard"),
        P(),
    )
    return jax.shard_map(
        per_device, mesh=mesh, in_specs=in_specs, out_specs=out_specs, check_vma=False
    )
```

time: 2600 us -> 1130 us (0.43)
  waiting for transfers between devices: 1630 us -> 275 us
  Pallas kernels: 0 us -> 436 us
  matrix products: 494 us -> 104 us
  blocking collectives: 184 us -> 0 us
  starting transfers between devices: 1.05 us -> 80.1 us
  other arithmetic: 113 us -> 75.7 us
    unnamed x21 -> x7, waiting for transfers between devices: 578 us -> 0.78 us
    pallas_call x0 -> x12, Pallas kernels: none -> 436 us  [the longest x4 271 us: expert_chunk(): pl.pallas_call(functools.partial(expert_kernel, first_expert, merged is n...]
    reduce_scatter x3 -> x2, waiting for transfers between devices: 398 us -> 0.01 us  [the longest x1 0.01 us: per_device(): lax.psum_scatter(grad_joint.astype(bf16), 'shard', scatter_dimension=0, t...]
    dot_general x44 -> x14, matrix products: 457 us -> 65.7 us  [the longest x5 19.6 us: per_device(): jnp.einsum('...km,...kn->...mn', left, own_right, precision=HIGHEST)]
    all_gather x7 -> x5, waiting for transfers between devices: 380 us -> 0.08 us  [the longest x4 0.06 us: per_device(): part = lax.all_gather(source[:, at:at + height], 'rep')]
    ppermute x0 -> x25, waiting for transfers between devices: none -> 274 us  [the longest x12 192 us: z_ring(): down = lax.ppermute(down, 'shard', [(i + 1, i) for i in range(size - 1)])]
    psum x3 -> x0, waiting for transfers between devices: 274 us -> none  [the longest x2 222 us: per_device(): lax.psum((local_right[0], local_right[1], local_right[2], local_right[3],...]
    all_gather x5 -> x0, blocking collectives: 95.3 us -> none  [the longest x1 26.8 us: per_device(): lax.all_gather(low_query, 'shard', axis=0, tiled=True)]
  transfers between devices with their start and end apart: 17 -> 32, of which waited for: 13 -> 18; matrix products, arithmetic and copies ran while one was open for 12% -> 25% of each run, Pallas kernels for 0% -> 31%
where the time goes in v1:
time: 1130 us
  Pallas kernels  436 us (39%)
  waiting for transfers between devices  275 us (24%)
  local copies, waits for them, and re-layouts  137 us (12%)
  matrix products  104 us (9%)
  starting transfers between devices  80.1 us (7%)
  other arithmetic  75.7 us (7%)
  between operations  18.1 us (2%)
    pallas_call x4, Pallas kernels, expert_chunk(): pl.pallas_call(functools.partial(expert_kernel, first_expert, merged is n...  271 us
    ppermute x12, waiting for transfers between devices, z_ring(): down = lax.ppermute(down, 'shard', [(i + 1, i) for i in range(size - 1)])  192 us
    ppermute x12, waiting for transfers between devices, z_ring(): up = lax.ppermute(up, 'shard', [(i, i + 1) for i in range(size - 1)])  80.8 us
    ppermute x12, starting transfers between devices, z_ring(): up = lax.ppermute(up, 'shard', [(i, i + 1) for i in range(size - 1)])  63.7 us
    pallas_call x1, Pallas kernels, left_sync(): pl.pallas_call(functools.partial(left_sync_kernel, reps, shards, wide, wi...  54.1 us
    pallas_call x1, Pallas kernels, right_sync(): pl.pallas_call(functools.partial(right_sync_kernel, reps, shards, piece),...  28.2 us
    unnamed x193, local copies, waits for them, and re-layouts  26.6 us
    pallas_call x1, Pallas kernels, feedback_experts(): pl.pallas_call(functools.partial(feedback_expert_kernel, replicas), grid=...  23 us
  transfers between devices with their start and end apart: 32, of which 18 were waited for; matrix products, arithmetic and copies ran while one was open for 25% of the time, Pallas kernels for 31%

profile of v1, /device:TPU:0, one launch (start us, length us, event | category | flops | bytes accessed | tf_op | source)
XLA Modules:
  0.0 1125.7 jit_solution(12191011611235274224)
XLA Ops:
  21.9 26.0 %collective-permute-done.19 = bf16[1152,384]{1,0:T(8,128)(2,1)S(1)} collective-permute-done((bf16[1152,384]{1,0:T(8,128)(2,1)S(1)}, bf16[1152,384]{1,0:T(8,128)(2,1)S(1)}, u32[]{:S(2)}, u32[]{:S(2)}) %collective-permute-start.19) | collective-permute-done | bytes 884768 | tf_op jit(solution)/shard_map/ppermute | solution.py:103
  59.4 22.2 %collective-permute-done.20 = bf16[1152,384]{1,0:T(8,128)(2,1)} collective-permute-done((bf16[1152,384]{1,0:T(8,128)(2,1)S(1)}, bf16[1152,384]{1,0:T(8,128)(2,1)}, u32[]{:S(2)}, u32[]{:S(2)}) %collective-permute-start.20) | collective-permute-done | bytes 884768 | tf_op jit(solution)/shard_map/ppermute | solution.py:103
  93.6 31.2 %collective-permute-done.21 = bf16[1152,384]{1,0:T(8,128)(2,1)} collective-permute-done((bf16[1152,384]{1,0:T(8,128)(2,1)}, bf16[1152,384]{1,0:T(8,128)(2,1)}, u32[]{:S(2)}, u32[]{:S(2)}) %collective-permute-start.21) | collective-permute-done | bytes 884768 | tf_op jit(solution)/shard_map/ppermute | solution.py:103
  147.2 16.3 %collective-permute-done.10 = bf16[1152,384]{1,0:T(8,128)(2,1)S(1)} collective-permute-done((bf16[1152,384]{1,0:T(8,128)(2,1)S(1)}, bf16[1152,384]{1,0:T(8,128)(2,1)S(1)}, u32[]{:S(2)}, u32[]{:S(2)}) %collective-permute-start.10) | collective-permute-done | bytes 884768 | tf_op jit(solution)/shard_map/ppermute | solution.py:104
  169.4 15.5 %collective-permute-done.11 = bf16[1152,384]{1,0:T(8,128)(2,1)S(1)} collective-permute-done((bf16[1152,384]{1,0:T(8,128)(2,1)S(1)}, bf16[1152,384]{1,0:T(8,128)(2,1)S(1)}, u32[]{:S(2)}, u32[]{:S(2)}) %collective-permute-start.11) | collective-permute-done | bytes 884768 | tf_op jit(solution)/shard_map/ppermute | solution.py:104
  190.7 14.6 %collective-permute-done.12 = bf16[1152,384]{1,0:T(8,128)(2,1)S(1)} collective-permute-done((bf16[1152,384]{1,0:T(8,128)(2,1)S(1)}, bf16[1152,384]{1,0:T(8,128)(2,1)S(1)}, u32[]{:S(2)}, u32[]{:S(2)}) %collective-permute-start.12) | collective-permute-done | bytes 884768 | tf_op jit(solution)/shard_map/ppermute | solution.py:104
  240.5 11.4 %fusion.101 = (bf16[8,4,192,384]{3,1,2,0:T(4,128)(2,1)}, bf16[8,192,4,384]{3,2,1,0:T(4,128)(2,1)}, bf16[8,4,192,384]{3,1,2,0:T(4,128)(2,1)}) fusion(bf16[8,4,464,384]{3,1,2,0:T(4,128)(2,1)} %copy-done.4), kind=kLoop, calls=%fused_computation.235 | loop fusion | bytes 23592960 | tf_op jit(solution)/shard_map/slice | solution.py:974
  317.3 29.3 %collective-permute-done.2 = bf16[1552,512]{1,0:T(8,128)(2,1)} collective-permute-done((bf16[1552,512]{1,0:T(8,128)(2,1)}, bf16[1552,512]{1,0:T(8,128)(2,1)}, u32[]{:S(2)}, u32[]{:S(2)}) %collective-permute-start.2) | collective-permute-done | bytes 1589280 | tf_op jit(solution)/shard_map/ppermute | solution.py:104
  362.5 24.3 %collective-permute-done.3 = bf16[1552,512]{1,0:T(8,128)(2,1)} collective-permute-done((bf16[1552,512]{1,0:T(8,128)(2,1)}, bf16[1552,512]{1,0:T(8,128)(2,1)}, u32[]{:S(2)}, u32[]{:S(2)}) %collective-permute-start.3) | collective-permute-done | bytes 1589280 | tf_op jit(solution)/shard_map/ppermute | solution.py:104
  393.8 26.7 %collective-permute-done.14 = bf16[1536,512]{1,0:T(8,128)(2,1)} collective-permute-done((bf16[1536,512]{1,0:T(8,128)(2,1)}, bf16[1536,512]{1,0:T(8,128)(2,1)}, u32[]{:S(2)}, u32[]{:S(2)}) %collective-permute-start.14) | collective-permute-done | bytes 1572896 | tf_op jit(solution)/shard_map/ppermute | solution.py:104
  443.7 10.9 collective-permute-done.4
  463.3 20.8 %collective-permute-done.15 = bf16[1536,512]{1,0:T(8,128)(2,1)} collective-permute-done((bf16[1536,512]{1,0:T(8,128)(2,1)}, bf16[1536,512]{1,0:T(8,128)(2,1)}, u32[]{:S(2)}, u32[]{:S(2)}) %collective-permute-start.15) | collective-permute-done | bytes 1572896 | tf_op jit(solution)/shard_map/ppermute | solution.py:104
  505.1 13.4 %collective-permute-done.16 = bf16[1536,512]{1,0:T(8,128)(2,1)} collective-permute-done((bf16[1536,512]{1,0:T(8,128)(2,1)}, bf16[1536,512]{1,0:T(8,128)(2,1)}, u32[]{:S(2)}, u32[]{:S(2)}) %collective-permute-start.16) | collective-permute-done | bytes 1572896 | tf_op jit(solution)/shard_map/ppermute | solution.py:104
  525.2 67.4 %experts.4 = (f32[2,8,384,768]{3,2,1,0:T(8,128)}, f32[8,192,1536]{2,1,0:T(8,128)}, f32[512,1536]{1,0:T(8,128)}, f32[512,1536]{1,0:T(8,128)}, f32[2,512,1]{2,1,0:...) custom-call(bf16[4,1552,512]{2,1,0:T(8,128)(2,1)} %copy.369.x_ref, ...), custom_call_target="tpu_custom_call" | custom-call | flops 43486543872 | bytes 28311552 | tf_op jit(solution)/shard_map/experts/pallas_call | solution.py:354
  592.7 67.7 %experts.5 = (f32[2,8,384,768]{3,2,1,0:T(8,128)}, f32[8,192,1536]{2,1,0:T(8,128)}, f32[512,1536]{1,0:T(8,128)}, f32[512,1536]{1,0:T(8,128)}, f32[2,512,1]{2,1,0:...) custom-call(bf16[4,1552,512]{2,1,0:T(8,128)(2,1)} %copy.369.x_ref, ...), custom_call_target="tpu_custom_call", output_to_operand_aliasing={{0}: (9, {}), {1}: (10, {})} | custom-call | flops 43486543872 | bytes 28311552 | tf_op jit(solution)/shard_map/experts/pallas_call | solution.py:354
  661.9 67.9 %experts.6 = (f32[2,8,384,768]{3,2,1,0:T(8,128)}, f32[8,192,1536]{2,1,0:T(8,128)}, f32[512,1536]{1,0:T(8,128)}, f32[512,1536]{1,0:T(8,128)}, f32[2,512,1]{2,1,0:...) custom-call(bf16[4,1552,512]{2,1,0:T(8,128)(2,1)} %copy.369.x_ref, ...), custom_call_target="tpu_custom_call", output_to_operand_aliasing={{0}: (9, {}), {1}: (10, {})} | custom-call | flops 43486543872 | bytes 28311552 | tf_op jit(solution)/shard_map/experts/pallas_call | solution.py:354
  729.9 68.1 %experts.7 = (f32[2,8,384,768]{3,2,1,0:T(8,128)}, f32[8,192,1536]{2,1,0:T(8,128)}, f32[512,1536]{1,0:T(8,128)}, f32[512,1536]{1,0:T(8,128)}, f32[2,512,1]{2,1,0:...) custom-call(bf16[4,1552,512]{2,1,0:T(8,128)(2,1)} %copy.369.x_ref, ...), custom_call_target="tpu_custom_call", output_to_operand_aliasing={{0}: (9, {}), {1}: (10, {})} | custom-call | flops 43486543872 | bytes 28311552 | tf_op jit(solution)/shard_map/experts/pallas_call | solution.py:354
  829.1 13.6 %fusion = (f32[2,6,512]{2,1,0:T(8,128)S(1)}, f32[2,512,512,6]{2,1,3,0:T(8,128)}) fusion(f32[2,6,512]{2,1,0:T(8,128)} %log_add_fusion, f32[2,512,512,6]{2,1,3,0:T(8,128)} %copy-done, pred[512,512]{0,1:T(8,128)(4,1)S(1)} %copy-done.21, bf16[512,2,128,1]{0,2,3,1:T(8,128)(2,1)} %bitcast.374, bf16[512,2,6,128]{0,3,2,1:T(8,128)(2,1)} %bitcast.350), kind=kOutput, calls=%fused_computation.2 | convolution fusion | flops 821028864 | bytes 27312128 | tf_op jit(solution)/shard_map/qkgd,tkd->kgqt/dot_general | solution.py:1078
  898.8 13.1 %left_parts.1 = (f32[4,8,2304]{2,1,0:T(8,128)}, f32[8,1536]{1,0:T(8,128)}) custom-call(bf16[512,1536]{1,0:T(8,128)(2,1)} %copy-done.16, bf16[512,2048]{1,0:T(8,128)(2,1)} %pad_maximum_fusion.4.joint_ref, bf16[512,1536]{1,0:T(8,128)(2,1)} %copy.387.mixed_ref, bf16[512,1536]{1,0:T(8,128)(2,1)} %copy-done.13, f32[8,1536]{1,0:T(8,128)} %bitcast.386, ...), custom_call_target="tpu_custom_call" | custom-call | tf_op jit(solution)/shard_map/left_parts/pallas_call | solution.py:406
  911.9 54.1 %left_sync.1 = (f32[160,384]{1,0:T(8,128)}, f32[64,256]{1,0:T(8,128)}, f32[2,8,384]{2,1,0:T(8,128)}, f32[8,128]{1,0:T(8,128)}, f32[4,32,384]{2,1,0:T(8,128)}) custom-call(f32[4,8,2304]{2,1,0:T(8,128)} %get-tuple-element.98.refs_0_, f32[8,1536]{1,0:T(8,128)} %get-tuple-element.99.refs_1_, f32[2,2,8,384]{3,2,1,0:T(8,128)} %get-tuple-element.100.refs_2_, ...), custom_call_target="tpu_custom_call" | custom-call | tf_op jit(solution)/shard_map/left_sync/pallas_call | solution.py:562
  979.9 13.2 %right_experts.1.experts_ref = f32[8,8,3072]{2,1,0:T(8,128)} custom-call(f32[2,8,8,384]{3,2,1,0:T(8,128)} %bitcast.367, f32[8,8,256]{2,1,0:T(8,128)} %bitcast.378, f32[2,8,384,768]{3,2,1,0:T(8,128)} %get-tuple-element.110.min_ref, f32[8,192,1536]{2,1,0:T(8,128)} %get-tuple-element.111.mout_ref), custom_call_target="tpu_custom_call" | custom-call | tf_op jit(solution)/shard_map/right_experts/pallas_call | solution.py:618
  993.1 28.2 %right_sync.1.right_ref = f32[8,28672]{1,0:T(8,128)} custom-call(f32[8,8,3072]{2,1,0:T(8,128)} %right_experts.1.experts_ref, f32[8,3584]{1,0:T(8,128)} %right_attention.1.attention_ref), custom_call_target="tpu_custom_call" | custom-call | tf_op jit(solution)/shard_map/right_sync/pallas_call | solution.py:708
  1021.4 23.0 %feedback_experts.1 = (f32[2,8,384,768]{3,2,1,0:T(8,128)}, f32[8,192,1536]{2,1,0:T(8,128)}, f32[8,128]{1,0:T(8,128)}) custom-call(f32[2,8,8,384]{3,2,1,0:T(8,128)} %bitcast.368, f32[8,8,256]{2,1,0:T(8,128)} %bitcast.379, f32[8,28672]{1,0:T(8,128)} %right_sync.1.right_ref, f32[2,8,384,768]{3,2,1,0:T(8,128)} %get-tuple-element.110.min_ref, ...), custom_call_target="tpu_custom_call" | custom-call | tf_op jit(solution)/shard_map/feedback_experts/pallas_call | solution.py:771
  1101.0 15.2 %squares_sync.1 = f32[8,128]{1,0:T(8,128)} custom-call(f32[8,128]{1,0:T(8,128)} %get-tuple-element.120.a_ref, f32[8,128]{1,0:T(8,128)} %get-tuple-element.121.b_ref), custom_call_target="tpu_custom_call" | custom-call | tf_op jit(solution)/shard_map/squares_sync/pallas_call | solution.py:844
  (401 shorter events, 413.4 us)
Async XLA Ops:
  7.2 134.0 %all-gather.11.cloned.1.call-start = ((), (), s32[]{:S(2)}) async-start(), calls=%async_computation.4 | async-start | bytes 11759616 | tf_op jit(solution)/shard_map/all_gather | solution.py:914
  11.6 513.6 %all-gather.13.cloned.1.call-start = ((), (), s32[]{:S(2)}) async-start(), calls=%async_computation.5 | async-start | bytes 15925248 | tf_op jit(solution)/shard_map/all_gather | solution.py:952
  20.6 37.5 %collective-permute-start.22 = (bf16[1152,384]{1,0:T(8,128)(2,1)S(1)}, bf16[1152,384]{1,0:T(8,128)(2,1)S(1)}, u32[]{:S(2)}, u32[]{:S(2)}) collective-permute-start(bf16[1152,384]{1,0:T(8,128)(2,1)S(1)} %bitcast.360), channel_id=1, source_target_pairs={{1,0},{2,1},{3,2},{5,4},{6,5},{7,6},{9,8},{10,9},{11,10},{13,12},{... | collective-permute-start | bytes 2654216 | tf_op jit(solution)/shard_map/ppermute | solution.py:104
  47.9 33.7 %collective-permute-start.20 = (bf16[1152,384]{1,0:T(8,128)(2,1)S(1)}, bf16[1152,384]{1,0:T(8,128)(2,1)}, u32[]{:S(2)}, u32[]{:S(2)}) collective-permute-start(bf16[1152,384]{1,0:T(8,128)(2,1)S(1)} %collective-permute-done.19), channel_id=1, source_target_pairs={{0,1},{1,2},{2,3},{4,5},{5,6},{6,7},{8,9},{9,10},{10,11},{12,13},{... | collective-permute-start | bytes 2654216 | tf_op jit(solution)/shard_map/ppermute | solution.py:103
  58.1 34.2 %collective-permute-start.23 = (bf16[1152,384]{1,0:T(8,128)(2,1)S(1)}, bf16[1152,384]{1,0:T(8,128)(2,1)}, u32[]{:S(2)}, u32[]{:S(2)}) collective-permute-start(bf16[1152,384]{1,0:T(8,128)(2,1)S(1)} %collective-permute-done.22), channel_id=1, source_target_pairs={{1,0},{2,1},{3,2},{5,4},{6,5},{7,6},{9,8},{10,9},{11,10},{13,12},{... | collective-permute-start | bytes 2654216 | tf_op jit(solution)/shard_map/ppermute | solution.py:104
  81.6 43.2 %collective-permute-start.21 = (bf16[1152,384]{1,0:T(8,128)(2,1)}, bf16[1152,384]{1,0:T(8,128)(2,1)}, u32[]{:S(2)}, u32[]{:S(2)}) collective-permute-start(bf16[1152,384]{1,0:T(8,128)(2,1)} %collective-permute-done.20), channel_id=1, source_target_pairs={{0,1},{1,2},{2,3},{4,5},{5,6},{6,7},{8,9},{9,10},{10,11},{12,13},{... | collective-permute-start | bytes 2654216 | tf_op jit(solution)/shard_map/ppermute | solution.py:103
  92.3 43.1 %collective-permute-start.24 = (bf16[1152,384]{1,0:T(8,128)(2,1)}, bf16[1152,384]{1,0:T(8,128)(2,1)}, u32[]{:S(2)}, u32[]{:S(2)}) collective-permute-start(bf16[1152,384]{1,0:T(8,128)(2,1)} %collective-permute-done.23), channel_id=1, source_target_pairs={{1,0},{2,1},{3,2},{5,4},{6,5},{7,6},{9,8},{10,9},{11,10},{13,12},{... | collective-permute-start | bytes 2654216 | tf_op jit(solution)/shard_map/ppermute | solution.py:104
  140.5 452.2 %all-gather.15.cloned.1.call-start = ((), (), s32[]{:S(2)}) async-start(), calls=%async_computation.6 | async-start | bytes 15925248 | tf_op jit(solution)/shard_map/all_gather | solution.py:952
  141.2 520.7 %all-gather.17.cloned.1.call-start = ((), (), s32[]{:S(2)}) async-start(), calls=%async_computation.7 | async-start | bytes 15925248 | tf_op jit(solution)/shard_map/all_gather | solution.py:952
  210.1 519.8 %all-gather.19.cloned.1.call-start = ((), (), s32[]{:S(2)}) async-start(), calls=%async_computation.8 | async-start | bytes 15925248 | tf_op jit(solution)/shard_map/all_gather | solution.py:952
  280.3 813.8 %reduce-scatter.5.cloned.1.call-start = ((), (), s32[]{:S(2)}) async-start(), calls=%async_computation.3 | async-start | bytes 5898240 | tf_op jit(solution)/shard_map/reduce_scatter | solution.py:1069
  309.4 37.1 %collective-permute-start.2 = (bf16[1552,512]{1,0:T(8,128)(2,1)}, bf16[1552,512]{1,0:T(8,128)(2,1)}, u32[]{:S(2)}, u32[]{:S(2)}) collective-permute-start(bf16[1552,512]{1,0:T(8,128)(2,1)} %copy.360), channel_id=1, source_target_pairs={{1,0},{2,1},{3,2},{5,4},{6,5},{7,6},{9,8},{10,9},{11,10},{13,12},{... | collective-permute-start | bytes 4767752 | tf_op jit(solution)/shard_map/ppermute | solution.py:104
  310.7 37.1 %collective-permute-start.1 = (bf16[1552,512]{1,0:T(8,128)(2,1)}, bf16[1552,512]{1,0:T(8,128)(2,1)}, u32[]{:S(2)}, u32[]{:S(2)}) collective-permute-start(bf16[1552,512]{1,0:T(8,128)(2,1)} %copy.360), channel_id=1, source_target_pairs={{0,1},{1,2},{2,3},{4,5},{5,6},{6,7},{8,9},{9,10},{10,11},{12,13},{... | collective-permute-start | bytes 4767752 | tf_op jit(solution)/shard_map/ppermute | solution.py:103
  346.5 40.3 %collective-permute-start.3 = (bf16[1552,512]{1,0:T(8,128)(2,1)}, bf16[1552,512]{1,0:T(8,128)(2,1)}, u32[]{:S(2)}, u32[]{:S(2)}) collective-permute-start(bf16[1552,512]{1,0:T(8,128)(2,1)} %collective-permute-done.2), channel_id=1, source_target_pairs={{1,0},{2,1},{3,2},{5,4},{6,5},{7,6},{9,8},{10,9},{11,10},{13,12},{... | collective-permute-start | bytes 4767752 | tf_op jit(solution)/shard_map/ppermute | solution.py:104
  347.8 40.4 %collective-permute-start.5 = (bf16[1552,512]{1,0:T(8,128)(2,1)}, bf16[1552,512]{1,0:T(8,128)(2,1)}, u32[]{:S(2)}, u32[]{:S(2)}) collective-permute-start(bf16[1552,512]{1,0:T(8,128)(2,1)} %collective-permute-done.1), channel_id=1, source_target_pairs={{0,1},{1,2},{2,3},{4,5},{5,6},{6,7},{8,9},{9,10},{10,11},{12,13},{... | collective-permute-start | bytes 4767752 | tf_op jit(solution)/shard_map/ppermute | solution.py:103
  355.5 65.0 %collective-permute-start.14 = (bf16[1536,512]{1,0:T(8,128)(2,1)}, bf16[1536,512]{1,0:T(8,128)(2,1)}, u32[]{:S(2)}, u32[]{:S(2)}) collective-permute-start(bf16[1536,512]{1,0:T(8,128)(2,1)} %bitcast.346), channel_id=1, source_target_pairs={{1,0},{2,1},{3,2},{5,4},{6,5},{7,6},{9,8},{10,9},{11,10},{13,12},{... | collective-permute-start | bytes 4718600 | tf_op jit(solution)/shard_map/ppermute | solution.py:104
  356.8 78.3 %collective-permute-start.13 = (bf16[1536,512]{1,0:T(8,128)(2,1)}, bf16[1536,512]{1,0:T(8,128)(2,1)}, u32[]{:S(2)}, u32[]{:S(2)}) collective-permute-start(bf16[1536,512]{1,0:T(8,128)(2,1)} %bitcast.347), channel_id=1, source_target_pairs={{0,1},{1,2},{2,3},{4,5},{5,6},{6,7},{8,9},{9,10},{10,11},{12,13},{... | collective-permute-start | bytes 4718600 | tf_op jit(solution)/shard_map/ppermute | solution.py:103
  386.8 67.8 %collective-permute-start.4 = (bf16[1552,512]{1,0:T(8,128)(2,1)}, bf16[1552,512]{1,0:T(8,128)(2,1)}, u32[]{:S(2)}, u32[]{:S(2)}) collective-permute-start(bf16[1552,512]{1,0:T(8,128)(2,1)} %collective-permute-done.3), channel_id=1, source_target_pairs={{1,0},{2,1},{3,2},{5,4},{6,5},{7,6},{9,8},{10,9},{11,10},{13,12},{... | collective-permute-start | bytes 4767752 | tf_op jit(solution)/shard_map/ppermute | solution.py:104
  388.3 69.8 %collective-permute-start.6 = (bf16[1552,512]{1,0:T(8,128)(2,1)}, bf16[1552,512]{1,0:T(8,128)(2,1)}, u32[]{:S(2)}, u32[]{:S(2)}) collective-permute-start(bf16[1552,512]{1,0:T(8,128)(2,1)} %collective-permute-done.5), channel_id=1, source_target_pairs={{0,1},{1,2},{2,3},{4,5},{5,6},{6,7},{8,9},{9,10},{10,11},{12,13},{... | collective-permute-start | bytes 4767752 | tf_op jit(solution)/shard_map/ppermute | solution.py:103
  420.5 63.6 %collective-permute-start.15 = (bf16[1536,512]{1,0:T(8,128)(2,1)}, bf16[1536,512]{1,0:T(8,128)(2,1)}, u32[]{:S(2)}, u32[]{:S(2)}) collective-permute-start(bf16[1536,512]{1,0:T(8,128)(2,1)} %collective-permute-done.14), channel_id=1, source_target_pairs={{1,0},{2,1},{3,2},{5,4},{6,5},{7,6},{9,8},{10,9},{11,10},{13,12},{... | collective-permute-start | bytes 4718600 | tf_op jit(solution)/shard_map/ppermute | solution.py:104
  435.1 50.5 %collective-permute-start.17 = (bf16[1536,512]{1,0:T(8,128)(2,1)}, bf16[1536,512]{1,0:T(8,128)(2,1)}, u32[]{:S(2)}, u32[]{:S(2)}) collective-permute-start(bf16[1536,512]{1,0:T(8,128)(2,1)} %collective-permute-done.13), channel_id=1, source_target_pairs={{0,1},{1,2},{2,3},{4,5},{5,6},{6,7},{8,9},{9,10},{10,11},{12,13},{... | collective-permute-start | bytes 4718600 | tf_op jit(solution)/shard_map/ppermute | solution.py:103
  484.1 34.5 %collective-permute-start.16 = (bf16[1536,512]{1,0:T(8,128)(2,1)}, bf16[1536,512]{1,0:T(8,128)(2,1)}, u32[]{:S(2)}, u32[]{:S(2)}) collective-permute-start(bf16[1536,512]{1,0:T(8,128)(2,1)} %collective-permute-done.15), channel_id=1, source_target_pairs={{1,0},{2,1},{3,2},{5,4},{6,5},{7,6},{9,8},{10,9},{11,10},{13,12},{... | collective-permute-start | bytes 4718600 | tf_op jit(solution)/shard_map/ppermute | solution.py:104
  485.6 34.5 %collective-permute-start.18 = (bf16[1536,512]{1,0:T(8,128)(2,1)}, bf16[1536,512]{1,0:T(8,128)(2,1)S(1)}, u32[]{:S(2)}, u32[]{:S(2)}) collective-permute-start(bf16[1536,512]{1,0:T(8,128)(2,1)} %collective-permute-done.17), channel_id=1, source_target_pairs={{0,1},{1,2},{2,3},{4,5},{5,6},{6,7},{8,9},{9,10},{10,11},{12,13},{... | collective-permute-start | bytes 4718600 | tf_op jit(solution)/shard_map/ppermute | solution.py:103
  817.4 276.7 %reduce-scatter.3.cloned.1.call-start = ((), (), s32[]{:S(2)}) async-start(), calls=%async_computation.2 | async-start | bytes 7864320 | tf_op jit(solution)/shard_map/reduce_scatter | solution.py:1102
  (100 other events, 1276.3 us)
Sparse Core Ops, SparseCore 0:
  11.7 119.6 all-gather.10
  140.6 78.4 all-gather.12
  221.5 78.7 all-gather.14
  302.7 78.7 all-gather.16
  383.8 78.7 all-gather.18
  817.5 86.1 reduce-scatter.4
  906.0 123.8 reduce-scatter.2

commit v2 on v1

--- a/solution.py
+++ b/solution.py
@@ -32,19 +32,6 @@
     )
 
 
-def rotate(heads_in, position, handed):
-    half_size = heads_in.shape[-1] // 2
-    frequency = ROPE_BASE ** (-2.0 * jnp.arange(half_size, dtype=jnp.float32) / heads_in.shape[-1])
-    angles = position.astype(jnp.float32)[:, None] * frequency[None, :]
-    cosine = jnp.cos(angles)[:, None, :]
-    sine_part = handed * jnp.sin(angles)[:, None, :]
-    former = heads_in[..., :half_size]
-    latter = heads_in[..., half_size:]
-    return jnp.concatenate(
-        [former * cosine - latter * sine_part, latter * cosine + former * sine_part], axis=-1
-    )
-
-
 def path_mask(segment, parent_row):
     table_ids = jnp.arange(parent_row.shape[0], dtype=jnp.int32)
     parent_one = jnp.sum(
@@ -66,18 +53,6 @@
         | (segment[None, :] == parent_one[:, None])
         | (segment[None, :] == parent_two[:, None])
     )
-
-
-def scores_of(query_block, key_rot, mask_block):
-    rows_here = query_block.shape[0]
-    key_heads = key_rot.shape[1]
-    shaped = query_block.reshape(
-        rows_here, key_heads, query_block.shape[1] // key_heads, query_block.shape[2]
-    )
-    raw = jnp.einsum(
-        "qkgd,tkd->kgqt", shaped, key_rot, preferred_element_type=jnp.float32
-    ) * query_block.shape[2] ** (-0.5)
-    return (jnp.where(mask_block[None, None], raw, -1e30), shaped)
 
 
 def advance(weight_now, moment_now, direction, step_rate, decay_rate):
@@ -94,38 +69,12 @@
 BF16 = jnp.bfloat16
 
 
-def z_ring(block):
+def z_slots(block):
     size = lax.axis_size("shard")
-    here = lax.axis_index("shard")
-    up = down = block
-    ups, downs = [block], [block]
-    for _ in range(size - 1):
-        up = lax.ppermute(up, "shard", [(i, i + 1) for i in range(size - 1)])
-        down = lax.ppermute(down, "shard", [(i + 1, i) for i in range(size - 1)])
-        ups.append(up)
-        downs.append(down)
-    return here, ups, downs
-
-
-def z_gather(block):
-    here, ups, downs = z_ring(block)
-    size = len(ups)
-    parts = []
-    for k in range(size):
-        part = ups[0]
-        for other in range(size):
-            if other > k:
-                part = jnp.where(here == other, ups[other - k], part)
-            elif other < k:
-                part = jnp.where(here == other, downs[k - other], part)
-        parts.append(part)
-    return jnp.stack(parts)
-
-
-def z_slots(block):
-    here, ups, downs = z_ring(block)
-    size = len(ups)
-    return jnp.stack([block] + [jnp.where(here >= j, ups[j], downs[size - j]) for j in range(1, size)])
+    return [block] + [
+        lax.ppermute(block, "shard", [(i, (i + step) % size) for i in range(size)])
+        for step in range(1, size)
+    ]
 
 
 def nn(a, b, precision=None):
@@ -191,65 +140,184 @@
     return jax.ShapeDtypeStruct(shape, dtype)
 
 
-def expert_kernel(
-    first_expert,
-    aliased,
-    x_ref,
-    u_ref,
-    up_ref,
-    w1_ref,
-    w2_ref,
-    err_in_ref,
-    err_out_ref,
-    start_in_ref,
-    start_out_ref,
-    *rest,
+def turn_heads(value, cosine, sine):
+    return value * cosine + pltpu.roll(value, HD // 2, 1) * sine
+
+
+def softmax_of(query, key, mask):
+    raw = nt(query, key) * HD ** (-0.5)
+    masked = jnp.where(mask > 0, raw, -1e30)
+    raised = jnp.exp(masked - jnp.max(masked, axis=-1, keepdims=True))
+    return raised / jnp.sum(raised, axis=-1, keepdims=True)
+
+
+def head_lanes(head):
+    return pl.ds(pl.multiple_of(head * HD, HD), HD)
+
+
+def attention_forward_kernel(
+    first_ref, query_ref, key_ref, value_ref, output_ref, tokens_ref, cosine_ref, sine_ref, mask_ref,
+    qrot_ref, krot_ref, values_ref, mixed_ref, middle_ref,
 ):
-    if aliased:
-        rest = rest[2:]
-    min_ref, mout_ref, y_ref, sg_ref, cg_ref, lin_ref, lout_ref, gt_ref, act_ref, br_ref = rest
-    expert = first_expert + pl.program_id(0)
-    tree = pl.program_id(1)
-    width = up_ref.shape[1]
+    first = first_ref[...]
+    cosine, sine = cosine_ref[...], sine_ref[...]
+    values_ref[...] = nt(first, value_ref[...]).astype(BF16)
+    keys = nt(first, key_ref[...])
+    for g in range(HK):
+        span = slice(g * HD, (g + 1) * HD)
+        krot_ref[:, span] = turn_heads(keys[:, span], cosine, sine).astype(BF16)
+    queries = nt(first, query_ref[...])
+    for h in range(HQ):
+        span = slice(h * HD, (h + 1) * HD)
+        qrot_ref[:, span] = turn_heads(queries[:, span], cosine, sine).astype(BF16)
+
+    @pl.loop(0, HQ)
+    def _(head):
+        group = head_lanes(head // (HQ // HK))
+        share = softmax_of(qrot_ref[:, head_lanes(head)], krot_ref[:, group], mask_ref[...])
+        mixed_ref[:, head_lanes(head)] = nn(share.astype(BF16), values_ref[:, group]).astype(BF16)
+
+    middle_ref[...] = tokens_ref[...].astype(F32) + nt(mixed_ref[...], output_ref[...])
+
+
+def attention_forward(operands):
+    length, width = operands[0].shape
+    kv = HK * HD
+    return pl.pallas_call(
+        attention_forward_kernel,
+        in_specs=vmem_specs(len(operands)),
+        out_specs=vmem_specs(5),
+        out_shape=[
+            struct((length, HQ * HD), BF16),
+            struct((length, kv), BF16),
+            struct((length, kv), BF16),
+            struct((length, HQ * HD), BF16),
+            struct((length, width)),
+        ],
+        cost_estimate=pl.CostEstimate(
+            flops=2 * length * width * (2 * HQ * HD + 2 * kv) + 4 * HQ * HD * length * length,
+            bytes_accessed=14 * length * width + 4 * width * HQ * HD,
+            transcendentals=HQ * length * length,
+        ),
+        compiler_params=params(),
+        name="attention_forward",
+    )(*operands)
+
+
+def attention_backward_kernel(
+    middle_ref, output_ref, qrot_ref, krot_ref, values_ref, cosine_ref, sine_ref, mask_ref, late_ref,
+    joint_ref, mixed_ref, dk_ref, dv_ref,
+):
+    cosine, sine = cosine_ref[...], -sine_ref[...]
+    mixed_ref[...] = nn(middle_ref[...], output_ref[...]).astype(BF16)
+    dk_ref[...] = jnp.zeros_like(dk_ref)
+    dv_ref[...] = jnp.zeros_like(dv_ref)
+
+    @pl.loop(0, HQ)
+    def _(head):
+        lanes, group = head_lanes(head), head_lanes(head // (HQ // HK))
+        query, key = qrot_ref[:, lanes], krot_ref[:, group]
+        upstream = mixed_ref[:, lanes]
+        share = softmax_of(query, key, mask_ref[...])
+        grad = nt(upstream, values_ref[:, group])
+        score = share * (grad - jnp.sum(share * grad, axis=-1, keepdims=True))
+        score = score.astype(BF16)
+        turned = nn(score, key) * HD ** (-0.5)
+        joint_ref[:, lanes] = turn_heads(turned, cosine, sine).astype(BF16)
+        dk_ref[:, group] += tn(score, query)
+        dv_ref[:, group] += tn(share.astype(BF16), upstream)
+
+    qw = HQ * HD
+    for g in range(HK):
+        span = slice(g * HD, (g + 1) * HD)
+        turned = dk_ref[:, span] * HD ** (-0.5)
+        joint_ref[:, qw + g * HD : qw + (g + 1) * HD] = turn_heads(turned, cosine, sine).astype(BF16)
+    joint_ref[:, qw + HK * HD :] = dv_ref[...].astype(BF16)
+
+
+def attention_backward(operands):
+    length, width = operands[0].shape
+    kv = HK * HD
+    return pl.pallas_call(
+        attention_backward_kernel,
+        in_specs=vmem_specs(len(operands)),
+        out_specs=pl.BlockSpec(memory_space=pltpu.VMEM),
+        out_shape=struct((length, HQ * HD + 2 * kv), BF16),
+        scratch_shapes=[
+            pltpu.VMEM((length, HQ * HD), BF16),
+            pltpu.VMEM((length, kv), F32),
+            pltpu.VMEM((length, kv), F32),
+        ],
+        cost_estimate=pl.CostEstimate(
+            flops=8 * length * width * HQ * HD, bytes_accessed=length * width, transcendentals=0
+        ),
+        compiler_params=params(),
+        name="attention_backward",
+    )(*operands)
+
+
+def weights_of(w1_ref, w2_ref, turned):
+    here = lax.axis_index("shard")
     groups, lanes, _, double, span1 = w1_ref.shape
     f_cols = double // 2
-    hidden = groups * f_cols
     lanes2, _, groups2, _, f_rows, span2 = w2_ref.shape
-    rows = min_ref.shape[2]
-    out_rows = mout_ref.shape[1]
-    here = lax.axis_index("shard")
-
-    def first_weight(a, low, high):
-        parts = [
-            w1_ref[low:high, k, 0, a * f_cols : (a + 1) * f_cols, :].reshape(
-                (high - low) * f_cols, span1
+
+    def joined(parts):
+        return parts[0] if len(parts) == 1 else jnp.concatenate(parts, axis=1)
+
+    def place(k, count):
+        return lax.rem(here + (count - k), count) if turned else k
+
+    def both():
+        return joined(
+            [
+                w1_ref[:, place(k, lanes), 0].reshape(groups * double, span1)
+                for k in range(lanes)
+            ]
+        )
+
+    def first(a):
+        return joined(
+            [
+                w1_ref[:, place(k, lanes), 0, a * f_cols : (a + 1) * f_cols, :].reshape(
+                    groups * f_cols, span1
+                )
+                for k in range(lanes)
+            ]
+        )
+
+    def second():
+        if not turned:
+            return joined(
+                [w2_ref[k, 0, :, 0].reshape(groups2 * f_rows, span2) for k in range(lanes2)]
             )
-            for k in range(lanes)
-        ]
-        return parts[0] if lanes == 1 else jnp.concatenate(parts, axis=1)
-
-    def second_weight(low, high):
-        parts = [
-            w2_ref[k, 0, low:high, 0, :, :].reshape((high - low) * f_rows, span2)
-            for k in range(lanes2)
-        ]
-        return parts[0] if lanes2 == 1 else jnp.concatenate(parts, axis=1)
-
-    x = x_ref[0, :width, :]
-    tail = x_ref[0, width:, :].astype(F32)
+        return jnp.concatenate(
+            [
+                joined([w2_ref[k, 0, place(g, groups2), 0] for k in range(lanes2)])
+                for g in range(groups2)
+            ],
+            axis=0,
+        )
+
+    return groups, f_cols, both, first, second
+
+
+def share_of(x_ref, expert, width):
+    tail = x_ref[width : width + 2 * E, :].astype(F32)
     shares8 = tail[:E] + tail[E:]
     picked = lax.broadcasted_iota(jnp.int32, shares8.shape, 0) == expert
-    share = jnp.sum(jnp.where(picked, shares8, 0.0), axis=0, keepdims=True)
-    br_ref[...] = (share * u_ref[0].astype(F32)).astype(BF16)
-    halves = 2 if groups % 2 == 0 and groups2 % 2 == 0 else 1
-    half = hidden // halves
-    for part in range(halves):
-        span = slice(part * half, (part + 1) * half)
-        g_low, g_high = part * groups // halves, (part + 1) * groups // halves
-        h_low, h_high = part * groups2 // halves, (part + 1) * groups2 // halves
-        gate = nn(first_weight(0, g_low, g_high), x)
-        up = nn(first_weight(1, g_low, g_high), x)
-        act_grad = nn(second_weight(h_low, h_high), br_ref[...])
+    return jnp.sum(jnp.where(picked, shares8, 0.0), axis=0, keepdims=True)
+
+
+def hidden_backward(x, w1_ref, w2_ref, turned, br, act_ref, gt_ref, lanes):
+    groups, f_cols, both, _, second = weights_of(w1_ref, w2_ref, turned)
+    hidden = groups * f_cols
+    units = nn(both(), x)
+    act_grads = nn(second(), br)
+    for r in range(groups):
+        gate = units[2 * r * f_cols : (2 * r + 1) * f_cols]
+        up = units[(2 * r + 1) * f_cols : (2 * r + 2) * f_cols]
+        act_grad = act_grads[r * f_cols : (r + 1) * f_cols]
         square = gate * gate
         bent = jnp.tanh(GELU_C * (gate + GELU_A * (square * gate)))
         lifted = 0.5 * (1.0 + bent)
@@ -257,119 +325,403 @@
         slope = lifted + 0.5 * gate * (1.0 - bent * bent) * (
             GELU_C * (1.0 + 3.0 * GELU_A * square)
         )
-        act_ref[span, :] = (gelu * up).astype(BF16)
-        gt_ref[span, :] = (act_grad * up * slope).astype(BF16)
-        gt_ref[hidden + part * half : hidden + (part + 1) * half, :] = (act_grad * gelu).astype(
-            BF16
-        )
-
-    @pl.when(tree == 0)
+        act_ref[r * f_cols : (r + 1) * f_cols, lanes] = (gelu * up).astype(BF16)
+        gt_ref[r * f_cols : (r + 1) * f_cols, lanes] = (act_grad * up * slope).astype(BF16)
+        gt_ref[hidden + r * f_cols : hidden + (r + 1) * f_cols, lanes] = (
+            act_grad * gelu
+        ).astype(BF16)
+
+
+def start_product(start, matrix):
+    high, low = two_terms(start)
+    both = jnp.concatenate([high.astype(F32), low.astype(F32)], axis=0).astype(BF16)
+    top, rest = two_terms(matrix)
+    first = nt(both, top)
+    return first[:8] + first[8:] + nt(both, rest)[:8]
+
+
+def own_kernel(
+    first_expert, turned, x_ref, u_ref, up_ref, w1_ref, w2_ref, err_in_ref, err_out_ref, gate_ref,
+    min_ref, mout_ref, y_ref, sg_ref, cg_ref, gt_ref, act_ref, br_ref,
+):
+    expert = first_expert + pl.program_id(0)
+    width = up_ref.shape[1]
+    _, _, _, first_weight, second_weight = weights_of(w1_ref, w2_ref, turned)
+    rows, out_rows = min_ref.shape[2], mout_ref.shape[1]
+    hidden = min_ref.shape[3]
+    here = lax.axis_index("shard")
+    share = share_of(x_ref, expert, width)
+    br_ref[...] = (share * u_ref[...].astype(F32)).astype(BF16)
+    hidden_backward(
+        x_ref[:width, :], w1_ref, w2_ref, turned, br_ref[...], act_ref, gt_ref, slice(None)
+    )
+    own_x = x_ref[pl.ds(pl.multiple_of(here * rows, 16), rows), :]
+    for a in range(2):
+        min_ref[a, 0] = err_in_ref[a, 0] + nt(own_x, gt_ref[a * hidden : (a + 1) * hidden, :])
+    own_act = act_ref[pl.ds(pl.multiple_of(here * out_rows, 16), out_rows), :]
+    mout_ref[0] = err_out_ref[0] + nt(own_act, br_ref[...])
+    expert_out = tn(act_ref[...], second_weight())
+    cg_ref[0] = jnp.sum(up_ref[...].astype(F32) * expert_out, axis=1, keepdims=True)
+    share_col = jnp.transpose(jnp.broadcast_to(share, (8, share.shape[1])))[:, :1]
+    added = share_col * expert_out
+    grown = tn(gt_ref[:hidden, :], first_weight(0)) + tn(gt_ref[hidden:, :], first_weight(1))
+
+    @pl.when(pl.program_id(0) == 0)
     def _():
-        min_ref[...] = err_in_ref[...]
-        mout_ref[...] = err_out_ref[...]
-
-    own_x = x_ref[0, pl.ds(pl.multiple_of(here * rows, 16), rows), :]
-    min_ref[0, 0] += nt(own_x, gt_ref[:hidden, :])
-    min_ref[1, 0] += nt(own_x, gt_ref[hidden:, :])
+        y_ref[...] = added
+        sg_ref[...] = grown
+
+    @pl.when(pl.program_id(0) > 0)
+    def _():
+        y_ref[...] += added
+        sg_ref[...] += grown
+
+
+def rest_kernel(
+    first_expert, trees, last, turned, w1_ref, w2_ref, start_in_ref, start_out_ref, min_in_ref,
+    mout_in_ref, *rest,
+):
+    x_refs, u_refs = rest[:trees], rest[trees : 2 * trees]
+    min_ref, mout_ref = rest[2 * trees + 1 : 2 * trees + 3]
+    gt_ref, act_ref, br_ref = rest[-3:]
+    expert = first_expert + pl.program_id(0)
+    rows, out_rows = min_ref.shape[2], mout_ref.shape[1]
+    hidden, width = min_ref.shape[3], mout_ref.shape[2]
+    length = x_refs[0].shape[1]
+    here = lax.axis_index("shard")
+    for tree in range(trees):
+        x_ref = x_refs[tree]
+        lanes = slice(tree * length, (tree + 1) * length)
+        share = share_of(x_ref, expert, width)
+        br_ref[:, lanes] = (share * u_refs[tree][...].astype(F32)).astype(BF16)
+        hidden_backward(
+            x_ref[:width, :], w1_ref, w2_ref, turned, br_ref[:, lanes], act_ref, gt_ref, lanes
+        )
+    own_x = jnp.concatenate(
+        [x_ref[pl.ds(pl.multiple_of(here * rows, 16), rows), :] for x_ref in x_refs], axis=1
+    )
+    for a in range(2):
+        min_ref[a, 0] = min_in_ref[a, 0] + nt(own_x, gt_ref[a * hidden : (a + 1) * hidden, :])
     own_act = act_ref[pl.ds(pl.multiple_of(here * out_rows, 16), out_rows), :]
-    mout_ref[0] += nt(own_act, br_ref[...])
-
-    @pl.when(tree == 0)
-    def _():
-        expert_out = tn(act_ref[...], second_weight(0, groups2))
-        cg_ref[0] = jnp.sum(up_ref[...].astype(F32) * expert_out, axis=1, keepdims=True)
-        share_col = jnp.transpose(jnp.broadcast_to(share, (8, share.shape[1])))[:, :1]
-        added = share_col * expert_out
-        grown = tn(gt_ref[:hidden, :], first_weight(0, 0, groups)) + tn(
-            gt_ref[hidden:, :], first_weight(1, 0, groups)
-        )
-        first = pl.program_id(0) == 0
-        y_ref[...] = jnp.where(first, added, y_ref[...] + added)
-        sg_ref[...] = jnp.where(first, grown, sg_ref[...] + grown)
-
-    @pl.when(tree == pl.num_programs(1) - 1)
-    def _():
+    mout_ref[0] = mout_in_ref[0] + nt(own_act, br_ref[...])
+    if last:
+        lin_ref, lout_ref = rest[2 * trees + 3 : 2 * trees + 5]
         lin_ref[...] = jnp.zeros_like(lin_ref)
         lout_ref[...] = jnp.zeros_like(lout_ref)
         for a in range(2):
-            lin_ref[0, a, :, :rows] = nt(start_in_ref[a, 0], min_ref[a, 0], HIGHEST)
-        lout_ref[0, :, :out_rows] = nt(start_out_ref[0], mout_ref[0], HIGHEST)
-
-
-def expert_chunk(
-    first_expert, x4, u4, upstream, w1, w2, err_in, err_out, start_in, start_out, merged
-):
+            lin_ref[0, a, :, :rows] = start_product(start_in_ref[a, 0], min_ref[a, 0])
+        lout_ref[0, :, :out_rows] = start_product(start_out_ref[0], mout_ref[0])
+
+
+def whole_block(shape):
+    return pl.BlockSpec(shape, lambda e: (0,) * len(shape), pipeline_mode=pl.Buffered(1))
+
+
+def weight_blocks(w1, w2):
+    last_block = w2.shape[3] - 1
+    return [
+        pl.BlockSpec((*w1.shape[:2], 1, *w1.shape[3:]), lambda e: (0, 0, e, 0, 0)),
+        pl.BlockSpec(
+            (w2.shape[0], 1, w2.shape[2], 1, *w2.shape[4:]), lambda e: (0, e, 0, last_block, 0, 0)
+        ),
+    ]
+
+
+def matrix_blocks(first_expert, shape_in, shape_out):
+    return [
+        pl.BlockSpec(
+            (shape_in[0], 1, *shape_in[2:]), lambda e: (0, first_expert + e, 0, 0)
+        ),
+        pl.BlockSpec((1, *shape_out[1:]), lambda e: (first_expert + e, 0, 0)),
+    ]
+
+
+def own_experts(first_expert, x, u, upstream, weights, err_in, err_out, gate):
+    w1, w2, turned = weights
     count = w2.shape[1]
-    hidden = err_in.shape[3]
-    trees, width, length = u4.shape
-    rows, out_rows = err_in.shape[2], err_out.shape[1]
-    last_block = w2.shape[3] - 1
-    one = pl.Buffered(1)
-
-    def spec(block, index, **more):
-        return pl.BlockSpec(block, index, **more)
-
+    hidden, rows = err_in.shape[3], err_in.shape[2]
+    length, width = upstream.shape
+    matrices = matrix_blocks(first_expert, err_in.shape, err_out.shape)
     in_specs = [
-        spec((1, x4.shape[1], length), lambda e, t: (t, 0, 0)),
-        spec((1, width, length), lambda e, t: (t, 0, 0)),
-        spec((length, width), lambda e, t: (0, 0), pipeline_mode=one),
-        spec((*w1.shape[:2], 1, *w1.shape[3:]), lambda e, t: (0, 0, e, 0, 0)),
-        spec(
-            (w2.shape[0], 1, w2.shape[2], 1, *w2.shape[4:]),
-            lambda e, t: (0, e, 0, last_block, 0, 0),
-        ),
-        spec((2, 1, rows, hidden), lambda e, t: (0, first_expert + e, 0, 0)),
-        spec((1, out_rows, width), lambda e, t: (first_expert + e, 0, 0)),
-        spec((2, 1, 8, hidden), lambda e, t: (0, first_expert + e, 0, 0)),
-        spec((1, 8, width), lambda e, t: (first_expert + e, 0, 0)),
+        whole_block(x.shape),
+        whole_block(u.shape),
+        whole_block(upstream.shape),
+        *weight_blocks(w1, w2),
+        *matrices,
+        pl.BlockSpec(memory_space=pl.ANY),
     ]
-    operands = [x4, u4, upstream, w1, w2, err_in, err_out, start_in, start_out]
-    aliases = {}
-    if merged is not None:
-        in_specs += [pl.BlockSpec(memory_space=pl.ANY)] * 2
-        aliases = {len(operands): 0, len(operands) + 1: 1}
-        operands += list(merged)
-    wide, wide_out = up_to(rows, 128), up_to(out_rows, 128)
-    out_specs = [
-        spec((2, 1, rows, hidden), lambda e, t: (0, first_expert + e, 0, 0)),
-        spec((1, out_rows, width), lambda e, t: (first_expert + e, 0, 0)),
-        spec((length, width), lambda e, t: (0, 0), pipeline_mode=one),
-        spec((length, width), lambda e, t: (0, 0), pipeline_mode=one),
-        spec((1, length, 1), lambda e, t: (e, 0, 0)),
-        spec((1, 2, 8, wide), lambda e, t: (e, 0, 0, 0)),
-        spec((1, 8, wide_out), lambda e, t: (e, 0, 0)),
-    ]
-    out_shape = [
-        struct(err_in.shape),
-        struct(err_out.shape),
-        struct((length, width)),
-        struct((length, width)),
-        struct((count, length, 1)),
-        struct((count, 2, 8, wide)),
-        struct((count, 8, wide_out)),
-    ]
-    flops = 2 * count * hidden * width * length * (3 * trees + 3) + 2 * count * trees * length * (
-        2 * rows * hidden + out_rows * width
-    )
+    operands = [x, u, upstream, w1, w2, err_in, err_out, gate]
+    part_in, part_out = (2, count, rows, hidden), (count, *err_out.shape[1:])
     return pl.pallas_call(
-        functools.partial(expert_kernel, first_expert, merged is not None),
-        grid=(count, trees),
+        functools.partial(own_kernel, first_expert, turned),
+        grid=(count,),
         in_specs=in_specs,
-        out_specs=out_specs,
-        out_shape=out_shape,
+        out_specs=[
+            *matrix_blocks(0, part_in, part_out),
+            whole_block((length, width)),
+            whole_block((length, width)),
+            pl.BlockSpec((1, length, 1), lambda e: (e, 0, 0)),
+        ],
+        out_shape=[
+            struct(part_in),
+            struct(part_out),
+            struct((length, width)),
+            struct((length, width)),
+            struct((count, length, 1)),
+        ],
         scratch_shapes=[
             pltpu.VMEM((2 * hidden, length), BF16),
             pltpu.VMEM((hidden, length), BF16),
             pltpu.VMEM((width, length), BF16),
         ],
-        input_output_aliases=aliases,
         cost_estimate=pl.CostEstimate(
-            flops=flops,
-            bytes_accessed=count * (2 * 3 * hidden * width + 8 * 3 * rows * hidden),
-            transcendentals=count * trees * length * hidden,
+            flops=28 * count * hidden * width * length,
+            bytes_accessed=count * (6 * hidden * width + 24 * rows * hidden) + 12 * length * width,
+            transcendentals=0,
         ),
         compiler_params=params(),
-        name="experts",
+        name="own_experts",
+    )(*operands)
+
+
+def rest_experts(first_expert, last, xs, us, weights, start_in, start_out, merged_in, merged_out, gate):
+    w1, w2, turned = weights
+    count, trees = w2.shape[1], len(xs)
+    hidden, rows = merged_in.shape[3], merged_in.shape[2]
+    out_rows = merged_out.shape[1]
+    width, length = merged_out.shape[2], xs[0].shape[1]
+    matrices = matrix_blocks(0, merged_in.shape, merged_out.shape)
+    wide, wide_out = up_to(rows, 128), up_to(out_rows, 128)
+    out_specs = list(matrices)
+    out_shape = [struct(merged_in.shape), struct(merged_out.shape)]
+    if last:
+        out_specs += [
+            pl.BlockSpec((1, 2, 8, wide), lambda e: (e, 0, 0, 0)),
+            pl.BlockSpec((1, 8, wide_out), lambda e: (e, 0, 0)),
+        ]
+        out_shape += [struct((count, 2, 8, wide)), struct((count, 8, wide_out))]
+    return pl.pallas_call(
+        functools.partial(rest_kernel, first_expert, trees, last, turned),
+        grid=(count,),
+        in_specs=[
+            *weight_blocks(w1, w2),
+            *matrix_blocks(first_expert, start_in.shape, start_out.shape),
+            *matrices,
+            *[whole_block(x.shape) for x in (*xs, *us)],
+            pl.BlockSpec(memory_space=pl.ANY),
+        ],
+        out_specs=out_specs,
+        out_shape=out_shape,
+        scratch_shapes=[
+            pltpu.VMEM((2 * hidden, trees * length), BF16),
+            pltpu.VMEM((hidden, trees * length), BF16),
+            pltpu.VMEM((width, trees * length), BF16),
+        ],
+        input_output_aliases={4: 0, 5: 1},
+        cost_estimate=pl.CostEstimate(
+            flops=14 * count * trees * hidden * width * length,
+            bytes_accessed=count * (6 * hidden * width + 24 * rows * hidden),
+            transcendentals=0,
+        ),
+        compiler_params=params(),
+        name="rest_experts",
+    )(w1, w2, start_in, start_out, merged_in, merged_out, *xs, *us, gate)
+
+
+def open_kernel(reps, shards, pieces, extra, *refs):
+    count = len(pieces)
+    sources, targets = refs[: count + 1 + extra], refs[count + 1 + extra : 2 * (count + 1 + extra)]
+    local_sem, up_send, up_recv, down_send, down_recv, chip_send, chip_recv, core_send, core_recv = refs[
+        2 * (count + 1 + extra) :
+    ]
+    rep, shard = lax.axis_index("rep"), lax.axis_index("shard")
+    chips, core = reps // 2, rep % 2
+    chip = rep // 2
+    total = count + 1 + extra
+
+    def slot(k, which):
+        if k > count:
+            return targets[k].at[which]
+        span = sources[k].shape[1]
+        lanes = pl.ds(pl.multiple_of(which * span, span), span)
+        height = sources[k].shape[0]
+        if k == count:
+            return targets[k].at[:, lanes]
+        row = pieces[k] + rep * height
+        return targets[k].at[pl.ds(pl.multiple_of(row, 16), height), lanes]
+
+    def band(k, which):
+        height = sources[k].shape[0]
+        row = pieces[k] + which * height
+        return targets[k].at[pl.ds(pl.multiple_of(row, 16), height), :]
+
+    barrier = pltpu.get_barrier_semaphore()
+    for step in range(1, shards):
+        pl.semaphore_signal(
+            barrier, inc=1, device_id={"shard": lax.rem(shard + step, shards)}, device_id_type=MESH
+        )
+    for step in range(1, chips):
+        to = lax.rem(chip + step, chips) * 2 + core
+        pl.semaphore_signal(barrier, inc=1, device_id={"rep": to}, device_id_type=MESH)
+    pl.semaphore_signal(barrier, inc=1, device_id={"rep": rep + 1 - 2 * core}, device_id_type=MESH)
+    pl.semaphore_wait(barrier, shards - 1 + chips)
+
+    locals_ = []
+    for k in range(total):
+        copy = pltpu.make_async_copy(sources[k], slot(k, shard), local_sem.at[k])
+        copy.start()
+        locals_.append(copy)
+
+    def up_copy(k, step):
+        source = sources[k] if step == 0 else slot(k, shard - step)
+        return pltpu.make_async_remote_copy(
+            src_ref=source,
+            dst_ref=slot(k, shard - step),
+            send_sem=up_send.at[k, step],
+            recv_sem=up_recv.at[k, step],
+            device_id={"shard": lax.rem(shard + 1, shards)},
+            device_id_type=MESH,
+        )
+
+    def down_copy(k, step):
+        source = sources[k] if step == 0 else slot(k, shard + step)
+        return pltpu.make_async_remote_copy(
+            src_ref=source,
+            dst_ref=slot(k, shard + step),
+            send_sem=down_send.at[k, step],
+            recv_sem=down_recv.at[k, step],
+            device_id={"shard": lax.rem(shard + shards - 1, shards)},
+            device_id_type=MESH,
+        )
+
+    def line_step(group, step):
+        @pl.when((shard < shards - 1) & (step <= shard))
+        def _():
+            for k in group:
+                up_copy(k, step).start()
+
+        @pl.when((shard > 0) & (step <= shards - 1 - shard))
+        def _():
+            for k in group:
+                down_copy(k, step).start()
+
+    def line_arrive(group, step):
+        @pl.when(step <= shard - 1)
+        def _():
+            for k in group:
+                pltpu.make_async_remote_copy(
+                    src_ref=slot(k, shard - 1 - step),
+                    dst_ref=slot(k, shard - 1 - step),
+                    send_sem=up_send.at[k, step],
+                    recv_sem=up_recv.at[k, step],
+                    device_id={"shard": lax.rem(shard + 1, shards)},
+                    device_id_type=MESH,
+                ).wait_recv()
+
+        @pl.when(step <= shards - 2 - shard)
+        def _():
+            for k in group:
+                pltpu.make_async_remote_copy(
+                    src_ref=slot(k, shard + 1 + step),
+                    dst_ref=slot(k, shard + 1 + step),
+                    send_sem=down_send.at[k, step],
+                    recv_sem=down_recv.at[k, step],
+                    device_id={"shard": lax.rem(shard + 1, shards)},
+                    device_id_type=MESH,
+                ).wait_recv()
+
+    def line_sent(group, step):
+        @pl.when((shard < shards - 1) & (step <= shard))
+        def _():
+            for k in group:
+                up_copy(k, step).wait_send()
+
+        @pl.when((shard > 0) & (step <= shards - 1 - shard))
+        def _():
+            for k in group:
+                down_copy(k, step).wait_send()
+
+    first = list(range(count + 1))
+    later = list(range(count + 1, total))
+    for step in range(shards - 1):
+        line_step(first, step)
+        line_arrive(first, step)
+    line_step(later, 0)
+    for copy in locals_:
+        copy.wait()
+
+    def chip_copy(k, step):
+        to = lax.rem(chip + step, chips) * 2 + core
+        return pltpu.make_async_remote_copy(
+            src_ref=band(k, rep),
+            dst_ref=band(k, rep),
+            send_sem=chip_send.at[k, step - 1],
+            recv_sem=chip_recv.at[k, step - 1],
+            device_id={"rep": to},
+            device_id_type=MESH,
+        )
+
+    def core_copy(k, step):
+        owner = lax.rem(chip + chips - step, chips) * 2 + core
+        return pltpu.make_async_remote_copy(
+            src_ref=band(k, owner),
+            dst_ref=band(k, owner),
+            send_sem=core_send.at[k, step],
+            recv_sem=core_recv.at[k, step],
+            device_id={"rep": rep + 1 - 2 * core},
+            device_id_type=MESH,
+        )
+
+    for step in range(1, chips):
+        for k in range(count):
+            chip_copy(k, step).start()
+    for k in range(count):
+        core_copy(k, 0).start()
+    for step in range(1, shards - 1):
+        line_arrive(later, step - 1)
+        line_step(later, step)
+    for step in range(1, chips):
+        for k in range(count):
+            chip_copy(k, step).wait_recv()
+            core_copy(k, step).start()
+    if shards > 1:
+        line_arrive(later, shards - 2)
+    for step in range(chips):
+        for k in range(count):
+            core_copy(k, step).wait()
+            if step:
+                chip_copy(k, step).wait_send()
+    for step in range(shards - 1):
+        line_sent(first + later, step)
+
+
+def open_gather(reps, shards, bands, small, lines):
+    operands = [operand for _, operand in bands] + [small] + list(lines)
+    dma = pltpu.SemaphoreType.DMA
+    count, total, chips = len(bands), len(operands), reps // 2
+    span = small.shape[1]
+    shapes = [struct((reps * operand.shape[0], shards * span), BF16) for _, operand in bands]
+    shapes.append(struct((small.shape[0], shards * span), BF16))
+    shapes += [struct((shards, *line.shape), BF16) for line in lines]
+    anywhere = pl.BlockSpec(memory_space=pl.ANY)
+    return pl.pallas_call(
+        functools.partial(open_kernel, reps, shards, [at for at, _ in bands], len(lines)),
+        in_specs=[anywhere] * total,
+        out_specs=[anywhere] * total,
+        out_shape=shapes,
+        scratch_shapes=[
+            dma((total,)),
+            dma((total, shards - 1)),
+            dma((total, shards - 1)),
+            dma((total, shards - 1)),
+            dma((total, shards - 1)),
+            dma((count, chips)),
+            dma((count, chips)),
+            dma((count, chips)),
+            dma((count, chips)),
+        ],
+        compiler_params=params(collective_id=4, has_side_effects=True),
+        name="open_gather",
     )(*operands)
 
 
@@ -392,10 +744,10 @@
                 piece[:, shard * rows : (shard + 1) * rows], wide
             )
     errors = (
-        nt(sq_ref[...], eq_ref[...], HIGHEST),
-        nt(sk_ref[...], ep_ref[0], HIGHEST),
-        nt(sv_ref[...], ep_ref[1], HIGHEST),
-        nt(so_ref[...], eo_ref[...], HIGHEST),
+        start_product(sq_ref[...], eq_ref[...]),
+        start_product(sk_ref[...], ep_ref[0]),
+        start_product(sv_ref[...], ep_ref[1]),
+        start_product(so_ref[...], eo_ref[...]),
     )
     for k, piece in enumerate(errors):
         own_ref[:, k * wide : (k + 1) * wide] = padded(piece, wide)
@@ -427,7 +779,7 @@
     pl.semaphore_wait(barrier, reps + shards - 2)
 
 
-def send_all(axis, size, source, target, send, recv):
+def start_all(axis, size, source, target, send, recv):
     here = lax.axis_index(axis)
     copies = []
     for step in range(1, size):
@@ -442,7 +794,11 @@
         )
         copy.start()
         copies.append(copy)
-    for copy in copies:
+    return copies
+
+
+def send_all(axis, size, source, target, send, recv):
+    for copy in start_all(axis, size, source, target, send, recv):
         copy.wait()
 
 
@@ -513,7 +869,13 @@
     more = jnp.where(lane == 0, jnp.sum(router * router, axis=1, keepdims=True), 0.0)
     more = jnp.where(lane == 1, jnp.sum(gains * gains, axis=1, keepdims=True), more)
     grams[shard] = jnp.concatenate([gram, gram_out, more], axis=1)
-    send_all("shard", shards, lambda to: grams.at[shard], lambda step: grams.at[shard], hs, hr)
+    lanes_z[shard] = stack[:32]
+    sent = start_all("shard", shards, lambda to: grams.at[shard], lambda step: grams.at[shard], hs, hr)
+    sent += start_all(
+        "shard", shards, lambda to: lanes_z.at[shard], lambda step: lanes_z.at[shard], ls, lr
+    )
+    for copy in sent:
+        copy.wait()
     gram = grams[0]
     for k in range(1, shards):
         gram = gram + grams[k]
@@ -542,13 +904,13 @@
             inverse[i] = inverse[i] - factor * inverse[k]
         inverse[k] = inverse[k] / jnp.sqrt(pivot)
     flat = exact_nt(jnp.concatenate(inverse, axis=1), chosen)
-    lefts = nn(spread_on_diagonal(flat[:, :size]), stack, HIGHEST)
+    solve = spread_on_diagonal(flat[:, :size])
+    lefts = nn(solve, stack, HIGHEST)
     lefts_out = nn(spread_on_diagonal(flat[:, size:]), stack_out, HIGHEST)
     left_ref[...] = lefts[: left_ref.shape[0]]
     left_out_ref[...] = lefts_out[: left_out_ref.shape[0]]
-    lanes_z[shard] = lefts[:32]
-    send_all("shard", shards, lambda to: lanes_z.at[shard], lambda step: lanes_z.at[shard], ls, lr)
-    leftz_ref[...] = lanes_z[...]
+    for k in range(shards):
+        leftz_ref[k] = nn(solve[:32, :32], lanes_z[k], HIGHEST)
 
 
 def left_sync(reps, shards, z_part, own, lins, louts):
@@ -593,25 +955,26 @@
     )(*operands)
 
 
+def left_product(left, matrix):
+    high, low = two_terms(left)
+    both = jnp.concatenate([high.astype(F32), low.astype(F32)], axis=0).astype(BF16)
+    top, rest = two_terms(matrix)
+    first = nn(both, top)
+    return first[:8] + first[8:] + nn(both, rest)[:8]
+
+
 def right_expert_kernel(left_ref, left_out_ref, min_ref, mout_ref, right_ref):
     rows, out_rows = min_ref.shape[2], mout_ref.shape[1]
     hidden = min_ref.shape[3]
 
-    def product(left, matrix):
-        high, low = two_terms(left)
-        both = jnp.concatenate([high.astype(F32), low.astype(F32)], axis=0).astype(BF16)
-        top, rest = two_terms(matrix)
-        first = nn(both, top)
-        return first[:8] + first[8:] + nn(both, rest)[:8]
-
     for a in range(2):
-        right_ref[0, :, a * hidden : (a + 1) * hidden] = product(
+        right_ref[0, :, a * hidden : (a + 1) * hidden] = left_product(
             left_ref[a, 0, :, :rows], min_ref[a, 0]
         )
-    right_ref[0, :, 2 * hidden :] = product(left_out_ref[0, :, :out_rows], mout_ref[0])
-
-
-def right_experts(lefts, lefts_out, merged_in, merged_out):
+    right_ref[0, :, 2 * hidden :] = left_product(left_out_ref[0, :, :out_rows], mout_ref[0])
+
+
+def right_experts(first_expert, lefts, lefts_out, merged_in, merged_out):
     count, rows, hidden = merged_in.shape[1:]
     out_rows, width = merged_out.shape[1:]
     wide, wide_out = lefts.shape[3], lefts_out.shape[2]
@@ -619,8 +982,8 @@
         right_expert_kernel,
         grid=(count,),
         in_specs=[
-            pl.BlockSpec((2, 1, 8, wide), lambda e: (0, e, 0, 0)),
-            pl.BlockSpec((1, 8, wide_out), lambda e: (e, 0, 0)),
+            pl.BlockSpec((2, 1, 8, wide), lambda e: (0, first_expert + e, 0, 0)),
+            pl.BlockSpec((1, 8, wide_out), lambda e: (first_expert + e, 0, 0)),
             pl.BlockSpec((2, 1, rows, hidden), lambda e: (0, e, 0, 0)),
             pl.BlockSpec((1, out_rows, width), lambda e: (e, 0, 0)),
         ],
@@ -650,10 +1013,10 @@
     at = 0
     for k, error in ((0, eq_ref[...]), (1, ep_ref[0]), (2, ep_ref[1])):
         grown = exact_nn(exact_nt(whole(k), first), joint_ref[:, at : at + error.shape[1]])
-        right_ref[:, at : at + error.shape[1]] = grown + nn(own(k), error, HIGHEST)
+        right_ref[:, at : at + error.shape[1]] = grown + left_product(own(k), error)
         at += error.shape[1]
     grown = exact_nn(exact_nt(whole(3), mixed_ref[...]), middle_ref[...])
-    right_ref[:, at : at + width] = grown + nn(own(3), eo_ref[...], HIGHEST)
+    right_ref[:, at : at + width] = grown + left_product(own(3), eo_ref[...])
 
 
 def right_attention(shards, rows, operands):
@@ -668,15 +1031,14 @@
     )(*operands)
 
 
-def right_sync_kernel(
-    reps, shards, piece, experts_ref, attention_ref, out_ref, parts, heard, across, total, ps, pr,
-    zs, zr, gs, gr,
-):
+def right_sync_kernel(reps, shards, piece, count, *refs):
+    experts_refs, attention_ref, out_ref = refs[:count], refs[count], refs[count + 1]
+    parts, heard, across, total, ps, pr, zs, zr, gs, gr = refs[count + 2 :]
     rep, shard = lax.axis_index("rep"), lax.axis_index("shard")
     half = piece // 2
     greet(reps, shards)
     line = jnp.concatenate(
-        [experts_ref[e] for e in range(experts_ref.shape[0])] + [attention_ref[...]], axis=1
+        [ref[e] for ref in experts_refs for e in range(ref.shape[0])] + [attention_ref[...]], axis=1
     )
     line = padded(line, reps * piece)
     for k in range(reps):
@@ -702,12 +1064,12 @@
 
 
 def right_sync(reps, shards, experts, attention):
-    columns = experts.shape[0] * experts.shape[2] + attention.shape[1]
+    columns = sum(part.shape[0] * part.shape[2] for part in experts) + attention.shape[1]
     piece = up_to(-(-columns // reps), 256)
     dma = pltpu.SemaphoreType.DMA
     return pl.pallas_call(
-        functools.partial(right_sync_kernel, reps, shards, piece),
-        in_specs=vmem_specs(2),
+        functools.partial(right_sync_kernel, reps, shards, piece, len(experts)),
+        in_specs=vmem_specs(len(experts) + 1),
         out_specs=pl.BlockSpec(memory_space=pltpu.VMEM),
         out_shape=struct((8, reps * piece)),
         scratch_shapes=[
@@ -724,7 +1086,7 @@
         ],
         compiler_params=params(collective_id=2, has_side_effects=True),
         name="right_sync",
-    )(experts, attention)
+    )(*experts, attention)
 
 
 def low_rank(left, right):
@@ -735,15 +1097,15 @@
 
 
 def feedback_expert_kernel(
-    replicas, left_ref, left_out_ref, right_ref, min_ref, mout_ref, fin_ref, fout_ref, sq_ref
+    replicas, first_expert, left_ref, left_out_ref, right_ref, min_ref, mout_ref, *rest
 ):
-    expert = pl.program_id(0)
+    fin_ref, fout_ref, sq_ref = rest[-3:]
     rows, hidden = min_ref.shape[2:]
     out_rows = mout_ref.shape[1]
     row = lax.broadcasted_iota(jnp.int32, (8, 128), 0)
     lane = lax.broadcasted_iota(jnp.int32, (8, 128), 1)
 
-    @pl.when(expert == 0)
+    @pl.when(pl.program_id(0) == 0)
     def _():
         sq_ref[...] = jnp.zeros_like(sq_ref)
 
@@ -759,30 +1121,41 @@
     left_over = mout_ref[0] - approx * (1.0 / replicas)
     fout_ref[0] = left_over
     added = jnp.where(lane == 2, jnp.sum(left_over * left_over), added)
-    sq_ref[...] += jnp.where(row == expert, added, 0.0)
-
-
-def feedback_experts(replicas, lefts, lefts_out, rights, merged_in, merged_out):
+    sq_ref[...] += jnp.where(row == first_expert + pl.program_id(0), added, 0.0)
+
+
+def feedback_experts(
+    replicas, first_expert, lefts, lefts_out, rights, merged_in, merged_out, whole_in, whole_out
+):
     count, rows, hidden = merged_in.shape[1:]
     out_rows, width = merged_out.shape[1:]
     wide, wide_out = lefts.shape[3], lefts_out.shape[2]
-    in_block = pl.BlockSpec((2, 1, rows, hidden), lambda e: (0, e, 0, 0))
-    out_block = pl.BlockSpec((1, out_rows, width), lambda e: (e, 0, 0))
+    shapes = (2, E, rows, hidden), (E, out_rows, width)
+    operands = [lefts, lefts_out, rights, merged_in, merged_out]
+    in_specs = [
+        pl.BlockSpec((2, 1, 8, wide), lambda e: (0, first_expert + e, 0, 0)),
+        pl.BlockSpec((1, 8, wide_out), lambda e: (first_expert + e, 0, 0)),
+        pl.BlockSpec((8, 2 * hidden + width), lambda e: (0, first_expert + e)),
+        *matrix_blocks(0, merged_in.shape, merged_out.shape),
+    ]
+    aliases = {}
+    if whole_in is not None:
+        operands += [whole_in, whole_out]
+        in_specs += [pl.BlockSpec(memory_space=pl.ANY)] * 2
+        aliases = {5: 0, 6: 1}
     return pl.pallas_call(
-        functools.partial(feedback_expert_kernel, replicas),
+        functools.partial(feedback_expert_kernel, replicas, first_expert),
         grid=(count,),
-        in_specs=[
-            pl.BlockSpec((2, 1, 8, wide), lambda e: (0, e, 0, 0)),
-            pl.BlockSpec((1, 8, wide_out), lambda e: (e, 0, 0)),
-            pl.BlockSpec((8, 2 * hidden + width), lambda e: (0, e)),
-            in_block,
-            out_block,
+        in_specs=in_specs,
+        out_specs=[
+            *matrix_blocks(first_expert, *shapes),
+            pl.BlockSpec((8, 128), lambda e: (0, 0)),
         ],
-        out_specs=[in_block, out_block, pl.BlockSpec((8, 128), lambda e: (0, 0))],
-        out_shape=[struct(merged_in.shape), struct(merged_out.shape), struct((8, 128))],
+        out_shape=[struct(shapes[0]), struct(shapes[1]), struct((8, 128))],
+        input_output_aliases=aliases,
         compiler_params=params(),
         name="feedback_experts",
-    )(lefts, lefts_out, rights, merged_in, merged_out)
+    )(*operands)
 
 
 def feedback_attention_kernel(
@@ -823,10 +1196,14 @@
     )(*operands)
 
 
-def squares_sync_kernel(reps, shards, a_ref, b_ref, out_ref, plane, line, ps, pr, zs, zr):
+def squares_sync_kernel(reps, shards, count, *refs):
+    out_ref, plane, line, ps, pr, zs, zr = refs[count:]
     rep, shard = lax.axis_index("rep"), lax.axis_index("shard")
     greet(reps, shards)
-    plane[rep] = a_ref[...] + b_ref[...]
+    added = refs[0][...]
+    for ref in refs[1:count]:
+        added = added + ref[...]
+    plane[rep] = added
     send_all("rep", reps, lambda to: plane.at[rep], lambda step: plane.at[rep], ps, pr)
     summed = plane[0]
     for k in range(1, reps):
@@ -839,11 +1216,11 @@
     out_ref[...] = summed
 
 
-def squares_sync(reps, shards, first, second):
+def squares_sync(reps, shards, parts):
     dma = pltpu.SemaphoreType.DMA
     return pl.pallas_call(
-        functools.partial(squares_sync_kernel, reps, shards),
-        in_specs=vmem_specs(2),
+        functools.partial(squares_sync_kernel, reps, shards, len(parts)),
+        in_specs=vmem_specs(len(parts)),
         out_specs=pl.BlockSpec(memory_space=pltpu.VMEM),
         out_shape=struct((8, 128)),
         scratch_shapes=[
@@ -856,7 +1233,7 @@
         ],
         compiler_params=params(collective_id=3, has_side_effects=True),
         name="squares_sync",
-    )(first, second)
+    )(*parts)
 
 
 def per_device(
@@ -908,15 +1285,11 @@
     f_rows = outer_low.shape[1]
     small = jnp.concatenate([router_t, gains_low], axis=0)
     small = jnp.pad(small, ((0, 16 - small.shape[0]), (0, 0)))
-    packed = jnp.concatenate(
-        [query_t, pair_t.reshape(2 * p_cols, own_rows), output_t, small], axis=0
-    )
-    spread = lax.all_gather(packed, both).reshape(replicas, shard_count, packed.shape[0], own_rows)
-
     per_chunk = E // CHUNKS
     outer_cols = outer_low.shape[2]
     paired = replicas % 2 == 0 and per_chunk == 2 and own_rows == 2 * outer_cols == 2 * f_rows
-    paired = paired and 2 * f_cols == f_rows and f_cols % 16 == 0 and own_rows % 128 == 0
+    paired = paired and 2 * f_cols == f_rows and own_rows % 128 == 0
+    paired = paired and q_cols % 16 == 0 and p_cols % 16 == 0 and f_cols % 16 == 0
 
     def whole_weights(inner_all, outer_all):
         inner_all = inner_all.reshape(replicas, shard_count, per_chunk, 2, f_cols, own_rows)
@@ -926,8 +1299,10 @@
         w2 = jnp.transpose(outer_all, (2, 1, 3, 0, 4)).reshape(
             1, per_chunk, 1, 1, shard_count * f_rows, replicas * outer_cols
         )
-        return w1, w2
-
+        return w1, w2, False
+
+    cot_t = jnp.transpose(cotangent)
+    chunk_weights = []
     if paired:
         core = lax.axis_index("rep") % 2
         outer_pairs = outer_low.reshape(CHUNKS, 2, f_rows, outer_cols)
@@ -937,25 +1312,38 @@
         wide_outer = jnp.concatenate(
             [jnp.where(core == 0, keep, got), jnp.where(core == 0, got, keep)], axis=2
         )
-        packs = jnp.concatenate(
-            [inner_t.reshape(CHUNKS, per_chunk * 2 * f_cols, own_rows), wide_outer], axis=1
-        )
-        height = packs.shape[1]
-        split = CHUNKS // 2
-        early = z_gather(packs[:split].reshape(split * height, own_rows))
-        held, spread = lax.optimization_barrier((packs[split:], spread))
-        late = z_gather(held.reshape((CHUNKS - split) * height, own_rows))
-        chunk_weights = []
-        for index in range(CHUNKS):
-            source = early if index < split else late
-            at = (index % split) * height
-            part = lax.all_gather(source[:, at : at + height], "rep")
-            w1 = part.reshape(replicas, shard_count, 3, f_rows, own_rows)
-            w2 = part.reshape(replicas // 2, 2, shard_count, 3, f_rows, own_rows)
-            chunk_weights.append((w1, w2))
-        _, cot_t = lax.optimization_barrier((late, jnp.transpose(cotangent)))
+        inner_packs = inner_t.reshape(CHUNKS, per_chunk * 2 * f_cols, own_rows)
+        packs = [
+            jnp.concatenate([inner_packs[k], wide_outer[k]], axis=0) for k in range(CHUNKS)
+        ]
+        opened = open_gather(
+            replicas,
+            shard_count,
+            [(0, query_t), (0, pair_t[0]), (0, pair_t[1]), (0, output_t)],
+            small,
+            packs[:1],
+        )
+        query_full, key_full, value_full, output_full, small_full = opened[:5]
+        height = packs[0].shape[0]
+        near = z_slots(packs[1])
+        first_line = opened[5]
     else:
-        chunk_weights = []
+        packed = jnp.concatenate(
+            [query_t, pair_t.reshape(2 * p_cols, own_rows), output_t, small], axis=0
+        )
+        spread = lax.all_gather(packed, both).reshape(
+            replicas, shard_count, packed.shape[0], own_rows
+        )
+
+        def joined(low, high):
+            piece = jnp.transpose(spread[:, :, low:high], (0, 2, 1, 3))
+            return piece.reshape(-1, shard_count * own_rows)
+
+        at = q_cols + 2 * p_cols
+        query_full = joined(0, q_cols)
+        key_full, value_full = joined(q_cols, q_cols + p_cols), joined(q_cols + p_cols, at)
+        output_full = joined(at, at + q_cols)
+        small_full = joined(at + q_cols, packed.shape[0])[: small.shape[0]]
         for index in range(CHUNKS):
             span = slice(index * per_chunk, (index + 1) * per_chunk)
             chunk_weights.append(
@@ -966,49 +1354,24 @@
                     ),
                 )
             )
-        cot_t = jnp.transpose(cotangent)
-
-    def joined(piece):
-        return jnp.transpose(piece, (0, 2, 1, 3)).reshape(-1, shard_count * own_rows)
-
-    query_full = joined(spread[:, :, :q_cols])
-    pair_full = jnp.stack(
-        [
-            joined(spread[:, :, q_cols + a * p_cols : q_cols + (a + 1) * p_cols])
-            for a in range(2)
-        ]
-    )
-    at = q_cols + 2 * p_cols
-    output_full = joined(spread[:, :, at : at + q_cols])
-    at += q_cols
-    router_full = joined(spread[:1, :, at : at + E])
-    gain_values = joined(spread[:1, :, at + E : at + E + 2]).astype(jnp.float32)
-
-    upstream_slots = z_slots(cot_t)
+    router_full = small_full[:E]
+    gain_values = small_full[E : E + 2].astype(jnp.float32)
 
     hidden = tokens.astype(jnp.float32)
     length = hidden.shape[0]
     position = positions[0]
     allowed = path_mask(seg_ids[0], parents[0])
     first_low = rms_norm(hidden, gain_values[0]).astype(bf16)
-    query_pre = jnp.einsum("td,qd->tq", first_low, query_full, preferred_element_type=jnp.float32)
-    pair_pre = jnp.einsum("td,awd->atw", first_low, pair_full, preferred_element_type=jnp.float32)
-    query_rot = rotate(query_pre.reshape(length, HQ, HD), position, 1.0).astype(bf16)
-    key_rot = rotate(pair_pre[0].reshape(length, HK, HD), position, 1.0).astype(bf16)
-    values = pair_pre[1].reshape(length, HK, HD).astype(bf16)
-    block_rows = min(512, length)
-    masked, shaped = scores_of(query_rot, key_rot, allowed)
-    top_score = jnp.max(masked, axis=-1, keepdims=True)
-    raised = jnp.exp(masked - top_score)
-    total_sum = jnp.sum(raised, axis=-1, keepdims=True)
-    attention = (raised / total_sum).astype(bf16)
-    lse_parts = top_score + jnp.log(total_sum)
-    mixed_block = jnp.einsum(
-        "kgqt,tkd->qkgd", attention, values, preferred_element_type=jnp.float32
-    )
-    mixed_low = mixed_block.reshape(block_rows, HQ * HD).astype(bf16)
-    middle = hidden + jnp.einsum(
-        "tq,dq->td", mixed_low, output_full, preferred_element_type=jnp.float32
+    half_head = HD // 2
+    frequency = ROPE_BASE ** (-2.0 * jnp.arange(half_head, dtype=jnp.float32) / HD)
+    angles = position.astype(jnp.float32)[:, None] * frequency[None, :]
+    cosine = jnp.concatenate([jnp.cos(angles), jnp.cos(angles)], axis=1)
+    sine = jnp.concatenate([-jnp.sin(angles), jnp.sin(angles)], axis=1)
+    mask = allowed.astype(bf16)
+    query_rot, key_rot, values, mixed_low, middle = attention_forward(
+        (
+            first_low, query_full, key_full, value_full, output_full, tokens, cosine, sine, mask,
+        )
     )
     second_low = rms_norm(middle, gain_values[1]).astype(bf16)
     logits = jnp.einsum("td,ed->te", second_low, router_full, preferred_element_type=jnp.float32)
@@ -1020,38 +1383,148 @@
     shares_t = jnp.transpose(shares)
     shares_high = shares_t.astype(bf16)
     shares_rest = (shares_t - shares_high.astype(jnp.float32)).astype(bf16)
-    second_slots = z_slots(
-        jnp.concatenate([jnp.transpose(second_low), shares_high, shares_rest], axis=0)
-    )
+    tree_x = jnp.concatenate([jnp.transpose(second_low), shares_high, shares_rest], axis=0)
+
+    token = tree_x[:16, :128]
+    far = None
+
+    def gathered(line, turned):
+        part = lax.all_gather(line, "rep")
+        w1 = part.reshape(replicas, shard_count, 3, f_rows, own_rows)
+        w2 = part.reshape(replicas // 2, 2, shard_count, 3, f_rows, own_rows)
+        chunk_weights.append((w1, w2, turned))
+
+    if paired:
+        near, held, token = lax.optimization_barrier(
+            (near, jnp.concatenate(packs[2:], axis=0), token)
+        )
+        far = z_slots(held)
+        gathered(first_line, False)
+        gathered(jnp.stack(near), True)
 
     upstream = cotangent.astype(jnp.float32)
     start_in = jnp.swapaxes(inner_start, 2, 3)
     start_out = jnp.swapaxes(outer_start, 1, 2)
-    merged_experts = None
-    combined = middle
-    second_grad = None
-    combine_parts, lins, louts = [], [], []
-    for index in range(CHUNKS):
-        w1, w2 = chunk_weights[index]
-        done = expert_chunk(
+    chunks = range(CHUNKS)
+    merged_parts, lins, louts = [None] * CHUNKS, [None] * CHUNKS, [None] * CHUNKS
+    y_parts, grad_parts, combine_parts = [None] * CHUNKS, [None] * CHUNKS, [None] * CHUNKS
+    slots_x, slots_u = {}, {}
+    state = {"gate": token, "x": tree_x, "u": cot_t}
+
+    def exchange(step, held_x, held_u):
+        ring = [(i, (i + step) % shard_count) for i in range(shard_count)]
+        slots_x[step] = lax.ppermute(held_x, "shard", ring)
+        slots_u[step] = lax.ppermute(held_u, "shard", ring)
+
+    def own(index):
+        done = own_experts(
             index * per_chunk,
-            second_slots,
-            upstream_slots,
+            state["x"],
+            state["u"],
             cotangent,
-            w1,
-            w2,
+            chunk_weights[index],
             inner_error[0],
             outer_error[0],
+            state["gate"],
+        )
+        merged_parts[index] = (done[0], done[1])
+        y_parts[index], grad_parts[index] = done[2], done[3]
+        combine_parts[index] = done[4][:, :, 0]
+        state["gate"] = done[0][0, 0, :16, :128].astype(bf16)
+
+    def others(index, steps, last):
+        done = rest_experts(
+            index * per_chunk,
+            last,
+            [slots_x[step] for step in steps],
+            [slots_u[step] for step in steps],
+            chunk_weights[index],
             start_in,
             start_out,
-            merged_experts,
-        )
-        merged_experts = (done[0], done[1])
-        combined = combined + done[2]
-        second_grad = done[3] if second_grad is None else second_grad + done[3]
-        combine_parts.append(done[4][:, :, 0])
-        lins.append(done[5])
-        louts.append(done[6])
+            *merged_parts[index],
+            state["gate"],
+        )
+        merged_parts[index] = (done[0], done[1])
+        if last:
+            lins[index], louts[index] = done[2], done[3]
+        state["gate"] = done[0][0, 0, :16, :128].astype(bf16)
+
+    def all_others(index, steps):
+        groups = [steps[at : at + 3] for at in range(0, len(steps), 3)]
+        for group in groups:
+            others(index, group, group is groups[-1])
+
+    steps = list(range(1, shard_count))
+    filled = shard_count == 4 and CHUNKS == 4
+    def far_weights():
+        lines, state["gate"] = lax.optimization_barrier((far, state["gate"]))
+        lines = jnp.stack(lines)
+        for k in range(CHUNKS - 2):
+            gathered(lines[:, k * height : (k + 1) * height], True)
+
+    def pass_on(ups, downs):
+        forth = [(i, i + 1) for i in range(shard_count - 1)]
+        back = [(i + 1, i) for i in range(shard_count - 1)]
+        return (
+            tuple(lax.ppermute(up, "shard", forth) for up in ups),
+            tuple(lax.ppermute(down, "shard", back) for down in downs),
+        )
+
+    def not_before(pair):
+        pair, state["gate"] = lax.optimization_barrier((pair, state["gate"]))
+        return pair
+
+    late = token
+    if filled and paired:
+        own(0)
+        state["x"], state["u"] = held = not_before((state["x"], state["u"]))
+        ups, downs = [held], [held]
+        up, down = pass_on(held, held)
+        ups.append(up)
+        downs.append(down)
+        far_weights()
+        own(1)
+        ups[1], downs[1] = not_before((ups[1], downs[1]))
+        up, down = pass_on(ups[1], downs[1])
+        ups.append(up)
+        downs.append(down)
+        slots_x[1], slots_u[1] = (jnp.where(here >= 1, ups[1][k], downs[1][k]) for k in range(2))
+        others(0, [1], False)
+        own(2)
+        others(1, [1], False)
+        ups[2], downs[2] = not_before((ups[2], downs[2]))
+        up, down = pass_on(ups[2], downs[2])
+        ups.append(up)
+        downs.append(down)
+        others(2, [1], False)
+        own(3)
+        slots_x[2], slots_u[2] = (
+            jnp.where(here == 0, downs[2][k], jnp.where(here == 3, ups[2][k], downs[1][k]))
+            for k in range(2)
+        )
+        slots_x[3], slots_u[3] = (
+            jnp.where(
+                here == 0,
+                downs[3][k],
+                jnp.where(here == 1, downs[2][k], jnp.where(here == 2, ups[2][k], ups[3][k])),
+            )
+            for k in range(2)
+        )
+        for array in (*ups[3], *downs[3]):
+            late = late + array[:16, :128]
+    else:
+        if paired:
+            far_weights()
+        for step in steps:
+            exchange(step, tree_x, cot_t)
+        for index in chunks:
+            own(index)
+    combined = middle
+    second_grad = grad_parts[0]
+    for index in chunks:
+        combined = combined + y_parts[index]
+        if index:
+            second_grad = second_grad + grad_parts[index]
     output = combined.astype(bf16)
     combine_grad = jnp.transpose(jnp.concatenate(combine_parts, axis=0))
     logit_low = (
@@ -1069,45 +1542,32 @@
     group_output = lax.psum_scatter(
         grad_output.astype(bf16), "shard", scatter_dimension=0, tiled=True
     )
-    mixed_grad = jnp.einsum(
-        "td,dq->tq", middle_low, output_full, preferred_element_type=jnp.float32
-    ).astype(bf16)
-    masked, shaped = scores_of(query_rot, key_rot, allowed)
-    attention_full = jnp.exp(masked - lse_parts)
-    upstream_block = mixed_grad.reshape(block_rows, HK, HQ // HK, HD)
-    attn_grad = jnp.einsum(
-        "qkgd,tkd->kgqt", upstream_block, values, preferred_element_type=jnp.float32
-    )
-    score_low = (
-        attention_full * (attn_grad - jnp.sum(attention_full * attn_grad, axis=-1, keepdims=True))
-    ).astype(bf16)
-    query_block_grad = jnp.einsum(
-        "kgqt,tkd->qkgd", score_low, key_rot, preferred_element_type=jnp.float32
-    ) * HD ** (-0.5)
-    query_parts = query_block_grad.reshape(block_rows, HQ, HD)
-    key_rot_grad = jnp.einsum(
-        "kgqt,qkgd->tkd", score_low, shaped, preferred_element_type=jnp.float32
-    ) * HD ** (-0.5)
-    value_grad = jnp.einsum(
-        "kgqt,qkgd->tkd",
-        attention_full.astype(bf16),
-        upstream_block,
-        preferred_element_type=jnp.float32,
-    )
-    query_grad = rotate(query_parts, position, -1.0).reshape(length, HQ * HD).astype(bf16)
-    key_grad = rotate(key_rot_grad, position, -1.0).reshape(length, HK * HD).astype(bf16)
-    value_low = value_grad.reshape(length, HK * HD).astype(bf16)
-    joint_grad = jnp.concatenate([query_grad, key_grad, value_low], axis=1)
+    joint_grad = attention_backward(
+        (middle_low, output_full, query_rot, key_rot, values, cosine, sine, mask, late)
+    )
     grad_joint = jnp.einsum("td,tq->dq", first_low, joint_grad, preferred_element_type=jnp.float32)
     group_joint = lax.psum_scatter(
         grad_joint.astype(bf16), "shard", scatter_dimension=0, tiled=True
     )
-    joint_full = jnp.concatenate([query_full, pair_full[0], pair_full[1]], axis=0)
-    first_grad = jnp.dot(joint_grad, joint_full, preferred_element_type=jnp.float32)
+    first_grad = (
+        nn(joint_grad[:, :QW], query_full)
+        + nn(joint_grad[:, QW : QW + HK * HD], key_full)
+        + nn(joint_grad[:, QW + HK * HD :], value_full)
+    )
     _, first_pull = jax.vjp(rms_norm, hidden, gain_values[0])
     hidden_part, gain_one = first_pull(first_grad)
     input_grad = (middle_grad + hidden_part).astype(bf16)
     grad_gains = jnp.stack([gain_one, gain_two])
+
+    state["gate"] = joint_grad
+    if filled and paired:
+        others(3, [1, 2, 3], True)
+        others(2, [2, 3], True)
+        others(0, [2, 3], True)
+        others(1, [2, 3], True)
+    else:
+        for index in chunks:
+            all_others(index, steps)
 
     small_rows = [jnp.transpose(grad_router), jnp.pad(grad_gains, ((0, 6), (0, 0)))]
     start_q, start_o = jnp.transpose(query_start), jnp.transpose(output_start)
@@ -1136,7 +1596,10 @@
     )
     bases = tuple(jnp.swapaxes(left, -1, -2) for left in lefts_t)
 
-    right_parts = right_experts(lefts_in, lefts_out, *merged_experts)
+    right_parts = [
+        right_experts(index * per_chunk, lefts_in, lefts_out, *merged_parts[index])
+        for index in range(CHUNKS)
+    ]
     right_rest = right_attention(
         shard_count,
         own_rows,
@@ -1146,7 +1609,7 @@
         ),
     )
     rights = right_sync(replicas, shard_count, right_parts, right_rest)
-    hidden_units = merged_experts[0].shape[3]
+    hidden_units = inner_error.shape[4]
     step = 2 * hidden_units + D
     by_expert = rights[:, : E * step].reshape(8, E, step)
     rest = rights[:, E * step :]
@@ -1160,9 +1623,14 @@
     )
     right_out = tuple(jnp.swapaxes(right, -1, -2) for right in rights_t)
 
-    feedback_in, feedback_out, squares_experts = feedback_experts(
-        replicas, lefts_in, lefts_out, rights, *merged_experts
-    )
+    feedback_in = feedback_out = None
+    squares_experts = []
+    for index in range(CHUNKS):
+        feedback_in, feedback_out, part = feedback_experts(
+            replicas, index * per_chunk, lefts_in, lefts_out, rights, *merged_parts[index],
+            feedback_in, feedback_out,
+        )
+        squares_experts.append(part)
     feedback_q, feedback_p, feedback_o, squares_rest = feedback_attention(
         replicas,
         own_rows,
@@ -1174,7 +1642,7 @@
     feedbacks = tuple(
         part[None] for part in (feedback_q, feedback_p, feedback_o, feedback_in, feedback_out)
     )
-    squares = squares_sync(replicas, shard_count, squares_experts, squares_rest)
+    squares = squares_sync(replicas, shard_count, squares_experts + [squares_rest])
     flat_squares = jnp.concatenate(
         [squares[0, 3:7], squares[:, 0], squares[:, 1], squares[:, 2]], axis=0
     )

time: 1130 us -> 912 us (0.81)
  waiting for transfers between devices: 275 us -> 69.1 us
  Pallas kernels: 436 us -> 604 us
  local copies, waits for them, and re-layouts: 137 us -> 53.3 us
  matrix products: 104 us -> 48.3 us
  starting transfers between devices: 80.1 us -> 52.5 us
  other arithmetic: 75.7 us -> 57.9 us
    ppermute x24 -> x18, waiting for transfers between devices: 273 us -> 53.4 us  [the longest x6 30.5 us: z_slots(): lax.ppermute(block, 'shard', [(i, (i + step) % size) for i in range(size)])]
    pallas_call x7 -> x20, Pallas kernels: 338 us -> 515 us  [the longest x7 187 us: rest_experts(): pl.pallas_call(functools.partial(rest_kernel, first_expert, trees, last,...]
    dot_general x11 -> x3, matrix products: 66 us -> 11 us  [nn(): return jnp.dot(a, b, preferred_element_type=F32, precision=precision)]
    ppermute x24 -> x18, starting transfers between devices: 79.1 us -> 51.2 us  [the longest x6 34.8 us: pass_on(): lax.ppermute(up, 'shard', forth)]
    another operation x16 -> x2, other arithmetic: 25 us -> 4.74 us  [the longest x1 2.77 us: per_device(): gathered(jnp.stack(near), True)]
    ppermute x6 -> x0, local copies, waits for them, and re-layouts: 20.2 us -> none  [the longest x3 10.5 us: z_ring(): up = lax.ppermute(up, 'shard', [(i, i + 1) for i in range(size - 1)])]
    unnamed x193 -> x148, local copies, waits for them, and re-layouts: 26.6 us -> 8.12 us
    all_gather x5 -> x4, waiting for transfers between devices: 0.08 us -> 15 us  [gathered(): part = lax.all_gather(line, 'rep')]
  transfers between devices with their start and end apart: 32 -> 25, of which waited for: 18 -> 5; matrix products, arithmetic and copies ran while one was open for 25% -> 16% of each run, Pallas kernels for 31% -> 54%
where the time goes in v2:
time: 912 us; the launch traced here: 902 us
  Pallas kernels  604 us (66%)
  waiting for transfers between devices  69.1 us (8%)
  other arithmetic  57.9 us (6%)
  local copies, waits for them, and re-layouts  53.3 us (6%)
  starting transfers between devices  52.5 us (6%)
  matrix products  48.3 us (5%)
  between operations  17.6 us (2%)
    pallas_call x7, Pallas kernels, rest_experts(): pl.pallas_call(functools.partial(rest_kernel, first_expert, trees, last,...  187 us
    pallas_call x4, Pallas kernels, own_experts(): pl.pallas_call(functools.partial(own_kernel, first_expert, turned), grid=...  117 us
    pallas_call x1, Pallas kernels, open_gather(): pl.pallas_call(functools.partial(open_kernel, reps, shards, [at for at, _...  98.1 us
    pallas_call x1, Pallas kernels, left_sync(): pl.pallas_call(functools.partial(left_sync_kernel, reps, shards, wide, wi...  46.2 us
    ppermute x6, starting transfers between devices, pass_on(): lax.ppermute(up, 'shard', forth)  34.8 us
    ppermute x6, waiting for transfers between devices, z_slots(): lax.ppermute(block, 'shard', [(i, (i + step) % size) for i in range(size)])  30.5 us
    pallas_call x1, Pallas kernels, right_sync(): pl.pallas_call(functools.partial(right_sync_kernel, reps, shards, piece,...  27.8 us
    pallas_call x1, Pallas kernels, attention_forward(): pl.pallas_call(attention_forward_kernel, in_specs=vmem_specs(len(operands...  25.5 us
  transfers between devices with their start and end apart: 25, of which 5 were waited for; matrix products, arithmetic and copies ran while one was open for 16% of the time, Pallas kernels for 54%

profile of v2, /device:TPU:0, one launch (start us, length us, event | category | flops | bytes accessed | tf_op | source)
XLA Modules:
  0.0 902.4 jit_solution(6336899618179237754)
XLA Ops:
  14.5 98.1 %open_gather.1 = (bf16[1536,1536]{1,0:T(8,128)(2,1)}, bf16[256,1536]{1,0:T(8,128)(2,1)}, bf16[256,1536]{1,0:T(8,128)(2,1)}, bf16[1536,1536]{1,0:T(8,128)(2,1)}, ...) custom-call(bf16[192,384]{1,0:T(8,128)(2,1)} %get-tuple-element.466.refs_0_, ...), custom_call_target="tpu_custom_call" | custom-call | tf_op jit(solution)/shard_map/open_gather/pallas_call | solution.py:707
  121.1 25.5 %attention_forward.1 = (bf16[512,1536]{1,0:T(8,128)(2,1)}, bf16[512,256]{1,0:T(8,128)(2,1)}, bf16[512,256]{1,0:T(8,128)(2,1)}, bf16[512,1536]{1,0:T(8,128)(2,1)}, f32[512,1536]{1,0:T(8,128)}) custom-call(bf16[512,1536]{1,0:T(8,128)(2,1)} %fusion.2.first_ref, bf16[1536,1536]{1,0:T(8,128)(2,1)} %get-tuple-element.133.query_ref, ...), custom_call_target="tpu_custom_call" | custom-call | flops 7247757312 | bytes 20447232 | tf_op jit(solution)/shard_map/attention_forward/pallas_call | solution.py:186
  174.6 15.0 %all-gather.9.cloned.1.call-done = bf16[32,576,384]{2,1,0:T(8,128)(2,1)} async-done(((bf16[4,576,384]{2,1,0:T(8,128)(2,1)}), bf16[32,576,384]{2,1,0:T(8,128)(2,1)}) %all-gather.9.cloned.1.call-update) | async-done | bytes 14155792 | tf_op jit(solution)/shard_map/all_gather | solution.py:1392
  189.6 28.9 %own_experts.4 = (f32[2,2,384,768]{3,2,1,0:T(8,128)}, f32[2,192,1536]{2,1,0:T(8,128)}, f32[512,1536]{1,0:T(8,128)}, f32[512,1536]{1,0:T(8,128)}, f32[2,512,1]{2,1,0:T(8,128)}) custom-call(bf16[1552,512]{1,0:T(8,128)(2,1)} %copy.287.x_ref, bf16[1536,512]{1,0:T(8,128)(2,1)} %copy.288.u_ref, bf16[512,1536]{1,0:T(8,128)(2,1)} %up_ref.7, ...), custom_call_target="tpu_custom_call" | custom-call | flops 33822867456 | bytes 37748736 | tf_op jit(solution)/shard_map/own_experts/pallas_call | solution.py:455
  219.8 28.5 %collective-permute-done.5 = bf16[1152,384]{1,0:T(8,128)(2,1)} collective-permute-done((bf16[1152,384]{1,0:T(8,128)(2,1)S(1)}, bf16[1152,384]{1,0:T(8,128)(2,1)}, u32[]{:S(2)}, u32[]{:S(2)}) %collective-permute-start.5) | collective-permute-done | bytes 884768 | tf_op jit(solution)/shard_map/ppermute | solution.py:75
  273.7 28.9 %own_experts.5 = (f32[2,2,384,768]{3,2,1,0:T(8,128)}, f32[2,192,1536]{2,1,0:T(8,128)}, f32[512,1536]{1,0:T(8,128)}, f32[512,1536]{1,0:T(8,128)}, f32[2,512,1]{2,1,0:T(8,128)}) custom-call(bf16[1552,512]{1,0:T(8,128)(2,1)} %copy.290.x_ref, bf16[1536,512]{1,0:T(8,128)(2,1)} %copy.291.u_ref, bf16[512,1536]{1,0:T(8,128)(2,1)} %up_ref.7, ...), custom_call_target="tpu_custom_call" | custom-call | flops 33822867456 | bytes 37748736 | tf_op jit(solution)/shard_map/own_experts/pallas_call | solution.py:455
  305.2 21.6 %collective-permute-done.9 = bf16[1552,512]{1,0:T(8,128)(2,1)S(1)} collective-permute-done((bf16[1552,512]{1,0:T(8,128)(2,1)}, bf16[1552,512]{1,0:T(8,128)(2,1)S(1)}, u32[]{:S(2)}, u32[]{:S(2)}) %collective-permute-start.9) | collective-permute-done | bytes 1589280 | tf_op jit(solution)/shard_map/ppermute | solution.py:1470
  346.9 17.6 %rest_experts.7 = (f32[2,2,384,768]{3,2,1,0:T(8,128)}, f32[2,192,1536]{2,1,0:T(8,128)}) custom-call(bf16[8,4,3,192,384]{4,3,2,1,0:T(8,128)(2,1)} %bitcast.260, bf16[4,2,4,3,192,384]{5,4,3,2,1,0:T(8,128)(2,1)} %bitcast.261, f32[2,8,8,768]{3,2,1,0:T(8,128)} %bitcast.287, f32[8,8,1536]{2,1,0:T(8,128)} %bitcast.294, ...), custom_call_target="tpu_custom_call", output_to_operand_aliasing={{0}: (4, {}), {1}: (5, {})} | custom-call | flops 16911433728 | bytes 28311552 | tf_op jit(solution)/shard_map/rest_experts/pallas_call | solution.py:503
  365.8 29.9 %own_experts.6 = (f32[2,2,384,768]{3,2,1,0:T(8,128)}, f32[2,192,1536]{2,1,0:T(8,128)}, f32[512,1536]{1,0:T(8,128)}, f32[512,1536]{1,0:T(8,128)}, f32[2,512,1]{2,1,0:T(8,128)}) custom-call(bf16[1552,512]{1,0:T(8,128)(2,1)} %copy.290.x_ref, bf16[1536,512]{1,0:T(8,128)(2,1)} %copy.291.u_ref, bf16[512,1536]{1,0:T(8,128)(2,1)} %up_ref.7, ...), custom_call_target="tpu_custom_call" | custom-call | flops 33822867456 | bytes 37748736 | tf_op jit(solution)/shard_map/own_experts/pallas_call | solution.py:455
  398.2 17.7 %rest_experts.8 = (f32[2,2,384,768]{3,2,1,0:T(8,128)}, f32[2,192,1536]{2,1,0:T(8,128)}) custom-call(bf16[8,4,3,192,384]{4,3,2,1,0:T(8,128)(2,1)} %bitcast.266, bf16[4,2,4,3,192,384]{5,4,3,2,1,0:T(8,128)(2,1)} %bitcast.267, f32[2,8,8,768]{3,2,1,0:T(8,128)} %bitcast.288, f32[8,8,1536]{2,1,0:T(8,128)} %bitcast.295, ...), custom_call_target="tpu_custom_call", output_to_operand_aliasing={{0}: (4, {}), {1}: (5, {})} | custom-call | flops 16911433728 | bytes 28311552 | tf_op jit(solution)/shard_map/rest_experts/pallas_call | solution.py:503
  431.9 17.4 %rest_experts.9 = (f32[2,2,384,768]{3,2,1,0:T(8,128)}, f32[2,192,1536]{2,1,0:T(8,128)}) custom-call(bf16[8,4,3,192,384]{4,3,2,1,0:T(8,128)(2,1)} %bitcast.272, bf16[4,2,4,3,192,384]{5,4,3,2,1,0:T(8,128)(2,1)} %bitcast.273, f32[2,8,8,768]{3,2,1,0:T(8,128)} %bitcast.289, f32[8,8,1536]{2,1,0:T(8,128)} %bitcast.296, ...), custom_call_target="tpu_custom_call", output_to_operand_aliasing={{0}: (4, {}), {1}: (5, {})} | custom-call | flops 16911433728 | bytes 28311552 | tf_op jit(solution)/shard_map/rest_experts/pallas_call | solution.py:503
  450.6 29.6 %own_experts.7 = (f32[2,2,384,768]{3,2,1,0:T(8,128)}, f32[2,192,1536]{2,1,0:T(8,128)}, f32[512,1536]{1,0:T(8,128)}, f32[512,1536]{1,0:T(8,128)}, f32[2,512,1]{2,1,0:T(8,128)}) custom-call(bf16[1552,512]{1,0:T(8,128)(2,1)} %copy.290.x_ref, bf16[1536,512]{1,0:T(8,128)(2,1)} %copy.291.u_ref, bf16[512,1536]{1,0:T(8,128)(2,1)} %up_ref.7, ...), custom_call_target="tpu_custom_call" | custom-call | flops 33822867456 | bytes 37748736 | tf_op jit(solution)/shard_map/own_experts/pallas_call | solution.py:455
  510.3 23.4 %attention_backward.1.joint_ref.rest_6_ = bf16[512,2048]{1,0:T(8,128)(2,1)} custom-call(bf16[512,1536]{1,0:T(8,128)(2,1)} %copy-done.14, bf16[1536,1536]{1,0:T(8,128)(2,1)} %get-tuple-element.136.output_ref, bf16[512,1536]{1,0:T(8,128)(2,1)} %get-tuple-element.180.qrot_ref, bf16[512,256]{1,0:T(8,128)(2,1)} %get-tuple-element.181.krot_ref, ...), custom_call_target="tpu_custom_call" | custom-call | flops 9663676416 | bytes 786432 | tf_op jit(solution)/shard_map/attention_backward/pallas_call | solution.py:241
  550.2 42.2 %rest_experts.10 = (f32[2,2,384,768]{3,2,1,0:T(8,128)}, f32[2,192,1536]{2,1,0:T(8,128)}, f32[2,2,8,384]{3,2,1,0:T(8,128)}, f32[2,8,256]{2,1,0:T(8,128)}) custom-call(bf16[8,4,3,192,384]{4,3,2,1,0:T(8,128)(2,1)} %bitcast.278, bf16[4,2,4,3,192,384]{5,4,3,2,1,0:T(8,128)(2,1)} %bitcast.279, ...), custom_call_target="tpu_custom_call", output_to_operand_aliasing={{0}: (4, {}), {1}: (5, {})} | custom-call | flops 50734301184 | bytes 28311552 | tf_op jit(solution)/shard_map/rest_experts/pallas_call | solution.py:503
  593.6 30.6 %rest_experts.11 = (f32[2,2,384,768]{3,2,1,0:T(8,128)}, f32[2,192,1536]{2,1,0:T(8,128)}, f32[2,2,8,384]{3,2,1,0:T(8,128)}, f32[2,8,256]{2,1,0:T(8,128)}) custom-call(bf16[8,4,3,192,384]{4,3,2,1,0:T(8,128)(2,1)} %bitcast.274, bf16[4,2,4,3,192,384]{5,4,3,2,1,0:T(8,128)(2,1)} %bitcast.275, ...), custom_call_target="tpu_custom_call", output_to_operand_aliasing={{0}: (4, {}), {1}: (5, {})} | custom-call | flops 33822867456 | bytes 28311552 | tf_op jit(solution)/shard_map/rest_experts/pallas_call | solution.py:503
  626.1 7.1 convolution_convert_fusion.1
  633.3 9.4 %left_parts.1 = (f32[4,8,2304]{2,1,0:T(8,128)}, f32[8,1536]{1,0:T(8,128)}) custom-call(bf16[512,1536]{1,0:T(8,128)(2,1)} %fusion.2.first_ref, bf16[512,2048]{1,0:T(8,128)(2,1)} %attention_backward.1.joint_ref.rest_6_, bf16[512,1536]{1,0:T(8,128)(2,1)} %get-tuple-element.187.mixed_ref, bf16[512,1536]{1,0:T(8,128)(2,1)} %copy-done.14, f32[8,1536]{1,0:T(8,128)} %bitcast.246, ...), custom_call_target="tpu_custom_call" | custom-call | tf_op jit(solution)/shard_map/left_parts/pallas_call | solution.py:758
  642.7 30.4 %rest_experts.12 = (f32[2,2,384,768]{3,2,1,0:T(8,128)}, f32[2,192,1536]{2,1,0:T(8,128)}, f32[2,2,8,384]{3,2,1,0:T(8,128)}, f32[2,8,256]{2,1,0:T(8,128)}) custom-call(bf16[8,4,3,192,384]{4,3,2,1,0:T(8,128)(2,1)} %bitcast.262, bf16[4,2,4,3,192,384]{5,4,3,2,1,0:T(8,128)(2,1)} %bitcast.263, ...), custom_call_target="tpu_custom_call", output_to_operand_aliasing={{0}: (4, {}), {1}: (5, {})} | custom-call | flops 33822867456 | bytes 28311552 | tf_op jit(solution)/shard_map/rest_experts/pallas_call | solution.py:503
  674.4 31.1 %rest_experts.13 = (f32[2,2,384,768]{3,2,1,0:T(8,128)}, f32[2,192,1536]{2,1,0:T(8,128)}, f32[2,2,8,384]{3,2,1,0:T(8,128)}, f32[2,8,256]{2,1,0:T(8,128)}) custom-call(bf16[8,4,3,192,384]{4,3,2,1,0:T(8,128)(2,1)} %bitcast.268, bf16[4,2,4,3,192,384]{5,4,3,2,1,0:T(8,128)(2,1)} %bitcast.269, ...), custom_call_target="tpu_custom_call", output_to_operand_aliasing={{0}: (4, {}), {1}: (5, {})} | custom-call | flops 33822867456 | bytes 28311552 | tf_op jit(solution)/shard_map/rest_experts/pallas_call | solution.py:503
  705.5 46.2 %left_sync.1 = (f32[160,384]{1,0:T(8,128)}, f32[64,256]{1,0:T(8,128)}, f32[2,8,384]{2,1,0:T(8,128)}, f32[8,128]{1,0:T(8,128)}, f32[4,32,384]{2,1,0:T(8,128)}) custom-call(f32[4,8,2304]{2,1,0:T(8,128)} %get-tuple-element.188.refs_0_, f32[8,1536]{1,0:T(8,128)} %get-tuple-element.189.refs_1_, f32[2,2,8,384]{3,2,1,0:T(8,128)} %get-tuple-element.196.refs_2_, ...), custom_call_target="tpu_custom_call" | custom-call | tf_op jit(solution)/shard_map/left_sync/pallas_call | solution.py:924
  767.8 9.0 %right_attention.1.refs_4_ = f32[8,3584]{1,0:T(8,128)} custom-call(f32[32,384]{1,0:T(8,128)} %slice.250.left_ref, f32[4,32,384]{2,1,0:T(8,128)} %get-tuple-element.213.leftz_ref, bf16[512,1536]{1,0:T(8,128)(2,1)} %fusion.2.first_ref, bf16[512,2048]{1,0:T(8,128)(2,1)} %attention_backward.1.joint_ref.rest_6_, bf16[512,1536]{1,0:T(8,128)(2,1)} %get-tuple-element.187.mixed_ref, ...), custom_call_target="tpu_custom_call" | custom-call | tf_op jit(solution)/shard_map/right_attention/pallas_call | solution.py:1024
  781.2 27.8 %right_sync.1.right_ref = f32[8,28672]{1,0:T(8,128)} custom-call(f32[2,8,3072]{2,1,0:T(8,128)} %right_experts.4.refs_0_, f32[2,8,3072]{2,1,0:T(8,128)} %right_experts.5.refs_1_, f32[2,8,3072]{2,1,0:T(8,128)} %right_experts.6.refs_2_, f32[2,8,3072]{2,1,0:T(8,128)} %right_experts.7.refs_3_, f32[8,3584]{1,0:T(8,128)} %right_attention.1.refs_4_), custom_call_target="tpu_custom_call" | custom-call | tf_op jit(solution)/shard_map/right_sync/pallas_call | solution.py:1070
  875.2 6.9 feedback_attention.1
  882.2 10.9 %squares_sync.1 = f32[8,128]{1,0:T(8,128)} custom-call(f32[8,128]{1,0:T(8,128)} %get-tuple-element.227.refs_0_, f32[8,128]{1,0:T(8,128)} %get-tuple-element.228.refs_1_, f32[8,128]{1,0:T(8,128)} %get-tuple-element.229.refs_2_, f32[8,128]{1,0:T(8,128)} %get-tuple-element.230.refs_3_, f32[8,128]{1,0:T(8,128)} %get-tuple-element.231.refs_4_), custom_call_target="tpu_custom_call" | custom-call | tf_op jit(solution)/shard_map/squares_sync/pallas_call | solution.py:1221
  (331 shorter events, 251.0 us)
Async XLA Ops:
  7.3 182.4 %all-gather.9.cloned.1.call-start = ((), (), s32[]{:S(2)}) async-start(), calls=%async_computation.4 | async-start | bytes 15925248 | tf_op jit(solution)/shard_map/all_gather | solution.py:1392
  112.6 161.2 %all-gather.11.cloned.1.call-start = ((), (), s32[]{:S(2)}) async-start(), calls=%async_computation.5 | async-start | bytes 15925248 | tf_op jit(solution)/shard_map/all_gather | solution.py:1392
  116.4 38.0 %collective-permute-start.3 = (bf16[576,384]{1,0:T(8,128)(2,1)S(1)}, bf16[576,384]{1,0:T(8,128)(2,1)}, u32[]{:S(2)}, u32[]{:S(2)}) collective-permute-start(bf16[576,384]{1,0:T(8,128)(2,1)S(1)} %pad_maximum_fusion.4), channel_id=1, source_target_pairs={{0,3},{1,0},{2,1},{3,2},{4,7},{5,4},{6,5},{7,6},{8,11},{9,8},{10,9... | collective-permute-start | bytes 1327112 | tf_op jit(solution)/shard_map/ppermute | solution.py:75
  118.8 37.7 %collective-permute-start.2 = (bf16[576,384]{1,0:T(8,128)(2,1)S(1)}, bf16[576,384]{1,0:T(8,128)(2,1)}, u32[]{:S(2)}, u32[]{:S(2)}) collective-permute-start(bf16[576,384]{1,0:T(8,128)(2,1)S(1)} %pad_maximum_fusion.4), channel_id=1, source_target_pairs={{0,2},{1,3},{2,0},{3,1},{4,6},{5,7},{6,4},{7,5},{8,10},{9,11},{10,... | collective-permute-start | bytes 1327112 | tf_op jit(solution)/shard_map/ppermute | solution.py:75
  118.8 37.7 %collective-permute-start.1 = (bf16[576,384]{1,0:T(8,128)(2,1)S(1)}, bf16[576,384]{1,0:T(8,128)(2,1)}, u32[]{:S(2)}, u32[]{:S(2)}) collective-permute-start(bf16[576,384]{1,0:T(8,128)(2,1)S(1)} %pad_maximum_fusion.4), channel_id=1, source_target_pairs={{0,1},{1,2},{2,3},{3,0},{4,5},{5,6},{6,7},{7,4},{8,9},{9,10},{10,1... | collective-permute-start | bytes 1327112 | tf_op jit(solution)/shard_map/ppermute | solution.py:75
  159.3 206.5 %all-gather.13.cloned.1.call-start = ((), (), s32[]{:S(2)}) async-start(), calls=%async_computation.6 | async-start | bytes 15925248 | tf_op jit(solution)/shard_map/all_gather | solution.py:1392
  168.5 51.3 %collective-permute-start.6 = (bf16[1152,384]{1,0:T(8,128)(2,1)S(1)}, bf16[1152,384]{1,0:T(8,128)(2,1)}, u32[]{:S(2)}, u32[]{:S(2)}) collective-permute-start(bf16[1152,384]{1,0:T(8,128)(2,1)S(1)} %copy-done.25), channel_id=1, source_target_pairs={{0,3},{1,0},{2,1},{3,2},{4,7},{5,4},{6,5},{7,6},{8,11},{9,8},{10,9... | collective-permute-start | bytes 2654216 | tf_op jit(solution)/shard_map/ppermute | solution.py:75
  169.9 78.4 %collective-permute-start.5 = (bf16[1152,384]{1,0:T(8,128)(2,1)S(1)}, bf16[1152,384]{1,0:T(8,128)(2,1)}, u32[]{:S(2)}, u32[]{:S(2)}) collective-permute-start(bf16[1152,384]{1,0:T(8,128)(2,1)S(1)} %copy-done.25), channel_id=1, source_target_pairs={{0,2},{1,3},{2,0},{3,1},{4,6},{5,7},{6,4},{7,5},{8,10},{9,11},{10,... | collective-permute-start | bytes 2654216 | tf_op jit(solution)/shard_map/ppermute | solution.py:75
  171.9 76.3 %collective-permute-start.4 = (bf16[1152,384]{1,0:T(8,128)(2,1)S(1)}, bf16[1152,384]{1,0:T(8,128)(2,1)}, u32[]{:S(2)}, u32[]{:S(2)}) collective-permute-start(bf16[1152,384]{1,0:T(8,128)(2,1)S(1)} %copy-done.25), channel_id=1, source_target_pairs={{0,1},{1,2},{2,3},{3,0},{4,5},{5,6},{6,7},{7,4},{8,9},{9,10},{10,1... | collective-permute-start | bytes 2654216 | tf_op jit(solution)/shard_map/ppermute | solution.py:75
  252.4 198.2 %all-gather.15.cloned.1.call-start = ((), (), s32[]{:S(2)}) async-start(), calls=%async_computation.7 | async-start | bytes 15925248 | tf_op jit(solution)/shard_map/all_gather | solution.py:1392
  253.0 622.2 %reduce-scatter.5.cloned.1.call-start = ((), (), s32[]{:S(2)}) async-start(), calls=%async_computation.3 | async-start | bytes 5898240 | tf_op jit(solution)/shard_map/reduce_scatter | solution.py:1542
  255.7 49.6 %collective-permute-start.10 = (bf16[1536,512]{0,1:T(8,128)(2,1)S(1)}, bf16[1536,512]{0,1:T(8,128)(2,1)}, u32[]{:S(2)}, u32[]{:S(2)}) collective-permute-start(bf16[1536,512]{0,1:T(8,128)(2,1)S(1)} %bitcast.205), channel_id=1, source_target_pairs={{1,0},{2,1},{3,2},{5,4},{6,5},{7,6},{9,8},{10,9},{11,10},{13,12},{... | collective-permute-start | bytes 4718600 | tf_op jit(solution)/shard_map/ppermute | solution.py:1470
  257.0 48.3 %collective-permute-start.8 = (bf16[1536,512]{0,1:T(8,128)(2,1)S(1)}, bf16[1536,512]{0,1:T(8,128)(2,1)}, u32[]{:S(2)}, u32[]{:S(2)}) collective-permute-start(bf16[1536,512]{0,1:T(8,128)(2,1)S(1)} %bitcast.206), channel_id=1, source_target_pairs={{0,1},{1,2},{2,3},{4,5},{5,6},{6,7},{8,9},{9,10},{10,11},{12,13},{... | collective-permute-start | bytes 4718600 | tf_op jit(solution)/shard_map/ppermute | solution.py:1469
  264.9 62.0 %collective-permute-start.9 = (bf16[1552,512]{1,0:T(8,128)(2,1)}, bf16[1552,512]{1,0:T(8,128)(2,1)S(1)}, u32[]{:S(2)}, u32[]{:S(2)}) collective-permute-start(bf16[1552,512]{1,0:T(8,128)(2,1)} %copy.290.x_ref), channel_id=1, source_target_pairs={{1,0},{2,1},{3,2},{5,4},{6,5},{7,6},{9,8},{10,9},{11,10},{13,12},{... | collective-permute-start | bytes 4767752 | tf_op jit(solution)/shard_map/ppermute | solution.py:1470
  266.1 62.0 %collective-permute-start.7 = (bf16[1552,512]{1,0:T(8,128)(2,1)}, bf16[1552,512]{1,0:T(8,128)(2,1)}, u32[]{:S(2)}, u32[]{:S(2)}) collective-permute-start(bf16[1552,512]{1,0:T(8,128)(2,1)} %copy.290.x_ref), channel_id=1, source_target_pairs={{0,1},{1,2},{2,3},{4,5},{5,6},{6,7},{8,9},{9,10},{10,11},{12,13},{... | collective-permute-start | bytes 4767752 | tf_op jit(solution)/shard_map/ppermute | solution.py:1469
  328.2 89.0 %collective-permute-start.12 = (bf16[1536,512]{0,1:T(8,128)(2,1)}, bf16[1536,512]{0,1:T(8,128)(2,1)}, u32[]{:S(2)}, u32[]{:S(2)}) collective-permute-start(bf16[1536,512]{0,1:T(8,128)(2,1)} %collective-permute-done.8), channel_id=1, source_target_pairs={{0,1},{1,2},{2,3},{4,5},{5,6},{6,7},{8,9},{9,10},{10,11},{12,13},{... | collective-permute-start | bytes 4718600 | tf_op jit(solution)/shard_map/ppermute | solution.py:1469
  333.7 83.5 %collective-permute-start.14 = (bf16[1536,512]{0,1:T(8,128)(2,1)}, bf16[1536,512]{0,1:T(8,128)(2,1)}, u32[]{:S(2)}, u32[]{:S(2)}) collective-permute-start(bf16[1536,512]{0,1:T(8,128)(2,1)} %collective-permute-done.10), channel_id=1, source_target_pairs={{1,0},{2,1},{3,2},{5,4},{6,5},{7,6},{9,8},{10,9},{11,10},{13,12},{... | collective-permute-start | bytes 4718600 | tf_op jit(solution)/shard_map/ppermute | solution.py:1470
  338.2 79.0 %collective-permute-start.11 = (bf16[1552,512]{1,0:T(8,128)(2,1)}, bf16[1552,512]{1,0:T(8,128)(2,1)}, u32[]{:S(2)}, u32[]{:S(2)}) collective-permute-start(bf16[1552,512]{1,0:T(8,128)(2,1)} %collective-permute-done.7), channel_id=1, source_target_pairs={{0,1},{1,2},{2,3},{4,5},{5,6},{6,7},{8,9},{9,10},{10,11},{12,13},{... | collective-permute-start | bytes 4767752 | tf_op jit(solution)/shard_map/ppermute | solution.py:1469
  344.0 73.2 %collective-permute-start.13 = (bf16[1552,512]{1,0:T(8,128)(2,1)S(1)}, bf16[1552,512]{1,0:T(8,128)(2,1)}, u32[]{:S(2)}, u32[]{:S(2)}) collective-permute-start(bf16[1552,512]{1,0:T(8,128)(2,1)S(1)} %collective-permute-done.9), channel_id=1, source_target_pairs={{1,0},{2,1},{3,2},{5,4},{6,5},{7,6},{9,8},{10,9},{11,10},{13,12},{... | collective-permute-start | bytes 4767752 | tf_op jit(solution)/shard_map/ppermute | solution.py:1470
  417.2 83.2 %collective-permute-start.16 = (bf16[1536,512]{0,1:T(8,128)(2,1)}, bf16[1536,512]{0,1:T(8,128)(2,1)}, u32[]{:S(2)}, u32[]{:S(2)}) collective-permute-start(bf16[1536,512]{0,1:T(8,128)(2,1)} %collective-permute-done.12), channel_id=1, source_target_pairs={{0,1},{1,2},{2,3},{4,5},{5,6},{6,7},{8,9},{9,10},{10,11},{12,13},{... | collective-permute-start | bytes 4718600 | tf_op jit(solution)/shard_map/ppermute | solution.py:1469
  423.6 76.8 %collective-permute-start.18 = (bf16[1536,512]{0,1:T(8,128)(2,1)}, bf16[1536,512]{0,1:T(8,128)(2,1)}, u32[]{:S(2)}, u32[]{:S(2)}) collective-permute-start(bf16[1536,512]{0,1:T(8,128)(2,1)} %collective-permute-done.14), channel_id=1, source_target_pairs={{1,0},{2,1},{3,2},{5,4},{6,5},{7,6},{9,8},{10,9},{11,10},{13,12},{... | collective-permute-start | bytes 4718600 | tf_op jit(solution)/shard_map/ppermute | solution.py:1470
  424.9 82.4 %collective-permute-start.15 = (bf16[1552,512]{1,0:T(8,128)(2,1)}, bf16[1552,512]{1,0:T(8,128)(2,1)}, u32[]{:S(2)}, u32[]{:S(2)}) collective-permute-start(bf16[1552,512]{1,0:T(8,128)(2,1)} %collective-permute-done.11), channel_id=1, source_target_pairs={{0,1},{1,2},{2,3},{4,5},{5,6},{6,7},{8,9},{9,10},{10,11},{12,13},{... | collective-permute-start | bytes 4767752 | tf_op jit(solution)/shard_map/ppermute | solution.py:1469
  430.6 77.5 %collective-permute-start.17 = (bf16[1552,512]{1,0:T(8,128)(2,1)}, bf16[1552,512]{1,0:T(8,128)(2,1)}, u32[]{:S(2)}, u32[]{:S(2)}) collective-permute-start(bf16[1552,512]{1,0:T(8,128)(2,1)} %collective-permute-done.13), channel_id=1, source_target_pairs={{1,0},{2,1},{3,2},{5,4},{6,5},{7,6},{9,8},{10,9},{11,10},{13,12},{... | collective-permute-start | bytes 4767752 | tf_op jit(solution)/shard_map/ppermute | solution.py:1470
  498.0 377.2 %reduce-scatter.3.cloned.1.call-start = ((), (), s32[]{:S(2)}) async-start(), calls=%async_computation.2 | async-start | bytes 7864320 | tf_op jit(solution)/shard_map/reduce_scatter | solution.py:1549
  (75 other events, 1084.2 us)
Sparse Core Ops, SparseCore 0:
  112.7 76.8 all-gather.8
  192.1 78.7 all-gather.10
  273.4 78.7 all-gather.12
  354.5 78.7 all-gather.14
  498.2 86.0 reduce-scatter.4
  633.4 119.0 reduce-scatter.2

commit v3 on v2

--- a/solution.py
+++ b/solution.py
@@ -61,6 +61,7 @@
 
 
 CHUNKS = 4
+PARTS = 2
 GELU_C = 0.7978845608028654
 GELU_A = 0.044715
 MESH = pl.DeviceIdType.MESH
@@ -205,8 +206,8 @@
 
 
 def attention_backward_kernel(
-    middle_ref, output_ref, qrot_ref, krot_ref, values_ref, cosine_ref, sine_ref, mask_ref, late_ref,
-    joint_ref, mixed_ref, dk_ref, dv_ref,
+    middle_ref, output_ref, qrot_ref, krot_ref, values_ref, cosine_ref, sine_ref, mask_ref, first_ref,
+    late_ref, joint_ref, grad_ref, mixed_ref, dk_ref, dv_ref,
 ):
     cosine, sine = cosine_ref[...], -sine_ref[...]
     mixed_ref[...] = nn(middle_ref[...], output_ref[...]).astype(BF16)
@@ -233,6 +234,12 @@
         turned = dk_ref[:, span] * HD ** (-0.5)
         joint_ref[:, qw + g * HD : qw + (g + 1) * HD] = turn_heads(turned, cosine, sine).astype(BF16)
     joint_ref[:, qw + HK * HD :] = dv_ref[...].astype(BF16)
+    block = HK * HD
+
+    @pl.loop(0, joint_ref.shape[1] // block)
+    def _(k):
+        lanes = pl.ds(pl.multiple_of(k * block, block), block)
+        grad_ref[:, lanes] = tn(first_ref[...], joint_ref[:, lanes]).astype(BF16)
 
 
 def attention_backward(operands):
@@ -241,8 +248,11 @@
     return pl.pallas_call(
         attention_backward_kernel,
         in_specs=vmem_specs(len(operands)),
-        out_specs=pl.BlockSpec(memory_space=pltpu.VMEM),
-        out_shape=struct((length, HQ * HD + 2 * kv), BF16),
+        out_specs=vmem_specs(2),
+        out_shape=[
+            struct((length, HQ * HD + 2 * kv), BF16),
+            struct((width, HQ * HD + 2 * kv), BF16),
+        ],
         scratch_shapes=[
             pltpu.VMEM((length, HQ * HD), BF16),
             pltpu.VMEM((length, kv), F32),
@@ -268,10 +278,10 @@
     def place(k, count):
         return lax.rem(here + (count - k), count) if turned else k
 
-    def both():
+    def both(low, high):
         return joined(
             [
-                w1_ref[:, place(k, lanes), 0].reshape(groups * double, span1)
+                w1_ref[low:high, place(k, lanes), 0].reshape((high - low) * double, span1)
                 for k in range(lanes)
             ]
         )
@@ -286,15 +296,15 @@
             ]
         )
 
-    def second():
+    def second(low=0, high=groups2):
         if not turned:
             return joined(
-                [w2_ref[k, 0, :, 0].reshape(groups2 * f_rows, span2) for k in range(lanes2)]
+                [w2_ref[k, 0, low:high, 0].reshape((high - low) * f_rows, span2) for k in range(lanes2)]
             )
         return jnp.concatenate(
             [
                 joined([w2_ref[k, 0, place(g, groups2), 0] for k in range(lanes2)])
-                for g in range(groups2)
+                for g in range(low, high)
             ],
             axis=0,
         )
@@ -312,12 +322,22 @@
 def hidden_backward(x, w1_ref, w2_ref, turned, br, act_ref, gt_ref, lanes):
     groups, f_cols, both, _, second = weights_of(w1_ref, w2_ref, turned)
     hidden = groups * f_cols
-    units = nn(both(), x)
-    act_grads = nn(second(), br)
-    for r in range(groups):
-        gate = units[2 * r * f_cols : (2 * r + 1) * f_cols]
-        up = units[(2 * r + 1) * f_cols : (2 * r + 2) * f_cols]
-        act_grad = act_grads[r * f_cols : (r + 1) * f_cols]
+    groups2 = w2_ref.shape[2]
+    parts = PARTS if groups % PARTS == 0 and groups2 % PARTS == 0 else 1
+    for part in range(parts):
+        low, high = part * groups // parts, (part + 1) * groups // parts
+        low2, high2 = part * groups2 // parts, (part + 1) * groups2 // parts
+        units = nn(both(low, high), x)
+        act_grads = nn(second(low2, high2), br)
+        hidden_part(low, high, f_cols, hidden, units, act_grads, act_ref, gt_ref, lanes)
+
+
+def hidden_part(low, high, f_cols, hidden, units, act_grads, act_ref, gt_ref, lanes):
+    for r in range(low, high):
+        at = r - low
+        gate = units[2 * at * f_cols : (2 * at + 1) * f_cols]
+        up = units[(2 * at + 1) * f_cols : (2 * at + 2) * f_cols]
+        act_grad = act_grads[at * f_cols : (at + 1) * f_cols]
         square = gate * gate
         bent = jnp.tanh(GELU_C * (gate + GELU_A * (square * gate)))
         lifted = 0.5 * (1.0 + bent)
@@ -530,10 +550,13 @@
 
 def open_kernel(reps, shards, pieces, extra, *refs):
     count = len(pieces)
-    sources, targets = refs[: count + 1 + extra], refs[count + 1 + extra : 2 * (count + 1 + extra)]
+    arrays = count + 1 + extra
+    sources, hop_ref = refs[:arrays], refs[arrays]
+    targets, from_below, from_above = refs[arrays + 1 : 2 * arrays + 1], refs[2 * arrays + 1], refs[2 * arrays + 2]
     local_sem, up_send, up_recv, down_send, down_recv, chip_send, chip_recv, core_send, core_recv = refs[
-        2 * (count + 1 + extra) :
+        2 * arrays + 3 : -2
     ]
+    hop_send, hop_recv = refs[-2:]
     rep, shard = lax.axis_index("rep"), lax.axis_index("shard")
     chips, core = reps // 2, rep % 2
     chip = rep // 2
@@ -591,6 +614,16 @@
             send_sem=down_send.at[k, step],
             recv_sem=down_recv.at[k, step],
             device_id={"shard": lax.rem(shard + shards - 1, shards)},
+            device_id_type=MESH,
+        )
+
+    def hop(to_above):
+        return pltpu.make_async_remote_copy(
+            src_ref=hop_ref,
+            dst_ref=from_below if to_above else from_above,
+            send_sem=hop_send.at[int(to_above)],
+            recv_sem=hop_recv.at[int(to_above)],
+            device_id={"shard": lax.rem(shard + (1 if to_above else shards - 1), shards)},
             device_id_type=MESH,
         )
 
@@ -647,6 +680,15 @@
         line_step(first, step)
         line_arrive(first, step)
     line_step(later, 0)
+
+    @pl.when(shard < shards - 1)
+    def _():
+        hop(True).start()
+
+    @pl.when(shard > 0)
+    def _():
+        hop(False).start()
+
     for copy in locals_:
         copy.wait()
 
@@ -694,20 +736,32 @@
     for step in range(shards - 1):
         line_sent(first + later, step)
 
-
-def open_gather(reps, shards, bands, small, lines):
+    @pl.when(shard < shards - 1)
+    def _():
+        hop(True).wait_send()
+        hop(False).wait_recv()
+
+    @pl.when(shard > 0)
+    def _():
+        hop(False).wait_send()
+        hop(True).wait_recv()
+
+
+def open_gather(reps, shards, bands, small, lines, hop):
     operands = [operand for _, operand in bands] + [small] + list(lines)
     dma = pltpu.SemaphoreType.DMA
     count, total, chips = len(bands), len(operands), reps // 2
+    operands.append(hop)
     span = small.shape[1]
     shapes = [struct((reps * operand.shape[0], shards * span), BF16) for _, operand in bands]
     shapes.append(struct((small.shape[0], shards * span), BF16))
     shapes += [struct((shards, *line.shape), BF16) for line in lines]
+    shapes += [struct(hop.shape, BF16)] * 2
     anywhere = pl.BlockSpec(memory_space=pl.ANY)
     return pl.pallas_call(
         functools.partial(open_kernel, reps, shards, [at for at, _ in bands], len(lines)),
-        in_specs=[anywhere] * total,
-        out_specs=[anywhere] * total,
+        in_specs=[anywhere] * (total + 1),
+        out_specs=[anywhere] * (total + 2),
         out_shape=shapes,
         scratch_shapes=[
             dma((total,)),
@@ -719,10 +773,22 @@
             dma((count, chips)),
             dma((count, chips)),
             dma((count, chips)),
+            dma((2,)),
+            dma((2,)),
         ],
         compiler_params=params(collective_id=4, has_side_effects=True),
         name="open_gather",
     )(*operands)
+
+
+def packed_rows(value):
+    half = value.shape[1] // 2
+    return jnp.concatenate([value[:, :half], value[:, half:]], axis=0).astype(BF16)
+
+
+def unpacked_rows(value):
+    value = value.astype(F32)
+    return jnp.concatenate([value[:8], value[8:]], axis=1)
 
 
 def left_parts_kernel(
@@ -739,10 +805,12 @@
     pieces.append(router_ref[...])
     pieces.append(gains_ref[...])
     for shard in range(shards):
-        for k, piece in enumerate(pieces):
-            z_ref[shard, :, k * wide : (k + 1) * wide] = padded(
-                piece[:, shard * rows : (shard + 1) * rows], wide
+        z_ref[shard] = packed_rows(
+            jnp.concatenate(
+                [padded(piece[:, shard * rows : (shard + 1) * rows], wide) for piece in pieces],
+                axis=1,
             )
+        )
     errors = (
         start_product(sq_ref[...], eq_ref[...]),
         start_product(sk_ref[...], ep_ref[0]),
@@ -759,7 +827,7 @@
         functools.partial(left_parts_kernel, shards, rows, wide),
         in_specs=vmem_specs(len(operands)),
         out_specs=vmem_specs(2),
-        out_shape=[struct((shards, 8, 6 * wide)), struct((8, 4 * wide))],
+        out_shape=[struct((shards, 16, 3 * wide), BF16), struct((8, 4 * wide))],
         compiler_params=params(),
         name="left_parts",
     )(*operands)
@@ -824,16 +892,15 @@
 def left_sync_kernel(reps, shards, wide, wide_out, piece, count, *refs):
     z_ref, own_ref = refs[:2]
     lin_refs, lout_refs = refs[2 : 2 + count], refs[2 + count : 2 + 2 * count]
-    left_ref, left_out_ref, totals_ref, squares_ref, leftz_ref = refs[2 + 2 * count : 7 + 2 * count]
-    (zbuf, parts, heard, total, grams, lanes_z, zs, zr, ps, pr, gs, gr, hs, hr, ls, lr) = refs[
-        7 + 2 * count :
-    ]
+    refs = refs[3 + 2 * count :]
+    left_ref, left_out_ref, totals_ref, squares_ref, leftz_ref = refs[:5]
+    (zbuf, parts, heard, total, grams, lanes_z, zs, zr, ps, pr, gs, gr, hs, hr, ls, lr) = refs[5:]
     rep, shard = lax.axis_index("rep"), lax.axis_index("shard")
     greet(reps, shards)
     send_all("shard", shards, lambda to: z_ref.at[to], lambda step: zbuf.at[step - 1], zs, zr)
-    front = z_ref[shard]
+    front = unpacked_rows(z_ref[shard])
     for step in range(shards - 1):
-        front = front + zbuf[step]
+        front = front + unpacked_rows(zbuf[step])
     ins = [ref[e, a] for a in range(2) for ref in lin_refs for e in range(ref.shape[0])]
     outs = [ref[e] for ref in lout_refs for e in range(ref.shape[0])]
     line = jnp.concatenate(
@@ -841,14 +908,14 @@
     )
     line = padded(line, reps * piece)
     for k in range(reps):
-        parts[k] = line[:, k * piece : (k + 1) * piece]
+        parts[k] = packed_rows(line[:, k * piece : (k + 1) * piece])
     send_all("rep", reps, lambda to: parts.at[to], lambda step: heard.at[step - 1], ps, pr)
-    mine = parts[rep]
+    mine = parts[rep].astype(F32)
     for step in range(reps - 1):
-        mine = mine + heard[step]
-    total[rep] = mine
+        mine = mine + heard[step].astype(F32)
+    total[rep] = mine.astype(BF16)
     send_all("rep", reps, lambda to: total.at[rep], lambda step: total.at[rep], gs, gr)
-    line = jnp.concatenate([total[k] for k in range(reps)], axis=1)
+    line = jnp.concatenate([unpacked_rows(total[k]) for k in range(reps)], axis=1)
     inner = len(ins)
     matrices = [line[:, k * wide : (k + 1) * wide] for k in range(4)]
     matrices += [line[:, (6 + k) * wide : (7 + k) * wide] for k in range(inner)]
@@ -913,14 +980,14 @@
         leftz_ref[k] = nn(solve[:32, :32], lanes_z[k], HIGHEST)
 
 
-def left_sync(reps, shards, z_part, own, lins, louts):
+def left_sync(reps, shards, z_part, own, lins, louts, late):
     wide, wide_out = lins[0].shape[3], louts[0].shape[2]
     inner, outer = 2 * sum(x.shape[0] for x in lins), sum(x.shape[0] for x in louts)
-    piece = up_to(-(-((6 + inner) * wide + outer * wide_out) // reps), 128)
+    piece = up_to(-(-((6 + inner) * wide + outer * wide_out) // reps), 256)
     matrices = 4 + inner
     size, size_out = up_to(8 * matrices, 128), up_to(8 * outer, 128)
     dma = pltpu.SemaphoreType.DMA
-    operands = [z_part, own, *lins, *louts]
+    operands = [z_part, own, *lins, *louts, late]
     return pl.pallas_call(
         functools.partial(left_sync_kernel, reps, shards, wide, wide_out, piece, len(lins)),
         in_specs=vmem_specs(len(operands)),
@@ -933,10 +1000,10 @@
             struct((shards, 32, wide)),
         ],
         scratch_shapes=[
-            pltpu.VMEM((shards - 1, 8, 6 * wide), F32),
-            pltpu.VMEM((reps, 8, piece), F32),
-            pltpu.VMEM((reps - 1, 8, piece), F32),
-            pltpu.VMEM((reps, 8, piece), F32),
+            pltpu.VMEM((shards - 1, 16, 3 * wide), BF16),
+            pltpu.VMEM((reps, 16, piece // 2), BF16),
+            pltpu.VMEM((reps - 1, 16, piece // 2), BF16),
+            pltpu.VMEM((reps, 16, piece // 2), BF16),
             pltpu.VMEM((shards, 8, size + size_out + 128), F32),
             pltpu.VMEM((shards, 32, wide), F32),
             dma((shards - 1,)),
@@ -1322,11 +1389,12 @@
             [(0, query_t), (0, pair_t[0]), (0, pair_t[1]), (0, output_t)],
             small,
             packs[:1],
+            cot_t,
         )
         query_full, key_full, value_full, output_full, small_full = opened[:5]
         height = packs[0].shape[0]
         near = z_slots(packs[1])
-        first_line = opened[5]
+        first_line, below_u, above_u = opened[5:]
     else:
         packed = jnp.concatenate(
             [query_t, pair_t.reshape(2 * p_cols, own_rows), output_t, small], axis=0
@@ -1479,9 +1547,9 @@
         own(0)
         state["x"], state["u"] = held = not_before((state["x"], state["u"]))
         ups, downs = [held], [held]
-        up, down = pass_on(held, held)
-        ups.append(up)
-        downs.append(down)
+        up, down = pass_on(held[:1], held[:1])
+        ups.append((up[0], below_u))
+        downs.append((down[0], above_u))
         far_weights()
         own(1)
         ups[1], downs[1] = not_before((ups[1], downs[1]))
@@ -1542,12 +1610,14 @@
     group_output = lax.psum_scatter(
         grad_output.astype(bf16), "shard", scatter_dimension=0, tiled=True
     )
-    joint_grad = attention_backward(
-        (middle_low, output_full, query_rot, key_rot, values, cosine, sine, mask, late)
-    )
-    grad_joint = jnp.einsum("td,tq->dq", first_low, joint_grad, preferred_element_type=jnp.float32)
+    joint_grad, grad_joint = attention_backward(
+        (
+            middle_low, output_full, query_rot, key_rot, values, cosine, sine, mask, first_low,
+            late,
+        )
+    )
     group_joint = lax.psum_scatter(
-        grad_joint.astype(bf16), "shard", scatter_dimension=0, tiled=True
+        grad_joint, "shard", scatter_dimension=0, tiled=True
     )
     first_grad = (
         nn(joint_grad[:, :QW], query_full)
@@ -1581,7 +1651,7 @@
         ),
     )
     left_flat, left_out_flat, totals, total_squares, left_lines = left_sync(
-        replicas, shard_count, z_part, own_left, lins, louts
+        replicas, shard_count, z_part, own_left, lins, louts, group_joint[:16, :128]
     )
     wide, wide_out = left_flat.shape[1], left_out_flat.shape[1]
     lefts = left_flat.reshape(-1, 8, wide)
@@ -1671,7 +1741,7 @@
             right, column_index * own_columns, own_columns, axis=right.ndim - 1
         )
         direction = (
-            jnp.einsum("...km,...kn->...mn", left, own_right, precision=HIGHEST)
+            jnp.einsum("...km,...kn->...mn", left, own_right, precision=lax.Precision.HIGH)
             / scale_norm[..., None, None]
         )
         new_master, new_moment = advance(

time: 912 us -> 876 us (0.961)
  Pallas kernels: 604 us -> 582 us
  matrix products: 48.3 us -> 34.6 us
  starting transfers between devices: 52.5 us -> 42.8 us
    all_gather x4, waiting for transfers between devices: 15 us -> 34.8 us  [gathered(): part = lax.all_gather(line, 'rep')]
    ppermute x6 -> x5, waiting for transfers between devices: 21.7 us -> 2.85 us  [pass_on(): lax.ppermute(down, 'shard', back)]
    pallas_call x1, Pallas kernels: 46.2 us -> 28.2 us  [left_sync(): pl.pallas_call(functools.partial(left_sync_kernel, reps, shards, wide, wi...]
    dot_general x6 -> x5, matrix products: 25.2 us -> 13.3 us  [per_device(): jnp.einsum('...km,...kn->...mn', left, own_right, precision=lax.Precision...]
    ppermute x6 -> x5, starting transfers between devices: 34.8 us -> 26.7 us  [pass_on(): lax.ppermute(up, 'shard', forth)]
  transfers between devices with their start and end apart: 25 -> 23, of which waited for: 5 -> 7; matrix products, arithmetic and copies ran while one was open for 16% -> 14% of each run, Pallas kernels for 54% -> 50%
where the time goes in v3:
time: 876 us; the launch traced here: 866 us
  Pallas kernels  582 us (66%)
  waiting for transfers between devices  68.5 us (8%)
  other arithmetic  61.8 us (7%)
  local copies, waits for them, and re-layouts  58.3 us (7%)
  starting transfers between devices  42.8 us (5%)
  matrix products  34.6 us (4%)
  between operations  17.6 us (2%)
    pallas_call x7, Pallas kernels, rest_experts(): pl.pallas_call(functools.partial(rest_kernel, first_expert, trees, last,...  182 us
    pallas_call x4, Pallas kernels, own_experts(): pl.pallas_call(functools.partial(own_kernel, first_expert, turned), grid=...  115 us
    pallas_call x1, Pallas kernels, open_gather(): pl.pallas_call(functools.partial(open_kernel, reps, shards, [at for at, _...  98.2 us
    all_gather x4, waiting for transfers between devices, gathered(): part = lax.all_gather(line, 'rep')  34.8 us
    pallas_call x1, Pallas kernels, attention_backward(): pl.pallas_call(attention_backward_kernel, in_specs=vmem_specs(len(operand...  30.5 us
    ppermute x6, waiting for transfers between devices, z_slots(): lax.ppermute(block, 'shard', [(i, (i + step) % size) for i in range(size)])  30.2 us
    pallas_call x1, Pallas kernels, left_sync(): pl.pallas_call(functools.partial(left_sync_kernel, reps, shards, wide, wi...  28.2 us
    ppermute x5, starting transfers between devices, pass_on(): lax.ppermute(up, 'shard', forth)  26.7 us
  transfers between devices with their start and end apart: 23, of which 7 were waited for; matrix products, arithmetic and copies ran while one was open for 14% of the time, Pallas kernels for 50%

profile of v3, /device:TPU:0, one launch (start us, length us, event | category | flops | bytes accessed | tf_op | source)
XLA Modules:
  0.0 866.0 jit_solution(8571966881712841407)
XLA Ops:
  18.7 98.2 %open_gather.1 = (bf16[1536,1536]{1,0:T(8,128)(2,1)}, bf16[256,1536]{1,0:T(8,128)(2,1)}, bf16[256,1536]{1,0:T(8,128)(2,1)}, bf16[1536,1536]{1,0:T(8,128)(2,1)}, ...) custom-call(bf16[192,384]{1,0:T(8,128)(2,1)} %get-tuple-element.474., ...), custom_call_target="tpu_custom_call" | custom-call | tf_op jit(solution)/shard_map/open_gather/pallas_call | solution.py:761
  125.5 25.5 %attention_forward.1 = (bf16[512,1536]{1,0:T(8,128)(2,1)}, bf16[512,256]{1,0:T(8,128)(2,1)}, bf16[512,256]{1,0:T(8,128)(2,1)}, bf16[512,1536]{1,0:T(8,128)(2,1)}, f32[512,1536]{1,0:T(8,128)}) custom-call(bf16[512,1536]{1,0:T(8,128)(2,1)} %fusion.2.first_ref, bf16[1536,1536]{1,0:T(8,128)(2,1)} %get-tuple-element.137.query_ref, ...), custom_call_target="tpu_custom_call" | custom-call | flops 7247757312 | bytes 20447232 | tf_op jit(solution)/shard_map/attention_forward/pallas_call | solution.py:187
  177.8 16.1 %all-gather.9.cloned.1.call-done = bf16[32,576,384]{2,1,0:T(8,128)(2,1)} async-done(((bf16[4,576,384]{2,1,0:T(8,128)(2,1)}), bf16[32,576,384]{2,1,0:T(8,128)(2,1)}) %all-gather.9.cloned.1.call-update) | async-done | bytes 14155792 | tf_op jit(solution)/shard_map/all_gather | solution.py:1460
  194.0 28.6 %own_experts.4 = (f32[2,2,384,768]{3,2,1,0:T(8,128)}, f32[2,192,1536]{2,1,0:T(8,128)}, f32[512,1536]{1,0:T(8,128)}, f32[512,1536]{1,0:T(8,128)}, f32[2,512,1]{2,1,0:T(8,128)}) custom-call(bf16[1552,512]{1,0:T(8,128)(2,1)} %copy.268.x_ref, bf16[1536,512]{1,0:T(8,128)(2,1)} %bitcast.223, bf16[512,1536]{1,0:T(8,128)(2,1)} %up_ref.7, ...), custom_call_target="tpu_custom_call" | custom-call | flops 33822867456 | bytes 37748736 | tf_op jit(solution)/shard_map/own_experts/pallas_call | solution.py:475
  223.8 27.7 %collective-permute-done.5 = bf16[1152,384]{1,0:T(8,128)(2,1)} collective-permute-done((bf16[1152,384]{1,0:T(8,128)(2,1)S(1)}, bf16[1152,384]{1,0:T(8,128)(2,1)}, u32[]{:S(2)}, u32[]{:S(2)}) %collective-permute-start.5) | collective-permute-done | bytes 884768 | tf_op jit(solution)/shard_map/ppermute | solution.py:76
  266.6 8.7 %all-gather.11.cloned.1.call-done = bf16[32,576,384]{2,1,0:T(8,128)(2,1)} async-done(((bf16[4,576,384]{2,1,0:T(8,128)(2,1)}), bf16[32,576,384]{2,1,0:T(8,128)(2,1)}) %all-gather.11.cloned.1.call-update) | async-done | bytes 14155792 | tf_op jit(solution)/shard_map/all_gather | solution.py:1460
  275.3 28.6 %own_experts.5 = (f32[2,2,384,768]{3,2,1,0:T(8,128)}, f32[2,192,1536]{2,1,0:T(8,128)}, f32[512,1536]{1,0:T(8,128)}, f32[512,1536]{1,0:T(8,128)}, f32[2,512,1]{2,1,0:T(8,128)}) custom-call(bf16[1552,512]{1,0:T(8,128)(2,1)} %copy.270.x_ref, bf16[1536,512]{1,0:T(8,128)(2,1)} %bitcast.224, bf16[512,1536]{1,0:T(8,128)(2,1)} %up_ref.7, ...), custom_call_target="tpu_custom_call" | custom-call | flops 33822867456 | bytes 37748736 | tf_op jit(solution)/shard_map/own_experts/pallas_call | solution.py:475
  328.4 17.0 %rest_experts.7 = (f32[2,2,384,768]{3,2,1,0:T(8,128)}, f32[2,192,1536]{2,1,0:T(8,128)}) custom-call(bf16[8,4,3,192,384]{4,3,2,1,0:T(8,128)(2,1)} %bitcast.260, bf16[4,2,4,3,192,384]{5,4,3,2,1,0:T(8,128)(2,1)} %bitcast.261, f32[2,8,8,768]{3,2,1,0:T(8,128)} %bitcast.287, f32[8,8,1536]{2,1,0:T(8,128)} %bitcast.294, ...), custom_call_target="tpu_custom_call", output_to_operand_aliasing={{0}: (4, {}), {1}: (5, {})} | custom-call | flops 16911433728 | bytes 28311552 | tf_op jit(solution)/shard_map/rest_experts/pallas_call | solution.py:523
  346.7 9.8 %all-gather.13.cloned.1.call-done = bf16[32,576,384]{2,1,0:T(8,128)(2,1)} async-done(((bf16[4,576,384]{2,1,0:T(8,128)(2,1)}), bf16[32,576,384]{2,1,0:T(8,128)(2,1)}) %all-gather.13.cloned.1.call-update) | async-done | bytes 14155792 | tf_op jit(solution)/shard_map/all_gather | solution.py:1460
  356.5 28.6 %own_experts.6 = (f32[2,2,384,768]{3,2,1,0:T(8,128)}, f32[2,192,1536]{2,1,0:T(8,128)}, f32[512,1536]{1,0:T(8,128)}, f32[512,1536]{1,0:T(8,128)}, f32[2,512,1]{2,1,0:T(8,128)}) custom-call(bf16[1552,512]{1,0:T(8,128)(2,1)} %copy.270.x_ref, bf16[1536,512]{1,0:T(8,128)(2,1)} %bitcast.225, bf16[512,1536]{1,0:T(8,128)(2,1)} %up_ref.7, ...), custom_call_target="tpu_custom_call" | custom-call | flops 33822867456 | bytes 37748736 | tf_op jit(solution)/shard_map/own_experts/pallas_call | solution.py:475
  387.7 17.3 %rest_experts.8 = (f32[2,2,384,768]{3,2,1,0:T(8,128)}, f32[2,192,1536]{2,1,0:T(8,128)}) custom-call(bf16[8,4,3,192,384]{4,3,2,1,0:T(8,128)(2,1)} %bitcast.266, bf16[4,2,4,3,192,384]{5,4,3,2,1,0:T(8,128)(2,1)} %bitcast.267, f32[2,8,8,768]{3,2,1,0:T(8,128)} %bitcast.288, f32[8,8,1536]{2,1,0:T(8,128)} %bitcast.295, ...), custom_call_target="tpu_custom_call", output_to_operand_aliasing={{0}: (4, {}), {1}: (5, {})} | custom-call | flops 16911433728 | bytes 28311552 | tf_op jit(solution)/shard_map/rest_experts/pallas_call | solution.py:523
  419.1 17.1 %rest_experts.9 = (f32[2,2,384,768]{3,2,1,0:T(8,128)}, f32[2,192,1536]{2,1,0:T(8,128)}) custom-call(bf16[8,4,3,192,384]{4,3,2,1,0:T(8,128)(2,1)} %bitcast.272, bf16[4,2,4,3,192,384]{5,4,3,2,1,0:T(8,128)(2,1)} %bitcast.273, f32[2,8,8,768]{3,2,1,0:T(8,128)} %bitcast.289, f32[8,8,1536]{2,1,0:T(8,128)} %bitcast.296, ...), custom_call_target="tpu_custom_call", output_to_operand_aliasing={{0}: (4, {}), {1}: (5, {})} | custom-call | flops 16911433728 | bytes 28311552 | tf_op jit(solution)/shard_map/rest_experts/pallas_call | solution.py:523
  437.7 29.4 %own_experts.7 = (f32[2,2,384,768]{3,2,1,0:T(8,128)}, f32[2,192,1536]{2,1,0:T(8,128)}, f32[512,1536]{1,0:T(8,128)}, f32[512,1536]{1,0:T(8,128)}, f32[2,512,1]{2,1,0:T(8,128)}) custom-call(bf16[1552,512]{1,0:T(8,128)(2,1)} %copy.270.x_ref, bf16[1536,512]{1,0:T(8,128)(2,1)} %bitcast.226, bf16[512,1536]{1,0:T(8,128)(2,1)} %up_ref.7, ...), custom_call_target="tpu_custom_call" | custom-call | flops 33822867456 | bytes 37748736 | tf_op jit(solution)/shard_map/own_experts/pallas_call | solution.py:475
  485.6 30.5 %attention_backward.1 = (bf16[512,2048]{1,0:T(8,128)(2,1)}, bf16[1536,2048]{1,0:T(8,128)(2,1)}) custom-call(bf16[512,1536]{1,0:T(8,128)(2,1)} %fusion.78.middle_ref, bf16[1536,1536]{1,0:T(8,128)(2,1)} %get-tuple-element.140.output_ref, bf16[512,1536]{1,0:T(8,128)(2,1)} %get-tuple-element.186.qrot_ref, bf16[512,256]{1,0:T(8,128)(2,1)} %get-tuple-element.187.krot_ref, ...), custom_call_target="tpu_custom_call" | custom-call | flops 9663676416 | bytes 786432 | tf_op jit(solution)/shard_map/attention_backward/pallas_call | solution.py:248
  548.7 40.5 %rest_experts.10 = (f32[2,2,384,768]{3,2,1,0:T(8,128)}, f32[2,192,1536]{2,1,0:T(8,128)}, f32[2,2,8,384]{3,2,1,0:T(8,128)}, f32[2,8,256]{2,1,0:T(8,128)}) custom-call(bf16[8,4,3,192,384]{4,3,2,1,0:T(8,128)(2,1)} %bitcast.278, bf16[4,2,4,3,192,384]{5,4,3,2,1,0:T(8,128)(2,1)} %bitcast.279, ...), custom_call_target="tpu_custom_call", output_to_operand_aliasing={{0}: (4, {}), {1}: (5, {})} | custom-call | flops 50734301184 | bytes 28311552 | tf_op jit(solution)/shard_map/rest_experts/pallas_call | solution.py:523
  590.5 29.4 %rest_experts.11 = (f32[2,2,384,768]{3,2,1,0:T(8,128)}, f32[2,192,1536]{2,1,0:T(8,128)}, f32[2,2,8,384]{3,2,1,0:T(8,128)}, f32[2,8,256]{2,1,0:T(8,128)}) custom-call(bf16[8,4,3,192,384]{4,3,2,1,0:T(8,128)(2,1)} %bitcast.274, bf16[4,2,4,3,192,384]{5,4,3,2,1,0:T(8,128)(2,1)} %bitcast.275, ...), custom_call_target="tpu_custom_call", output_to_operand_aliasing={{0}: (4, {}), {1}: (5, {})} | custom-call | flops 33822867456 | bytes 28311552 | tf_op jit(solution)/shard_map/rest_experts/pallas_call | solution.py:523
  621.8 9.5 %left_parts.1 = (bf16[4,16,1152]{2,1,0:T(8,128)(2,1)}, f32[8,1536]{1,0:T(8,128)}) custom-call(bf16[512,1536]{1,0:T(8,128)(2,1)} %fusion.2.first_ref, bf16[512,2048]{1,0:T(8,128)(2,1)} %get-tuple-element.193.joint_ref.rest_6_, bf16[512,1536]{1,0:T(8,128)(2,1)} %get-tuple-element.194.mixed_ref, bf16[512,1536]{1,0:T(8,128)(2,1)} %fusion.78.middle_ref, ...), custom_call_target="tpu_custom_call" | custom-call | tf_op jit(solution)/shard_map/left_parts/pallas_call | solution.py:826
  631.3 30.5 %rest_experts.12 = (f32[2,2,384,768]{3,2,1,0:T(8,128)}, f32[2,192,1536]{2,1,0:T(8,128)}, f32[2,2,8,384]{3,2,1,0:T(8,128)}, f32[2,8,256]{2,1,0:T(8,128)}) custom-call(bf16[8,4,3,192,384]{4,3,2,1,0:T(8,128)(2,1)} %bitcast.262, bf16[4,2,4,3,192,384]{5,4,3,2,1,0:T(8,128)(2,1)} %bitcast.263, ...), custom_call_target="tpu_custom_call", output_to_operand_aliasing={{0}: (4, {}), {1}: (5, {})} | custom-call | flops 33822867456 | bytes 28311552 | tf_op jit(solution)/shard_map/rest_experts/pallas_call | solution.py:523
  663.1 10.3 %fusion.6 = (bf16[512,1536]{1,0:T(8,128)(2,1)}, bf16[512,1536]{1,0:T(8,128)(2,1)}) fusion(bf16[512,1536]{1,0:T(8,128)(2,1)} %tokens_ref.1, f32[512,1536]{1,0:T(8,128)} %get-tuple-element.462, f32[512]{0:T(512)S(1)} %multiply_multiply_fusion, f32[1536]{0:T(1024)S(1)} %copy-done.41, f32[512]{0:T(512)S(1)} %copy-done.51, f32[512,1536]{1,0:T(8,128)S(1)} %copy-done.2, ...), kind=kLoop, calls=%fused_computation.17 | loop fusion | flops 15728640 | bytes 28332032 | tf_op jit(solution)/shard_map/convert_element_type | solution.py:1629
  673.5 29.8 %rest_experts.13 = (f32[2,2,384,768]{3,2,1,0:T(8,128)}, f32[2,192,1536]{2,1,0:T(8,128)}, f32[2,2,8,384]{3,2,1,0:T(8,128)}, f32[2,8,256]{2,1,0:T(8,128)}) custom-call(bf16[8,4,3,192,384]{4,3,2,1,0:T(8,128)(2,1)} %bitcast.268, bf16[4,2,4,3,192,384]{5,4,3,2,1,0:T(8,128)(2,1)} %bitcast.269, ...), custom_call_target="tpu_custom_call", output_to_operand_aliasing={{0}: (4, {}), {1}: (5, {})} | custom-call | flops 33822867456 | bytes 28311552 | tf_op jit(solution)/shard_map/rest_experts/pallas_call | solution.py:523
  704.6 28.2 %left_sync.1 = (f32[160,384]{1,0:T(8,128)}, f32[64,256]{1,0:T(8,128)}, f32[2,8,384]{2,1,0:T(8,128)}, f32[8,128]{1,0:T(8,128)}, f32[4,32,384]{2,1,0:T(8,128)}) custom-call(bf16[4,16,1152]{2,1,0:T(8,128)(2,1)} %get-tuple-element.195.refs_0_, f32[8,1536]{1,0:T(8,128)} %get-tuple-element.196.refs_1_, f32[2,2,8,384]{3,2,1,0:T(8,128)} %get-tuple-element.203.refs_2_, ...), custom_call_target="tpu_custom_call" | custom-call | tf_op jit(solution)/shard_map/left_sync/pallas_call | solution.py:991
  749.1 9.0 %right_attention.1.refs_4_ = f32[8,3584]{1,0:T(8,128)} custom-call(f32[32,384]{1,0:T(8,128)} %slice.254.left_ref, f32[4,32,384]{2,1,0:T(8,128)} %get-tuple-element.221.leftz_ref, bf16[512,1536]{1,0:T(8,128)(2,1)} %fusion.2.first_ref, bf16[512,2048]{1,0:T(8,128)(2,1)} %get-tuple-element.193.joint_ref.rest_6_, bf16[512,1536]{1,0:T(8,128)(2,1)} %get-tuple-element.194.mixed_ref, ...), custom_call_target="tpu_custom_call" | custom-call | tf_op jit(solution)/shard_map/right_attention/pallas_call | solution.py:1091
  762.5 24.5 %right_sync.1.right_ref = f32[8,28672]{1,0:T(8,128)} custom-call(f32[2,8,3072]{2,1,0:T(8,128)} %right_experts.4.refs_0_, f32[2,8,3072]{2,1,0:T(8,128)} %right_experts.5.refs_1_, f32[2,8,3072]{2,1,0:T(8,128)} %right_experts.6.refs_2_, f32[2,8,3072]{2,1,0:T(8,128)} %right_experts.7.refs_3_, f32[8,3584]{1,0:T(8,128)} %right_attention.1.refs_4_), custom_call_target="tpu_custom_call" | custom-call | tf_op jit(solution)/shard_map/right_sync/pallas_call | solution.py:1137
  825.6 11.2 %squares_sync.1 = f32[8,128]{1,0:T(8,128)} custom-call(f32[8,128]{1,0:T(8,128)} %get-tuple-element.235.refs_0_, f32[8,128]{1,0:T(8,128)} %get-tuple-element.236.refs_1_, f32[8,128]{1,0:T(8,128)} %get-tuple-element.237.refs_2_, f32[8,128]{1,0:T(8,128)} %get-tuple-element.238.refs_3_, f32[8,128]{1,0:T(8,128)} %get-tuple-element.239.refs_4_), custom_call_target="tpu_custom_call" | custom-call | tf_op jit(solution)/shard_map/squares_sync/pallas_call | solution.py:1288
  (329 shorter events, 242.6 us)
Async XLA Ops:
  7.3 186.7 %all-gather.9.cloned.1.call-start = ((), (), s32[]{:S(2)}) async-start(), calls=%async_computation.4 | async-start | bytes 15925248 | tf_op jit(solution)/shard_map/all_gather | solution.py:1460
  9.7 6.8 collective-permute-start
  17.8 99.2 %copy-start.54 = (s32[1,512]{1,0:T(1,128)S(1)}, s32[1,512]{1,0:T(1,128)}, u32[]{:S(2)}) copy-start(s32[1,512]{1,0:T(1,128)} %param.33) | copy-start | bytes 6148
  116.9 158.3 %all-gather.11.cloned.1.call-start = ((), (), s32[]{:S(2)}) async-start(), calls=%async_computation.5 | async-start | bytes 15925248 | tf_op jit(solution)/shard_map/all_gather | solution.py:1460
  120.8 37.4 %collective-permute-start.3 = (bf16[576,384]{1,0:T(8,128)(2,1)S(1)}, bf16[576,384]{1,0:T(8,128)(2,1)}, u32[]{:S(2)}, u32[]{:S(2)}) collective-permute-start(bf16[576,384]{1,0:T(8,128)(2,1)S(1)} %pad_maximum_fusion.4), channel_id=1, source_target_pairs={{0,3},{1,0},{2,1},{3,2},{4,7},{5,4},{6,5},{7,6},{8,11},{9,8},{10,9... | collective-permute-start | bytes 1327112 | tf_op jit(solution)/shard_map/ppermute | solution.py:76
  123.2 37.6 %collective-permute-start.2 = (bf16[576,384]{1,0:T(8,128)(2,1)S(1)}, bf16[576,384]{1,0:T(8,128)(2,1)}, u32[]{:S(2)}, u32[]{:S(2)}) collective-permute-start(bf16[576,384]{1,0:T(8,128)(2,1)S(1)} %pad_maximum_fusion.4), channel_id=1, source_target_pairs={{0,2},{1,3},{2,0},{3,1},{4,6},{5,7},{6,4},{7,5},{8,10},{9,11},{10,... | collective-permute-start | bytes 1327112 | tf_op jit(solution)/shard_map/ppermute | solution.py:76
  123.2 37.6 %collective-permute-start.1 = (bf16[576,384]{1,0:T(8,128)(2,1)S(1)}, bf16[576,384]{1,0:T(8,128)(2,1)}, u32[]{:S(2)}, u32[]{:S(2)}) collective-permute-start(bf16[576,384]{1,0:T(8,128)(2,1)S(1)} %pad_maximum_fusion.4), channel_id=1, source_target_pairs={{0,1},{1,2},{2,3},{3,0},{4,5},{5,6},{6,7},{7,4},{8,9},{9,10},{10,1... | collective-permute-start | bytes 1327112 | tf_op jit(solution)/shard_map/ppermute | solution.py:76
  163.6 193.0 %all-gather.13.cloned.1.call-start = ((), (), s32[]{:S(2)}) async-start(), calls=%async_computation.6 | async-start | bytes 15925248 | tf_op jit(solution)/shard_map/all_gather | solution.py:1460
  171.6 52.2 %collective-permute-start.6 = (bf16[1152,384]{1,0:T(8,128)(2,1)S(1)}, bf16[1152,384]{1,0:T(8,128)(2,1)S(1)}, u32[]{:S(2)}, u32[]{:S(2)}) collective-permute-start(bf16[1152,384]{1,0:T(8,128)(2,1)S(1)} %copy-done.21), channel_id=1, source_target_pairs={{0,3},{1,0},{2,1},{3,2},{4,7},{5,4},{6,5},{7,6},{8,11},{9,8},{10,9... | collective-permute-start | bytes 2654216 | tf_op jit(solution)/shard_map/ppermute | solution.py:76
  172.4 79.1 %collective-permute-start.5 = (bf16[1152,384]{1,0:T(8,128)(2,1)S(1)}, bf16[1152,384]{1,0:T(8,128)(2,1)}, u32[]{:S(2)}, u32[]{:S(2)}) collective-permute-start(bf16[1152,384]{1,0:T(8,128)(2,1)S(1)} %copy-done.21), channel_id=1, source_target_pairs={{0,2},{1,3},{2,0},{3,1},{4,6},{5,7},{6,4},{7,5},{8,10},{9,11},{10,... | collective-permute-start | bytes 2654216 | tf_op jit(solution)/shard_map/ppermute | solution.py:76
  175.1 76.4 %collective-permute-start.4 = (bf16[1152,384]{1,0:T(8,128)(2,1)S(1)}, bf16[1152,384]{1,0:T(8,128)(2,1)}, u32[]{:S(2)}, u32[]{:S(2)}) collective-permute-start(bf16[1152,384]{1,0:T(8,128)(2,1)S(1)} %copy-done.21), channel_id=1, source_target_pairs={{0,1},{1,2},{2,3},{3,0},{4,5},{5,6},{6,7},{7,4},{8,9},{9,10},{10,1... | collective-permute-start | bytes 2654216 | tf_op jit(solution)/shard_map/ppermute | solution.py:76
  255.4 182.3 %all-gather.15.cloned.1.call-start = ((), (), s32[]{:S(2)}) async-start(), calls=%async_computation.7 | async-start | bytes 15925248 | tf_op jit(solution)/shard_map/all_gather | solution.py:1460
  256.0 447.3 %reduce-scatter.3.cloned.1.call-start = ((), (), s32[]{:S(2)}) async-start(), calls=%async_computation.2 | async-start | bytes 7864320 | tf_op jit(solution)/shard_map/reduce_scatter | solution.py:1619
  258.3 48.2 %collective-permute-start.8 = (bf16[1552,512]{1,0:T(8,128)(2,1)}, bf16[1552,512]{1,0:T(8,128)(2,1)S(1)}, u32[]{:S(2)}, u32[]{:S(2)}) collective-permute-start(bf16[1552,512]{1,0:T(8,128)(2,1)} %copy.270.x_ref), channel_id=1, source_target_pairs={{1,0},{2,1},{3,2},{5,4},{6,5},{7,6},{9,8},{10,9},{11,10},{13,12},{... | collective-permute-start | bytes 4767752 | tf_op jit(solution)/shard_map/ppermute | solution.py:1538
  259.6 46.9 %collective-permute-start.7 = (bf16[1552,512]{1,0:T(8,128)(2,1)}, bf16[1552,512]{1,0:T(8,128)(2,1)}, u32[]{:S(2)}, u32[]{:S(2)}) collective-permute-start(bf16[1552,512]{1,0:T(8,128)(2,1)} %copy.270.x_ref), channel_id=1, source_target_pairs={{0,1},{1,2},{2,3},{4,5},{5,6},{6,7},{8,9},{9,10},{10,11},{12,13},{... | collective-permute-start | bytes 4767752 | tf_op jit(solution)/shard_map/ppermute | solution.py:1537
  311.3 95.0 %collective-permute-start.10 = (bf16[1536,512]{0,1:T(8,128)(2,1)}, bf16[1536,512]{0,1:T(8,128)(2,1)}, u32[]{:S(2)}, u32[]{:S(2)}) collective-permute-start(bf16[1536,512]{0,1:T(8,128)(2,1)} %copy.274), channel_id=1, source_target_pairs={{0,1},{1,2},{2,3},{4,5},{5,6},{6,7},{8,9},{9,10},{10,11},{12,13},{... | collective-permute-start | bytes 4718600 | tf_op jit(solution)/shard_map/ppermute | solution.py:1537
  315.8 90.4 %collective-permute-start.12 = (bf16[1536,512]{0,1:T(8,128)(2,1)}, bf16[1536,512]{0,1:T(8,128)(2,1)}, u32[]{:S(2)}, u32[]{:S(2)}) collective-permute-start(bf16[1536,512]{0,1:T(8,128)(2,1)} %copy.275), channel_id=1, source_target_pairs={{1,0},{2,1},{3,2},{5,4},{6,5},{7,6},{9,8},{10,9},{11,10},{13,12},{... | collective-permute-start | bytes 4718600 | tf_op jit(solution)/shard_map/ppermute | solution.py:1538
  317.1 89.1 %collective-permute-start.9 = (bf16[1552,512]{1,0:T(8,128)(2,1)}, bf16[1552,512]{1,0:T(8,128)(2,1)}, u32[]{:S(2)}, u32[]{:S(2)}) collective-permute-start(bf16[1552,512]{1,0:T(8,128)(2,1)} %collective-permute-done.7), channel_id=1, source_target_pairs={{0,1},{1,2},{2,3},{4,5},{5,6},{6,7},{8,9},{9,10},{10,11},{12,13},{... | collective-permute-start | bytes 4767752 | tf_op jit(solution)/shard_map/ppermute | solution.py:1537
  322.8 83.4 %collective-permute-start.11 = (bf16[1552,512]{1,0:T(8,128)(2,1)S(1)}, bf16[1552,512]{1,0:T(8,128)(2,1)}, u32[]{:S(2)}, u32[]{:S(2)}) collective-permute-start(bf16[1552,512]{1,0:T(8,128)(2,1)S(1)} %collective-permute-done.8), channel_id=1, source_target_pairs={{1,0},{2,1},{3,2},{5,4},{6,5},{7,6},{9,8},{10,9},{11,10},{13,12},{... | collective-permute-start | bytes 4767752 | tf_op jit(solution)/shard_map/ppermute | solution.py:1538
  406.3 77.9 %collective-permute-start.14 = (bf16[1536,512]{0,1:T(8,128)(2,1)}, bf16[1536,512]{0,1:T(8,128)(2,1)}, u32[]{:S(2)}, u32[]{:S(2)}) collective-permute-start(bf16[1536,512]{0,1:T(8,128)(2,1)} %collective-permute-done.10), channel_id=1, source_target_pairs={{0,1},{1,2},{2,3},{4,5},{5,6},{6,7},{8,9},{9,10},{10,11},{12,13},{... | collective-permute-start | bytes 4718600 | tf_op jit(solution)/shard_map/ppermute | solution.py:1537
  410.8 73.4 %collective-permute-start.16 = (bf16[1536,512]{0,1:T(8,128)(2,1)}, bf16[1536,512]{0,1:T(8,128)(2,1)}, u32[]{:S(2)}, u32[]{:S(2)}) collective-permute-start(bf16[1536,512]{0,1:T(8,128)(2,1)} %collective-permute-done.12), channel_id=1, source_target_pairs={{1,0},{2,1},{3,2},{5,4},{6,5},{7,6},{9,8},{10,9},{11,10},{13,12},{... | collective-permute-start | bytes 4718600 | tf_op jit(solution)/shard_map/ppermute | solution.py:1538
  412.1 67.6 %collective-permute-start.13 = (bf16[1552,512]{1,0:T(8,128)(2,1)}, bf16[1552,512]{1,0:T(8,128)(2,1)}, u32[]{:S(2)}, u32[]{:S(2)}) collective-permute-start(bf16[1552,512]{1,0:T(8,128)(2,1)} %collective-permute-done.9), channel_id=1, source_target_pairs={{0,1},{1,2},{2,3},{4,5},{5,6},{6,7},{8,9},{9,10},{10,11},{12,13},{... | collective-permute-start | bytes 4767752 | tf_op jit(solution)/shard_map/ppermute | solution.py:1537
  417.8 65.6 %collective-permute-start.15 = (bf16[1552,512]{1,0:T(8,128)(2,1)}, bf16[1552,512]{1,0:T(8,128)(2,1)}, u32[]{:S(2)}, u32[]{:S(2)}) collective-permute-start(bf16[1552,512]{1,0:T(8,128)(2,1)} %collective-permute-done.11), channel_id=1, source_target_pairs={{1,0},{2,1},{3,2},{5,4},{6,5},{7,6},{9,8},{10,9},{11,10},{13,12},{... | collective-permute-start | bytes 4767752 | tf_op jit(solution)/shard_map/ppermute | solution.py:1538
  516.2 302.4 %reduce-scatter.5.cloned.1.call-start = ((), (), s32[]{:S(2)}) async-start(), calls=%async_computation.3 | async-start | bytes 5898240 | tf_op jit(solution)/shard_map/reduce_scatter | solution.py:1610
  (74 other events, 1008.0 us)
Sparse Core Ops, SparseCore 0:
  117.0 76.9 all-gather.8
  196.4 78.7 all-gather.10
  277.7 78.7 all-gather.12
  358.9 78.7 all-gather.14
  516.3 108.9 reduce-scatter.2
  627.5 87.9 reduce-scatter.4

commit v4 on v3

--- a/solution.py
+++ b/solution.py
@@ -172,7 +172,7 @@
         span = slice(h * HD, (h + 1) * HD)
         qrot_ref[:, span] = turn_heads(queries[:, span], cosine, sine).astype(BF16)
 
-    @pl.loop(0, HQ)
+    @pl.loop(0, HQ, unroll=2)
     def _(head):
         group = head_lanes(head // (HQ // HK))
         share = softmax_of(qrot_ref[:, head_lanes(head)], krot_ref[:, group], mask_ref[...])
@@ -214,7 +214,7 @@
     dk_ref[...] = jnp.zeros_like(dk_ref)
     dv_ref[...] = jnp.zeros_like(dv_ref)
 
-    @pl.loop(0, HQ)
+    @pl.loop(0, HQ, unroll=2)
     def _(head):
         lanes, group = head_lanes(head), head_lanes(head // (HQ // HK))
         query, key = qrot_ref[:, lanes], krot_ref[:, group]

time: 876 us -> 875 us (level)
  no operation moved by 1% of the time
where the time goes in v4:
time: 875 us; the launch traced here: 865 us
  Pallas kernels  578 us (66%)
  waiting for transfers between devices  74 us (8%)
  other arithmetic  60.8 us (7%)
  local copies, waits for them, and re-layouts  57.4 us (7%)
  starting transfers between devices  42.8 us (5%)
  matrix products  34.6 us (4%)
  between operations  17.6 us (2%)
    pallas_call x7, Pallas kernels, rest_experts(): pl.pallas_call(functools.partial(rest_kernel, first_expert, trees, last,...  182 us
    pallas_call x4, Pallas kernels, own_experts(): pl.pallas_call(functools.partial(own_kernel, first_expert, turned), grid=...  115 us
    pallas_call x1, Pallas kernels, open_gather(): pl.pallas_call(functools.partial(open_kernel, reps, shards, [at for at, _...  98.2 us
    ppermute x6, waiting for transfers between devices, z_slots(): lax.ppermute(block, 'shard', [(i, (i + step) % size) for i in range(size)])  35.7 us
    all_gather x4, waiting for transfers between devices, gathered(): part = lax.all_gather(line, 'rep')  34.8 us
    pallas_call x1, Pallas kernels, attention_backward(): pl.pallas_call(attention_backward_kernel, in_specs=vmem_specs(len(operand...  29.5 us
    pallas_call x1, Pallas kernels, left_sync(): pl.pallas_call(functools.partial(left_sync_kernel, reps, shards, wide, wi...  28.2 us
    ppermute x5, starting transfers between devices, pass_on(): lax.ppermute(up, 'shard', forth)  26.7 us
  transfers between devices with their start and end apart: 23, of which 7 were waited for; matrix products, arithmetic and copies ran while one was open for 14% of the time, Pallas kernels for 50%

profile of v4, /device:TPU:0, one launch (start us, length us, event | category | flops | bytes accessed | tf_op | source)
XLA Modules:
  0.0 865.0 jit_solution(18000651516074964464)
XLA Ops:
  18.7 98.2 %open_gather.1 = (bf16[1536,1536]{1,0:T(8,128)(2,1)}, bf16[256,1536]{1,0:T(8,128)(2,1)}, bf16[256,1536]{1,0:T(8,128)(2,1)}, bf16[1536,1536]{1,0:T(8,128)(2,1)}, ...) custom-call(bf16[192,384]{1,0:T(8,128)(2,1)} %get-tuple-element.474., ...), custom_call_target="tpu_custom_call" | custom-call | tf_op jit(solution)/shard_map/open_gather/pallas_call | solution.py:761
  125.5 21.8 %attention_forward.1 = (bf16[512,1536]{1,0:T(8,128)(2,1)}, bf16[512,256]{1,0:T(8,128)(2,1)}, bf16[512,256]{1,0:T(8,128)(2,1)}, bf16[512,1536]{1,0:T(8,128)(2,1)}, f32[512,1536]{1,0:T(8,128)}) custom-call(bf16[512,1536]{1,0:T(8,128)(2,1)} %fusion.2.first_ref, bf16[1536,1536]{1,0:T(8,128)(2,1)} %get-tuple-element.137.query_ref, ...), custom_call_target="tpu_custom_call" | custom-call | flops 7247757312 | bytes 20447232 | tf_op jit(solution)/shard_map/attention_forward/pallas_call | solution.py:187
  177.8 16.1 %all-gather.9.cloned.1.call-done = bf16[32,576,384]{2,1,0:T(8,128)(2,1)} async-done(((bf16[4,576,384]{2,1,0:T(8,128)(2,1)}), bf16[32,576,384]{2,1,0:T(8,128)(2,1)}) %all-gather.9.cloned.1.call-update) | async-done | bytes 14155792 | tf_op jit(solution)/shard_map/all_gather | solution.py:1460
  194.0 28.6 %own_experts.4 = (f32[2,2,384,768]{3,2,1,0:T(8,128)}, f32[2,192,1536]{2,1,0:T(8,128)}, f32[512,1536]{1,0:T(8,128)}, f32[512,1536]{1,0:T(8,128)}, f32[2,512,1]{2,1,0:T(8,128)}) custom-call(bf16[1552,512]{1,0:T(8,128)(2,1)} %copy.268.x_ref, bf16[1536,512]{1,0:T(8,128)(2,1)} %bitcast.223, bf16[512,1536]{1,0:T(8,128)(2,1)} %up_ref.7, ...), custom_call_target="tpu_custom_call" | custom-call | flops 33822867456 | bytes 37748736 | tf_op jit(solution)/shard_map/own_experts/pallas_call | solution.py:475
  223.8 27.7 %collective-permute-done.5 = bf16[1152,384]{1,0:T(8,128)(2,1)} collective-permute-done((bf16[1152,384]{1,0:T(8,128)(2,1)S(1)}, bf16[1152,384]{1,0:T(8,128)(2,1)}, u32[]{:S(2)}, u32[]{:S(2)}) %collective-permute-start.5) | collective-permute-done | bytes 884768 | tf_op jit(solution)/shard_map/ppermute | solution.py:76
  266.6 8.7 %all-gather.11.cloned.1.call-done = bf16[32,576,384]{2,1,0:T(8,128)(2,1)} async-done(((bf16[4,576,384]{2,1,0:T(8,128)(2,1)}), bf16[32,576,384]{2,1,0:T(8,128)(2,1)}) %all-gather.11.cloned.1.call-update) | async-done | bytes 14155792 | tf_op jit(solution)/shard_map/all_gather | solution.py:1460
  275.3 28.6 %own_experts.5 = (f32[2,2,384,768]{3,2,1,0:T(8,128)}, f32[2,192,1536]{2,1,0:T(8,128)}, f32[512,1536]{1,0:T(8,128)}, f32[512,1536]{1,0:T(8,128)}, f32[2,512,1]{2,1,0:T(8,128)}) custom-call(bf16[1552,512]{1,0:T(8,128)(2,1)} %copy.270.x_ref, bf16[1536,512]{1,0:T(8,128)(2,1)} %bitcast.224, bf16[512,1536]{1,0:T(8,128)(2,1)} %up_ref.7, ...), custom_call_target="tpu_custom_call" | custom-call | flops 33822867456 | bytes 37748736 | tf_op jit(solution)/shard_map/own_experts/pallas_call | solution.py:475
  328.4 17.0 %rest_experts.7 = (f32[2,2,384,768]{3,2,1,0:T(8,128)}, f32[2,192,1536]{2,1,0:T(8,128)}) custom-call(bf16[8,4,3,192,384]{4,3,2,1,0:T(8,128)(2,1)} %bitcast.260, bf16[4,2,4,3,192,384]{5,4,3,2,1,0:T(8,128)(2,1)} %bitcast.261, f32[2,8,8,768]{3,2,1,0:T(8,128)} %bitcast.287, f32[8,8,1536]{2,1,0:T(8,128)} %bitcast.294, ...), custom_call_target="tpu_custom_call", output_to_operand_aliasing={{0}: (4, {}), {1}: (5, {})} | custom-call | flops 16911433728 | bytes 28311552 | tf_op jit(solution)/shard_map/rest_experts/pallas_call | solution.py:523
  346.7 9.8 %all-gather.13.cloned.1.call-done = bf16[32,576,384]{2,1,0:T(8,128)(2,1)} async-done(((bf16[4,576,384]{2,1,0:T(8,128)(2,1)}), bf16[32,576,384]{2,1,0:T(8,128)(2,1)}) %all-gather.13.cloned.1.call-update) | async-done | bytes 14155792 | tf_op jit(solution)/shard_map/all_gather | solution.py:1460
  356.5 28.6 %own_experts.6 = (f32[2,2,384,768]{3,2,1,0:T(8,128)}, f32[2,192,1536]{2,1,0:T(8,128)}, f32[512,1536]{1,0:T(8,128)}, f32[512,1536]{1,0:T(8,128)}, f32[2,512,1]{2,1,0:T(8,128)}) custom-call(bf16[1552,512]{1,0:T(8,128)(2,1)} %copy.270.x_ref, bf16[1536,512]{1,0:T(8,128)(2,1)} %bitcast.225, bf16[512,1536]{1,0:T(8,128)(2,1)} %up_ref.7, ...), custom_call_target="tpu_custom_call" | custom-call | flops 33822867456 | bytes 37748736 | tf_op jit(solution)/shard_map/own_experts/pallas_call | solution.py:475
  387.7 17.3 %rest_experts.8 = (f32[2,2,384,768]{3,2,1,0:T(8,128)}, f32[2,192,1536]{2,1,0:T(8,128)}) custom-call(bf16[8,4,3,192,384]{4,3,2,1,0:T(8,128)(2,1)} %bitcast.266, bf16[4,2,4,3,192,384]{5,4,3,2,1,0:T(8,128)(2,1)} %bitcast.267, f32[2,8,8,768]{3,2,1,0:T(8,128)} %bitcast.288, f32[8,8,1536]{2,1,0:T(8,128)} %bitcast.295, ...), custom_call_target="tpu_custom_call", output_to_operand_aliasing={{0}: (4, {}), {1}: (5, {})} | custom-call | flops 16911433728 | bytes 28311552 | tf_op jit(solution)/shard_map/rest_experts/pallas_call | solution.py:523
  419.1 17.1 %rest_experts.9 = (f32[2,2,384,768]{3,2,1,0:T(8,128)}, f32[2,192,1536]{2,1,0:T(8,128)}) custom-call(bf16[8,4,3,192,384]{4,3,2,1,0:T(8,128)(2,1)} %bitcast.272, bf16[4,2,4,3,192,384]{5,4,3,2,1,0:T(8,128)(2,1)} %bitcast.273, f32[2,8,8,768]{3,2,1,0:T(8,128)} %bitcast.289, f32[8,8,1536]{2,1,0:T(8,128)} %bitcast.296, ...), custom_call_target="tpu_custom_call", output_to_operand_aliasing={{0}: (4, {}), {1}: (5, {})} | custom-call | flops 16911433728 | bytes 28311552 | tf_op jit(solution)/shard_map/rest_experts/pallas_call | solution.py:523
  437.7 29.4 %own_experts.7 = (f32[2,2,384,768]{3,2,1,0:T(8,128)}, f32[2,192,1536]{2,1,0:T(8,128)}, f32[512,1536]{1,0:T(8,128)}, f32[512,1536]{1,0:T(8,128)}, f32[2,512,1]{2,1,0:T(8,128)}) custom-call(bf16[1552,512]{1,0:T(8,128)(2,1)} %copy.270.x_ref, bf16[1536,512]{1,0:T(8,128)(2,1)} %bitcast.226, bf16[512,1536]{1,0:T(8,128)(2,1)} %up_ref.7, ...), custom_call_target="tpu_custom_call" | custom-call | flops 33822867456 | bytes 37748736 | tf_op jit(solution)/shard_map/own_experts/pallas_call | solution.py:475
  485.6 29.5 %attention_backward.1 = (bf16[512,2048]{1,0:T(8,128)(2,1)}, bf16[1536,2048]{1,0:T(8,128)(2,1)}) custom-call(bf16[512,1536]{1,0:T(8,128)(2,1)} %fusion.78.middle_ref, bf16[1536,1536]{1,0:T(8,128)(2,1)} %get-tuple-element.140.output_ref, bf16[512,1536]{1,0:T(8,128)(2,1)} %get-tuple-element.186.qrot_ref, bf16[512,256]{1,0:T(8,128)(2,1)} %get-tuple-element.187.krot_ref, ...), custom_call_target="tpu_custom_call" | custom-call | flops 9663676416 | bytes 786432 | tf_op jit(solution)/shard_map/attention_backward/pallas_call | solution.py:248
  547.7 40.5 %rest_experts.10 = (f32[2,2,384,768]{3,2,1,0:T(8,128)}, f32[2,192,1536]{2,1,0:T(8,128)}, f32[2,2,8,384]{3,2,1,0:T(8,128)}, f32[2,8,256]{2,1,0:T(8,128)}) custom-call(bf16[8,4,3,192,384]{4,3,2,1,0:T(8,128)(2,1)} %bitcast.278, bf16[4,2,4,3,192,384]{5,4,3,2,1,0:T(8,128)(2,1)} %bitcast.279, ...), custom_call_target="tpu_custom_call", output_to_operand_aliasing={{0}: (4, {}), {1}: (5, {})} | custom-call | flops 50734301184 | bytes 28311552 | tf_op jit(solution)/shard_map/rest_experts/pallas_call | solution.py:523
  589.5 29.4 %rest_experts.11 = (f32[2,2,384,768]{3,2,1,0:T(8,128)}, f32[2,192,1536]{2,1,0:T(8,128)}, f32[2,2,8,384]{3,2,1,0:T(8,128)}, f32[2,8,256]{2,1,0:T(8,128)}) custom-call(bf16[8,4,3,192,384]{4,3,2,1,0:T(8,128)(2,1)} %bitcast.274, bf16[4,2,4,3,192,384]{5,4,3,2,1,0:T(8,128)(2,1)} %bitcast.275, ...), custom_call_target="tpu_custom_call", output_to_operand_aliasing={{0}: (4, {}), {1}: (5, {})} | custom-call | flops 33822867456 | bytes 28311552 | tf_op jit(solution)/shard_map/rest_experts/pallas_call | solution.py:523
  620.8 9.5 %left_parts.1 = (bf16[4,16,1152]{2,1,0:T(8,128)(2,1)}, f32[8,1536]{1,0:T(8,128)}) custom-call(bf16[512,1536]{1,0:T(8,128)(2,1)} %fusion.2.first_ref, bf16[512,2048]{1,0:T(8,128)(2,1)} %get-tuple-element.193.joint_ref.rest_6_, bf16[512,1536]{1,0:T(8,128)(2,1)} %get-tuple-element.194.mixed_ref, bf16[512,1536]{1,0:T(8,128)(2,1)} %fusion.78.middle_ref, ...), custom_call_target="tpu_custom_call" | custom-call | tf_op jit(solution)/shard_map/left_parts/pallas_call | solution.py:826
  630.3 30.5 %rest_experts.12 = (f32[2,2,384,768]{3,2,1,0:T(8,128)}, f32[2,192,1536]{2,1,0:T(8,128)}, f32[2,2,8,384]{3,2,1,0:T(8,128)}, f32[2,8,256]{2,1,0:T(8,128)}) custom-call(bf16[8,4,3,192,384]{4,3,2,1,0:T(8,128)(2,1)} %bitcast.262, bf16[4,2,4,3,192,384]{5,4,3,2,1,0:T(8,128)(2,1)} %bitcast.263, ...), custom_call_target="tpu_custom_call", output_to_operand_aliasing={{0}: (4, {}), {1}: (5, {})} | custom-call | flops 33822867456 | bytes 28311552 | tf_op jit(solution)/shard_map/rest_experts/pallas_call | solution.py:523
  662.2 10.3 %fusion.6 = (bf16[512,1536]{1,0:T(8,128)(2,1)}, bf16[512,1536]{1,0:T(8,128)(2,1)}) fusion(bf16[512,1536]{1,0:T(8,128)(2,1)} %tokens_ref.1, f32[512,1536]{1,0:T(8,128)} %get-tuple-element.462, f32[512]{0:T(512)S(1)} %multiply_multiply_fusion, f32[1536]{0:T(1024)S(1)} %copy-done.41, f32[512]{0:T(512)S(1)} %copy-done.51, f32[512,1536]{1,0:T(8,128)S(1)} %copy-done.2, ...), kind=kLoop, calls=%fused_computation.17 | loop fusion | flops 15728640 | bytes 28332032 | tf_op jit(solution)/shard_map/convert_element_type | solution.py:1629
  672.5 29.8 %rest_experts.13 = (f32[2,2,384,768]{3,2,1,0:T(8,128)}, f32[2,192,1536]{2,1,0:T(8,128)}, f32[2,2,8,384]{3,2,1,0:T(8,128)}, f32[2,8,256]{2,1,0:T(8,128)}) custom-call(bf16[8,4,3,192,384]{4,3,2,1,0:T(8,128)(2,1)} %bitcast.268, bf16[4,2,4,3,192,384]{5,4,3,2,1,0:T(8,128)(2,1)} %bitcast.269, ...), custom_call_target="tpu_custom_call", output_to_operand_aliasing={{0}: (4, {}), {1}: (5, {})} | custom-call | flops 33822867456 | bytes 28311552 | tf_op jit(solution)/shard_map/rest_experts/pallas_call | solution.py:523
  703.6 28.2 %left_sync.1 = (f32[160,384]{1,0:T(8,128)}, f32[64,256]{1,0:T(8,128)}, f32[2,8,384]{2,1,0:T(8,128)}, f32[8,128]{1,0:T(8,128)}, f32[4,32,384]{2,1,0:T(8,128)}) custom-call(bf16[4,16,1152]{2,1,0:T(8,128)(2,1)} %get-tuple-element.195.refs_0_, f32[8,1536]{1,0:T(8,128)} %get-tuple-element.196.refs_1_, f32[2,2,8,384]{3,2,1,0:T(8,128)} %get-tuple-element.203.refs_2_, ...), custom_call_target="tpu_custom_call" | custom-call | tf_op jit(solution)/shard_map/left_sync/pallas_call | solution.py:991
  748.1 9.0 %right_attention.1.refs_4_ = f32[8,3584]{1,0:T(8,128)} custom-call(f32[32,384]{1,0:T(8,128)} %slice.254.left_ref, f32[4,32,384]{2,1,0:T(8,128)} %get-tuple-element.221.leftz_ref, bf16[512,1536]{1,0:T(8,128)(2,1)} %fusion.2.first_ref, bf16[512,2048]{1,0:T(8,128)(2,1)} %get-tuple-element.193.joint_ref.rest_6_, bf16[512,1536]{1,0:T(8,128)(2,1)} %get-tuple-element.194.mixed_ref, ...), custom_call_target="tpu_custom_call" | custom-call | tf_op jit(solution)/shard_map/right_attention/pallas_call | solution.py:1091
  761.5 24.5 %right_sync.1.right_ref = f32[8,28672]{1,0:T(8,128)} custom-call(f32[2,8,3072]{2,1,0:T(8,128)} %right_experts.4.refs_0_, f32[2,8,3072]{2,1,0:T(8,128)} %right_experts.5.refs_1_, f32[2,8,3072]{2,1,0:T(8,128)} %right_experts.6.refs_2_, f32[2,8,3072]{2,1,0:T(8,128)} %right_experts.7.refs_3_, f32[8,3584]{1,0:T(8,128)} %right_attention.1.refs_4_), custom_call_target="tpu_custom_call" | custom-call | tf_op jit(solution)/shard_map/right_sync/pallas_call | solution.py:1137
  824.7 11.2 %squares_sync.1 = f32[8,128]{1,0:T(8,128)} custom-call(f32[8,128]{1,0:T(8,128)} %get-tuple-element.235.refs_0_, f32[8,128]{1,0:T(8,128)} %get-tuple-element.236.refs_1_, f32[8,128]{1,0:T(8,128)} %get-tuple-element.237.refs_2_, f32[8,128]{1,0:T(8,128)} %get-tuple-element.238.refs_3_, f32[8,128]{1,0:T(8,128)} %get-tuple-element.239.refs_4_), custom_call_target="tpu_custom_call" | custom-call | tf_op jit(solution)/shard_map/squares_sync/pallas_call | solution.py:1288
  (329 shorter events, 246.2 us)
Async XLA Ops:
  7.3 186.7 %all-gather.9.cloned.1.call-start = ((), (), s32[]{:S(2)}) async-start(), calls=%async_computation.4 | async-start | bytes 15925248 | tf_op jit(solution)/shard_map/all_gather | solution.py:1460
  9.7 6.8 collective-permute-start
  17.8 99.2 %copy-start.54 = (s32[1,512]{1,0:T(1,128)S(1)}, s32[1,512]{1,0:T(1,128)}, u32[]{:S(2)}) copy-start(s32[1,512]{1,0:T(1,128)} %param.33) | copy-start | bytes 6148
  116.9 158.3 %all-gather.11.cloned.1.call-start = ((), (), s32[]{:S(2)}) async-start(), calls=%async_computation.5 | async-start | bytes 15925248 | tf_op jit(solution)/shard_map/all_gather | solution.py:1460
  120.8 31.9 %collective-permute-start.3 = (bf16[576,384]{1,0:T(8,128)(2,1)S(1)}, bf16[576,384]{1,0:T(8,128)(2,1)}, u32[]{:S(2)}, u32[]{:S(2)}) collective-permute-start(bf16[576,384]{1,0:T(8,128)(2,1)S(1)} %pad_maximum_fusion.4), channel_id=1, source_target_pairs={{0,3},{1,0},{2,1},{3,2},{4,7},{5,4},{6,5},{7,6},{8,11},{9,8},{10,9... | collective-permute-start | bytes 1327112 | tf_op jit(solution)/shard_map/ppermute | solution.py:76
  123.2 37.6 %collective-permute-start.2 = (bf16[576,384]{1,0:T(8,128)(2,1)S(1)}, bf16[576,384]{1,0:T(8,128)(2,1)}, u32[]{:S(2)}, u32[]{:S(2)}) collective-permute-start(bf16[576,384]{1,0:T(8,128)(2,1)S(1)} %pad_maximum_fusion.4), channel_id=1, source_target_pairs={{0,2},{1,3},{2,0},{3,1},{4,6},{5,7},{6,4},{7,5},{8,10},{9,11},{10,... | collective-permute-start | bytes 1327112 | tf_op jit(solution)/shard_map/ppermute | solution.py:76
  123.2 37.6 %collective-permute-start.1 = (bf16[576,384]{1,0:T(8,128)(2,1)S(1)}, bf16[576,384]{1,0:T(8,128)(2,1)}, u32[]{:S(2)}, u32[]{:S(2)}) collective-permute-start(bf16[576,384]{1,0:T(8,128)(2,1)S(1)} %pad_maximum_fusion.4), channel_id=1, source_target_pairs={{0,1},{1,2},{2,3},{3,0},{4,5},{5,6},{6,7},{7,4},{8,9},{9,10},{10,1... | collective-permute-start | bytes 1327112 | tf_op jit(solution)/shard_map/ppermute | solution.py:76
  163.6 193.0 %all-gather.13.cloned.1.call-start = ((), (), s32[]{:S(2)}) async-start(), calls=%async_computation.6 | async-start | bytes 15925248 | tf_op jit(solution)/shard_map/all_gather | solution.py:1460
  171.6 52.2 %collective-permute-start.6 = (bf16[1152,384]{1,0:T(8,128)(2,1)S(1)}, bf16[1152,384]{1,0:T(8,128)(2,1)S(1)}, u32[]{:S(2)}, u32[]{:S(2)}) collective-permute-start(bf16[1152,384]{1,0:T(8,128)(2,1)S(1)} %copy-done.21), channel_id=1, source_target_pairs={{0,3},{1,0},{2,1},{3,2},{4,7},{5,4},{6,5},{7,6},{8,11},{9,8},{10,9... | collective-permute-start | bytes 2654216 | tf_op jit(solution)/shard_map/ppermute | solution.py:76
  171.6 79.9 %collective-permute-start.5 = (bf16[1152,384]{1,0:T(8,128)(2,1)S(1)}, bf16[1152,384]{1,0:T(8,128)(2,1)}, u32[]{:S(2)}, u32[]{:S(2)}) collective-permute-start(bf16[1152,384]{1,0:T(8,128)(2,1)S(1)} %copy-done.21), channel_id=1, source_target_pairs={{0,2},{1,3},{2,0},{3,1},{4,6},{5,7},{6,4},{7,5},{8,10},{9,11},{10,... | collective-permute-start | bytes 2654216 | tf_op jit(solution)/shard_map/ppermute | solution.py:76
  175.1 76.3 %collective-permute-start.4 = (bf16[1152,384]{1,0:T(8,128)(2,1)S(1)}, bf16[1152,384]{1,0:T(8,128)(2,1)}, u32[]{:S(2)}, u32[]{:S(2)}) collective-permute-start(bf16[1152,384]{1,0:T(8,128)(2,1)S(1)} %copy-done.21), channel_id=1, source_target_pairs={{0,1},{1,2},{2,3},{3,0},{4,5},{5,6},{6,7},{7,4},{8,9},{9,10},{10,1... | collective-permute-start | bytes 2654216 | tf_op jit(solution)/shard_map/ppermute | solution.py:76
  255.4 182.3 %all-gather.15.cloned.1.call-start = ((), (), s32[]{:S(2)}) async-start(), calls=%async_computation.7 | async-start | bytes 15925248 | tf_op jit(solution)/shard_map/all_gather | solution.py:1460
  256.0 446.3 %reduce-scatter.3.cloned.1.call-start = ((), (), s32[]{:S(2)}) async-start(), calls=%async_computation.2 | async-start | bytes 7864320 | tf_op jit(solution)/shard_map/reduce_scatter | solution.py:1619
  258.3 48.2 %collective-permute-start.8 = (bf16[1552,512]{1,0:T(8,128)(2,1)}, bf16[1552,512]{1,0:T(8,128)(2,1)S(1)}, u32[]{:S(2)}, u32[]{:S(2)}) collective-permute-start(bf16[1552,512]{1,0:T(8,128)(2,1)} %copy.270.x_ref), channel_id=1, source_target_pairs={{1,0},{2,1},{3,2},{5,4},{6,5},{7,6},{9,8},{10,9},{11,10},{13,12},{... | collective-permute-start | bytes 4767752 | tf_op jit(solution)/shard_map/ppermute | solution.py:1538
  259.6 46.9 %collective-permute-start.7 = (bf16[1552,512]{1,0:T(8,128)(2,1)}, bf16[1552,512]{1,0:T(8,128)(2,1)}, u32[]{:S(2)}, u32[]{:S(2)}) collective-permute-start(bf16[1552,512]{1,0:T(8,128)(2,1)} %copy.270.x_ref), channel_id=1, source_target_pairs={{0,1},{1,2},{2,3},{4,5},{5,6},{6,7},{8,9},{9,10},{10,11},{12,13},{... | collective-permute-start | bytes 4767752 | tf_op jit(solution)/shard_map/ppermute | solution.py:1537
  311.2 95.0 %collective-permute-start.10 = (bf16[1536,512]{0,1:T(8,128)(2,1)}, bf16[1536,512]{0,1:T(8,128)(2,1)}, u32[]{:S(2)}, u32[]{:S(2)}) collective-permute-start(bf16[1536,512]{0,1:T(8,128)(2,1)} %copy.274), channel_id=1, source_target_pairs={{0,1},{1,2},{2,3},{4,5},{5,6},{6,7},{8,9},{9,10},{10,11},{12,13},{... | collective-permute-start | bytes 4718600 | tf_op jit(solution)/shard_map/ppermute | solution.py:1537
  315.8 90.4 %collective-permute-start.12 = (bf16[1536,512]{0,1:T(8,128)(2,1)}, bf16[1536,512]{0,1:T(8,128)(2,1)}, u32[]{:S(2)}, u32[]{:S(2)}) collective-permute-start(bf16[1536,512]{0,1:T(8,128)(2,1)} %copy.275), channel_id=1, source_target_pairs={{1,0},{2,1},{3,2},{5,4},{6,5},{7,6},{9,8},{10,9},{11,10},{13,12},{... | collective-permute-start | bytes 4718600 | tf_op jit(solution)/shard_map/ppermute | solution.py:1538
  317.1 89.1 %collective-permute-start.9 = (bf16[1552,512]{1,0:T(8,128)(2,1)}, bf16[1552,512]{1,0:T(8,128)(2,1)}, u32[]{:S(2)}, u32[]{:S(2)}) collective-permute-start(bf16[1552,512]{1,0:T(8,128)(2,1)} %collective-permute-done.7), channel_id=1, source_target_pairs={{0,1},{1,2},{2,3},{4,5},{5,6},{6,7},{8,9},{9,10},{10,11},{12,13},{... | collective-permute-start | bytes 4767752 | tf_op jit(solution)/shard_map/ppermute | solution.py:1537
  322.8 83.4 %collective-permute-start.11 = (bf16[1552,512]{1,0:T(8,128)(2,1)S(1)}, bf16[1552,512]{1,0:T(8,128)(2,1)}, u32[]{:S(2)}, u32[]{:S(2)}) collective-permute-start(bf16[1552,512]{1,0:T(8,128)(2,1)S(1)} %collective-permute-done.8), channel_id=1, source_target_pairs={{1,0},{2,1},{3,2},{5,4},{6,5},{7,6},{9,8},{10,9},{11,10},{13,12},{... | collective-permute-start | bytes 4767752 | tf_op jit(solution)/shard_map/ppermute | solution.py:1538
  406.3 77.9 %collective-permute-start.14 = (bf16[1536,512]{0,1:T(8,128)(2,1)}, bf16[1536,512]{0,1:T(8,128)(2,1)}, u32[]{:S(2)}, u32[]{:S(2)}) collective-permute-start(bf16[1536,512]{0,1:T(8,128)(2,1)} %collective-permute-done.10), channel_id=1, source_target_pairs={{0,1},{1,2},{2,3},{4,5},{5,6},{6,7},{8,9},{9,10},{10,11},{12,13},{... | collective-permute-start | bytes 4718600 | tf_op jit(solution)/shard_map/ppermute | solution.py:1537
  410.8 73.3 %collective-permute-start.16 = (bf16[1536,512]{0,1:T(8,128)(2,1)}, bf16[1536,512]{0,1:T(8,128)(2,1)}, u32[]{:S(2)}, u32[]{:S(2)}) collective-permute-start(bf16[1536,512]{0,1:T(8,128)(2,1)} %collective-permute-done.12), channel_id=1, source_target_pairs={{1,0},{2,1},{3,2},{5,4},{6,5},{7,6},{9,8},{10,9},{11,10},{13,12},{... | collective-permute-start | bytes 4718600 | tf_op jit(solution)/shard_map/ppermute | solution.py:1538
  412.1 67.6 %collective-permute-start.13 = (bf16[1552,512]{1,0:T(8,128)(2,1)}, bf16[1552,512]{1,0:T(8,128)(2,1)}, u32[]{:S(2)}, u32[]{:S(2)}) collective-permute-start(bf16[1552,512]{1,0:T(8,128)(2,1)} %collective-permute-done.9), channel_id=1, source_target_pairs={{0,1},{1,2},{2,3},{4,5},{5,6},{6,7},{8,9},{9,10},{10,11},{12,13},{... | collective-permute-start | bytes 4767752 | tf_op jit(solution)/shard_map/ppermute | solution.py:1537
  417.8 65.5 %collective-permute-start.15 = (bf16[1552,512]{1,0:T(8,128)(2,1)}, bf16[1552,512]{1,0:T(8,128)(2,1)}, u32[]{:S(2)}, u32[]{:S(2)}) collective-permute-start(bf16[1552,512]{1,0:T(8,128)(2,1)} %collective-permute-done.11), channel_id=1, source_target_pairs={{1,0},{2,1},{3,2},{5,4},{6,5},{7,6},{9,8},{10,9},{11,10},{13,12},{... | collective-permute-start | bytes 4767752 | tf_op jit(solution)/shard_map/ppermute | solution.py:1538
  515.2 302.4 %reduce-scatter.5.cloned.1.call-start = ((), (), s32[]{:S(2)}) async-start(), calls=%async_computation.3 | async-start | bytes 5898240 | tf_op jit(solution)/shard_map/reduce_scatter | solution.py:1610
  (74 other events, 1008.0 us)
Sparse Core Ops, SparseCore 0:
  117.0 76.8 all-gather.8
  196.4 78.7 all-gather.10
  277.7 78.7 all-gather.12
  358.9 78.7 all-gather.14
  515.3 108.9 reduce-scatter.2
  626.5 87.9 reduce-scatter.4
